TPU v7x, 32 devices: a whole 2x2x4 slice. The times are simulated.
32 devices in a mesh: ctx: 8 (over z, y), wa: 4 (over x, core).
Axes of the slice: x: 2, y: 2, z: 4, core: 2. Of those that a mesh axis runs over, the one named last changes fastest.
Arguments:
- tokens: bfloat16 [1024, 2048], P('ctx'), may hold values from -6 to 6
- positions: int32 [1024], P('ctx'), may hold values from 0 to 511, as said below
- routes: int32 [1024, 8], P(('ctx', 'wa')), may hold values from 0 to 31, all different within a row; in each aligned block of 32 rows (0 to 31, 32 to 63, ...) at most 10 rows name the same one
- query_weight: bfloat16 [2048, 4096], P(None, 'wa'), may hold values from -0.125 to 0.125
- key_matrix: bfloat16 [2048, 512], P(None, 'wa'), may hold values from -0.125 to 0.125
- value_matrix: bfloat16 [2048, 512], P(None, 'wa'), may hold values from -0.125 to 0.125
- out_weight: bfloat16 [4096, 2048], P('wa'), may hold values from -1 to 1
- query_gain: float32 [128], replicated, may hold values from 0.5 to 1.5
- key_gain: float32 [128], replicated, may hold values from 0.5 to 1.5
- input_norm: float32 [2048], replicated, may hold values from 0.5 to 1.5
- post_norm: float32 [2048], replicated, may hold values from 0.5 to 1.5
- router: bfloat16 [2048, 32], replicated, may hold values from -0.0625 to 0.0625
- gate_weight: bfloat16 [32, 2048, 768], P(('ctx', 'wa')), may hold values from -0.125 to 0.125
- up_weight: bfloat16 [32, 2048, 768], P(('ctx', 'wa')), may hold values from -0.125 to 0.125
- down_weight: bfloat16 [32, 768, 2048], P(('ctx', 'wa')), may hold values from -0.625 to 0.625
- cotangent: bfloat16 [1024, 2048], P(('ctx', 'wa')), may hold values from -6 to 6
Outputs:
- output: bfloat16 [1024, 2048], P(('ctx', 'wa'))
- grad_tokens: bfloat16 [1024, 2048], P('ctx')
- grad_query_weight: float32 [2048, 4096], P('ctx', 'wa')
- grad_key_weight: float32 [2048, 512], P('ctx', 'wa')
- grad_value_weight: float32 [2048, 512], P('ctx', 'wa')
- grad_out_weight: float32 [4096, 2048], P('wa', 'ctx')
- grad_query_gain: float32 [128], replicated
- grad_key_gain: float32 [128], replicated
- grad_input_norm: float32 [2048], P('ctx')
- grad_post_norm: float32 [2048], replicated
- grad_router: float32 [2048, 32], replicated
- grad_gate_weight: float32 [32, 2048, 768], P(('ctx', 'wa'))
- grad_up_weight: float32 [32, 2048, 768], P(('ctx', 'wa'))
- grad_down_weight: float32 [32, 768, 2048], P(('ctx', 'wa'))
Inputs may be any that keep to these rules, and one draw needn't show every extreme that they name: In sequence order, each sequence's positions are 0 at place 0 and from one place to the next either rise by one or return to 0; in one of the 2 sequences they never return to 0. `routes`: each row names 8 different experts. Within each aligned block of 32 rows (the rows of one device) no expert is named more than 10 times, and in some block one expert is named exactly 10 times.
All inputs are finite; a program needn't handle non-finite values.
Results may differ from a plain program's by a relative error of at most 0.024.
Values may be sent and summed in bfloat16 or wider, within the bound.
No kernel may reach another device: no remote copies, remote signals or barrier semaphores. Data moves between devices by JAX's collectives and lax.ppermute only.
A program may use at most 128 MiB of HBM per device.

v0:
```python
import math

import jax
import jax.numpy as jnp
import numpy as np
from jax import lax
from jax.experimental import pallas as pl
from jax.experimental.pallas import tpu as pltpu
from jax.sharding import Mesh
from jax.sharding import PartitionSpec as P

SEQS = 2


EPSILON = 1e-06
BF16, F32, I32 = jnp.bfloat16, jnp.float32, jnp.int32


def dot(left, right):
    return jnp.dot(left, right, preferred_element_type=F32)


def contract_last(left, right):
    return lax.dot_general(
        left, right, (((1,), (1,)), ((), ())), preferred_element_type=F32
    )


def contract_first(left, right):
    return lax.dot_general(
        left, right, (((0,), (0,)), ((), ())), preferred_element_type=F32
    )


def split_low(values):
    high = values.astype(BF16)
    return high, (values - high.astype(F32)).astype(BF16)


def norm_stats(values):
    return lax.rsqrt(jnp.mean(values * values, axis=-1, keepdims=True) + EPSILON)


def norm_backward(grad_normed, normed, inverse, gain):
    scaled = grad_normed * gain
    return inverse * (scaled - normed * jnp.mean(scaled * normed, axis=-1, keepdims=True))


def half_turn(values):
    return pltpu.roll(values, values.shape[-1] // 2, values.ndim - 1)


def xor_permute(value, axis, offset):
    names = (axis,) if isinstance(axis, str) else axis
    count = math.prod(lax.axis_size(name) for name in names)
    return lax.ppermute(value, axis, [(i, i ^ offset) for i in range(count)])


def exchange(pieces, axis):
    return [pieces[0]] + [xor_permute(pieces[k], axis, k) for k in range(1, len(pieces))]


def gather_ctx_pieces(value):
    low_count = lax.axis_size("low")
    held = {j * low_count: v for j, v in enumerate(exchange([value] * 4, "lead"))}
    bit = 1
    while bit < low_count:
        held.update({k ^ bit: xor_permute(v, "low", bit) for k, v in list(held.items())})
        bit *= 2
    return [held[k] for k in range(4 * low_count)]


def gather_wa_pieces(value):
    over = xor_permute(value, "wa", 2)
    return [value, xor_permute(value, "wa", 1), over, xor_permute(over, "wa", 1)]


def gather(value, axis):
    return lax.all_gather(value, axis, axis=0, tiled=True)


def swap(value, axes):
    return lax.all_to_all(value, axes, split_axis=0, concat_axis=0, tiled=True)


class Incoming:
    def __init__(self, ref, copies):
        self.ref, self.copies = ref, dict(enumerate(copies))
        self.step = ref.shape[-1] // len(copies)
        self.shape, self.dtype, self.ndim = ref.shape, ref.dtype, ref.ndim

    def ready(self):
        for k in list(self.copies):
            self.copies.pop(k).wait()
        return self.ref

    def part(self, k):
        if k in self.copies:
            self.copies.pop(k).wait()
        return self.ref[:, k * self.step : (k + 1) * self.step]

    def __getitem__(self, index):
        return self.ready()[index]


class Outgoing:
    def __init__(self, ref, copies):
        self.ref, self.copies, self.sent = ref, copies, set()
        self.shape, self.dtype, self.ndim = ref.shape, ref.dtype, ref.ndim

    def send(self, part=None):
        for k, copy in enumerate(self.copies):
            if k not in self.sent and part in (None, k):
                copy.start()
                self.sent.add(k)

    def __getitem__(self, index):
        return self.ref[index]

    def __setitem__(self, index, value):
        self.ref[index] = value


class Near:
    def __init__(self, value):
        self.value = value


class Rows:
    def __init__(self, value, first, count):
        self.value, self.first, self.count = value, first, count


def near(values):
    return [Near(value) for value in values]


def vcall(body, outs, *operands, scratch=(), after=(), split=None, flops=0, megabytes=24):
    split = split or {}
    close = [isinstance(o, Near) for o in operands]
    ranges = {i: (o.first, o.count) for i, o in enumerate(operands) if isinstance(o, Rows)}
    operands = [o.value if isinstance(o, (Near, Rows)) else o for o in operands]
    close_out = [len(o) > 2 for o in outs]
    outs = [o[:2] for o in outs]
    places = [i for i, o in enumerate(operands) if o.ndim > 1 and not close[i]]
    far_outs = [i for i, c in enumerate(close_out) if not c]
    arrays = [
        jax.ShapeDtypeStruct((ranges[i][1],) + operands[i].shape[1:], operands[i].dtype)
        if i in ranges
        else operands[i]
        for i in places
    ]
    sizes = [o.size * o.dtype.itemsize for o in arrays]
    in_parts = [split.get(i, 1) for i in places]
    out_parts = [split.get(-1 - i, 1) for i in far_outs]
    count = len(arrays)

    def kernel(*refs):
        given = list(refs[: len(operands)])
        rest = refs[len(operands) + len(after) :]
        results, rest = rest[: len(outs)], rest[len(outs) :]
        inner = count + len(far_outs)
        buffers, sems, own = rest[:inner], rest[inner], rest[inner + 1 :]
        used = 0
        incoming = []
        for k, i in enumerate(places):
            source, target, parts = given[i], buffers[k], in_parts[k]
            if i in ranges:
                source = source.at[pl.ds(*ranges[i])]
            copies = []
            for c in range(parts):
                step = source.shape[-1] // parts
                if parts > 1:
                    piece = (slice(None), pl.ds(c * step, step))
                    copy = pltpu.make_async_copy(source.at[piece], target.at[piece], sems.at[used])
                else:
                    copy = pltpu.make_async_copy(source, target, sems.at[used])
                copies.append(copy)
                used += 1
            incoming.append(copies)
            given[i] = Incoming(target, copies)
        for c in range(max(in_parts, default=0)):
            for k in sorted(range(count), key=lambda k: sizes[k] / in_parts[k]):
                if c < in_parts[k]:
                    incoming[k][c].start()
        leaving = [Outgoing(result, []) for result in results]
        for k, i in enumerate(far_outs):
            result, source, parts = results[i], buffers[count + k], out_parts[k]
            copies = []
            for c in range(parts):
                step = result.shape[0] // parts
                if parts > 1:
                    piece = pl.ds(c * step, step)
                    copy = pltpu.make_async_copy(source.at[piece], result.at[piece], sems.at[used])
                else:
                    copy = pltpu.make_async_copy(source, result, sems.at[used])
                copies.append(copy)
                used += 1
            leaving[i] = Outgoing(source, copies)
        body(*given, *leaving, *own)
        for value in given:
            if isinstance(value, Incoming):
                value.ready()
        for value in leaving:
            value.send()
        for value in leaving:
            for copy in value.copies:
                copy.wait()

    moved = sum(sizes) + sum(math.prod(s) * jnp.dtype(d).itemsize for s, d in outs)
    in_hbm = pl.BlockSpec(memory_space=pltpu.HBM)

    def pinned(value):
        return pltpu.with_memory_space_constraint(value, pltpu.HBM)

    return pl.pallas_call(
        kernel,
        out_shape=[
            jax.ShapeDtypeStruct(s, d) if c else pltpu.HBM(s, d)
            for (s, d), c in zip(outs, close_out)
        ],
        in_specs=[
            pl.BlockSpec(memory_space=pltpu.SMEM)
            if o.ndim == 1
            else (pl.BlockSpec(memory_space=pltpu.VMEM) if c else in_hbm)
            for o, c in zip(operands, close)
        ]
        + [in_hbm] * len(after),
        out_specs=[pl.BlockSpec(memory_space=pltpu.VMEM) if c else in_hbm for c in close_out],
        scratch_shapes=[pltpu.VMEM(o.shape, o.dtype) for o in arrays]
        + [pltpu.VMEM(*outs[i]) for i in far_outs]
        + [pltpu.SemaphoreType.DMA((max(1, sum(in_parts) + sum(out_parts)),))]
        + list(scratch),
        compiler_params=pltpu.CompilerParams(vmem_limit_bytes=megabytes << 20),
        cost_estimate=pl.CostEstimate(flops=flops, bytes_accessed=moved, transcendentals=0),
    )(*[pinned(o) if i in places else o for i, o in enumerate(operands)], *[pinned(o) for o in after])


def as_column(row):
    count = row.shape[1]
    here = row_index((count, count)) == lane_index((count, count))
    return jnp.sum(jnp.where(here, row.astype(F32), 0.0), axis=-1, keepdims=True)


def lane_index(shape):
    return lax.broadcasted_iota(I32, shape, len(shape) - 1)


def row_index(shape):
    return lax.broadcasted_iota(I32, shape, len(shape) - 2)


def kv_kernel(tok, gain, wk, wv, pos, rates, key_gain, a_out, kv_out, raw_out, cos, sin):
    wide = tok[...].astype(F32)
    low = (wide * norm_stats(wide) * gain[...]).astype(BF16)
    a_out[...] = low
    size = wk.shape[1]
    angles = as_column(pos[...]) * rates[...]
    cos[...] = jnp.cos(angles)
    sine = jnp.sin(angles)
    sin[...] = jnp.where(lane_index(sine.shape) < size // 2, -sine, sine)
    raw = dot(low, wk[...])
    raw_out[...] = raw
    scaled = raw * norm_stats(raw) * key_gain[...]
    key = (scaled * cos[...] + half_turn(scaled) * sin[...]).astype(BF16)
    value = dot(low, wv[...]).astype(BF16)
    kv_out[:, :size] = key
    kv_out[:, size:] = value


def query_kernel(a, wq, cos, sin, query_gain, q_out, raw_out):
    size = cos.shape[1]
    span = a.shape[0] // SEQS
    for h in range(wq.shape[1] // size):
        if h % 2 == 0:
            pair = dot(a[...], wq[:, h * size : (h + 2) * size])
        raw = pair[:, (h % 2) * size : (h % 2 + 1) * size]
        scaled = raw * norm_stats(raw) * query_gain[...]
        rot = (scaled * cos[...] + half_turn(scaled) * sin[...]).astype(BF16)
        for s in range(SEQS):
            q_out[s, h * span : (h + 1) * span] = rot[s * span : (s + 1) * span]
            raw_out[s, h * span : (h + 1) * span] = raw[s * span : (s + 1) * span]


def attend_kernel(count, ids, q, pos, wo, *refs):
    kv, (k_out, v_out, p_out, att_out) = refs[:count], refs[count : count + 4]
    pieces, scr = refs[count + 4 : -1], refs[-1]
    ctx = ids[0]
    span = pos.shape[1] // SEQS
    part = span // 2
    size = q.shape[2]
    rows = q.shape[1]
    length = count * span
    scaling = 1.0 / math.sqrt(size)

    def place_of(owner, inner):
        late = (2 * count - 1 - owner) * part + inner - part
        return jnp.where(inner < part, owner * part + inner, late)

    lane = lane_index((span, length))
    key_place = place_of(lane >> (span.bit_length() - 1), lane & (span - 1))
    query_place = place_of(ctx, row_index((span, length)))
    for s in range(SEQS):
        for j in range(count):
            here = pl.ds(pl.multiple_of((ctx ^ j) * span, span), span)
            k_out[s, here] = kv[j][s * span : (s + 1) * span, :size]
            v_out[s, here] = kv[j][s * span : (s + 1) * span, size:]
        start = query_place - as_column(pos[:, s * span : (s + 1) * span]).astype(I32)
        visible = (key_place <= query_place) & (key_place >= start)
        scores = contract_last(q[s], k_out[s]) * scaling
        scores = scores.reshape(rows // span, span, length)
        scores = jnp.where(visible[None], scores, -1e30)
        weights = jnp.exp(scores - jnp.max(scores, axis=-1, keepdims=True))
        weights = weights / jnp.sum(weights, axis=-1, keepdims=True)
        low = weights.reshape(rows, length).astype(BF16)
        p_out[s] = low
        attended = dot(low, v_out[s]).astype(BF16)
        for h in range(rows // span):
            att_out[s * span : (s + 1) * span, h * size : (h + 1) * size] = attended[
                h * span : (h + 1) * span
            ]
    for out in (k_out, v_out, p_out, att_out):
        out.send()
    split_rows(ids[1], dot(att_out[...], wo[...]), pieces, scr)


def split_rows(wa, full, pieces, scr):
    quarter = pieces[0].shape[0]
    scr[...] = full.astype(BF16)
    for k, piece in enumerate(pieces):
        first = pl.multiple_of((wa ^ k) * quarter, quarter)
        piece[...] = scr[pl.ds(first, quarter)]


def join_rows(wa, pieces, out):
    quarter = pieces[0].shape[0]
    for k, piece in enumerate(pieces):
        out[pl.ds(pl.multiple_of((wa ^ k) * quarter, quarter), quarter)] = piece[...]


def added(pieces):
    total = pieces[0][...].astype(F32)
    for piece in pieces[1:]:
        total = total + piece[...].astype(F32)
    return total


def own_rows(ids, array, quarter):
    return array[pl.ds(pl.multiple_of(ids[1] * quarter, quarter), quarter)].astype(F32)


def hot_routes(columns, width):
    lane = lane_index((columns[0].shape[0], width))
    hot = columns[0] == lane
    for column in columns[1:]:
        hot = hot | (column == lane)
    return hot


def hidden_kernel(ids, tok, routes, post_norm, router, *refs):
    pieces, (send, hidden_out, prob_out) = refs[:-3], refs[-3:]
    quarter, width = pieces[0].shape
    experts = router.shape[0]
    hidden = own_rows(ids, tok, quarter) + added(pieces)
    hidden_out[...] = hidden
    ffn = (hidden * norm_stats(hidden) * post_norm[...]).astype(BF16)
    named = [as_column(routes[j : j + 1]).astype(I32) for j in range(routes.shape[0])]
    hot = hot_routes(named, experts)
    logits = contract_last(ffn, router[...])
    masked = jnp.where(hot, logits, -1e30)
    exps = jnp.where(hot, jnp.exp(logits - jnp.max(masked, axis=-1, keepdims=True)), 0.0)
    probs = exps / jnp.sum(exps, axis=-1, keepdims=True)
    prob_out[...] = probs
    high, low = split_low(probs)
    send[:, :width] = ffn
    if send.shape[1] > width + 2 * experts:
        send[:, width:] = jnp.zeros((quarter, send.shape[1] - width), BF16)
    send[:, width : width + experts] = high
    send[:, width + experts : width + 2 * experts] = low


def pack_kernel(cot, routes, out):
    quarter, width = cot.shape
    out[:, :width] = cot[...]
    lane = lane_index((quarter, 128))
    named = jnp.zeros((quarter, 128), F32)
    for j in range(routes.shape[0]):
        named = jnp.where(lane == j, as_column(routes[j : j + 1]), named)
    out[:, width:] = named.astype(BF16)


def route_kernel(experts, top, planes, ids, columns, *refs):
    pieces, t_out, rows_out = refs[:4], refs[4], refs[5 : 5 + planes]
    scr, rows_scr = refs[5 + planes :]
    quarter = pieces[0].shape[0]
    width = rows_out[0].shape[1]
    total = 4 * quarter
    lanes = -(-experts // 128) * 128
    for k, piece in enumerate(pieces):
        scr[pl.ds(pl.multiple_of((ids[3] ^ k) * quarter, quarter), quarter)] = piece[...]
    named = scr[:, width : width + 128].astype(F32).astype(I32)
    hot = hot_routes([named[:, j : j + 1] for j in range(top)], lanes)
    row, col = row_index((total, total)), lane_index((total, total))
    shift = quarter.bit_length() - 1
    before = (row >= col) & ((row >> shift) == (col >> shift))
    counts = dot(before.astype(F32).astype(BF16), hot.astype(F32).astype(BF16))
    slots = jnp.where(hot, counts - 1.0, -1.0).astype(BF16)
    slot_rows = columns.shape[1]
    spread = row_index((lanes, slot_rows)) == (ids[3] * planes + columns[0:1])
    slot = dot(slots, spread.astype(F32).astype(BF16))
    lead = row_index((total, slot_rows)) >> shift
    chosen = (slot == columns[2:3].astype(F32)) & (lead == columns[1:2])
    chosen = chosen.astype(F32).astype(BF16)
    t_out[...] = chosen
    t_out.send()
    rows_scr[...] = contract_first(chosen, scr[:, :width])
    split_groups(ids[4], rows_scr, rows_out)


def split_groups(mine, scr, pieces):
    group = pieces[0].shape[0]
    for k, piece in enumerate(pieces):
        first = pl.multiple_of((mine ^ k) * group, group)
        piece[...] = scr[pl.ds(first, group)].astype(BF16)
        piece.send()


def join_groups(mine, pieces, scr):
    group = pieces[0].shape[0]
    for k, piece in enumerate(pieces):
        first = pl.multiple_of((mine ^ k) * group, group)
        scr[pl.ds(first, group)] = piece[...].astype(F32)
    return scr[...].astype(BF16)


def pick_kernel(ids, chosen, attended, att_in, *refs):
    pieces, (rows_out, attended_out, scr) = refs[:4], refs[4:]
    quarter = pieces[0].shape[0]
    for k, piece in enumerate(pieces):
        scr[pl.ds(pl.multiple_of((ids[3] ^ k) * quarter, quarter), quarter)] = piece[...]
    rows_out[...] = contract_first(chosen[...], scr[...]).astype(BF16)
    rows_out.send()
    count, wide = attended.shape
    attended_out[:count] = attended[...]
    mine = att_in[pl.ds(pl.multiple_of(ids[1] * quarter, quarter), quarter)]
    for j in range(mine.shape[1] // wide):
        row = count + j * quarter
        attended_out[row : row + quarter] = mine[:, j * wide : (j + 1) * wide]


def cot_rows_kernel(planes, ids, wd, *refs):
    pieces, (rows_out, grad_out, scr) = refs[:planes], refs[planes:]
    rows = join_groups(ids[4], pieces, scr)
    rows_out[...] = rows
    rows_out.send()
    grad_out[...] = contract_last(rows, wd[...])


def expert_kernel(experts, ids, wg, wu, grad_raw, rows_in, act_out, dg_out, du_out, prob_out, back):
    width = wg.shape[0]
    extra = rows_in.shape[1] - width
    total = rows_in.shape[0]
    rows = rows_in[:, :width]
    lane = lane_index((total, extra))
    mine_high, mine_low = lane == ids[2], lane == ids[2] + experts
    prob = jnp.sum(
        jnp.where(mine_high | mine_low, rows_in[:, width:].astype(F32), 0.0),
        axis=-1,
        keepdims=True,
    )
    prob_out[...] = jnp.broadcast_to(prob, prob_out.shape)
    gate_grad = jnp.zeros((total, 1), F32)
    step = wg.shape[1] // 3
    for c in range(3):
        here = slice(c * step, (c + 1) * step)
        gate, up = dot(rows, wg.part(c)), dot(rows, wu.part(c))
        sig = jax.nn.sigmoid(gate)
        lifted = gate * sig
        act = (lifted * up).astype(BF16)
        act_out[:, here] = act
        raw = grad_raw[:, here]
        gate_grad = gate_grad + jnp.sum(act.astype(F32) * raw, axis=-1, keepdims=True)
        grad_act = prob * raw
        dg_out[:, here] = (grad_act * up * sig * (1.0 + gate * (1.0 - sig))).astype(BF16)
        du_out[:, here] = (grad_act * lifted).astype(BF16)
    for out in (act_out, dg_out, du_out, prob_out):
        out.send()
    grad_in = contract_last(dg_out[...], wg[...]) + contract_last(du_out[...], wu[...])
    back[:, :width] = grad_in.astype(BF16)
    high = gate_grad.astype(BF16).astype(F32)
    tail = jnp.where(mine_high, high, jnp.where(mine_low, gate_grad - high, 0.0))
    back[:, width:] = tail.astype(BF16)


def expert_weights_kernel(rows, dg, du, act, cot_rows, prob, gate_out, up_out, down_out):
    width, units = gate_out.shape
    step = width // 4
    for c in range(4):
        here = slice(c * step, (c + 1) * step)
        left = rows[:, here]
        gate_out[here] = contract_first(left, dg[...])
        gate_out.send(c)
        up_out[here] = contract_first(left, du[...])
        up_out.send(c)
    grad_rows = (cot_rows[...].astype(F32) * prob[:, 0:1]).astype(BF16)
    step = units // 3
    for c in range(3):
        here = slice(c * step, (c + 1) * step)
        down_out[here] = contract_first(act[:, here], grad_rows)
        down_out.send(c)


def out_rows_kernel(act, wd, prob, rows_out):
    rows = dot(act[...], wd[...]).astype(BF16).astype(F32) * prob[:, 0:1]
    rows_out[...] = rows.astype(BF16)


def combine_kernel(ids, chosen, rows, *refs):
    pieces, scr = refs[:-1], refs[-1]
    quarter = pieces[0].shape[0]
    scr[...] = dot(chosen[...], rows[...])
    for k, out in enumerate(pieces):
        first = pl.multiple_of((ids[3] ^ k) * quarter, quarter)
        out[...] = scr[pl.ds(first, quarter)].astype(out.dtype)


def grad_hidden_kernel(ids, hidden_ref, prob_ref, router, cot, post_norm, *refs):
    pieces, low_out, lates, scr = refs[:4], refs[4], refs[5:9], refs[9]
    width = hidden_ref.shape[1]
    experts = router.shape[0]
    total = added(pieces)
    gate_grad = total[:, width : width + experts] + total[:, width + experts : width + 2 * experts]
    prob = prob_ref[...]
    grad_logits = prob * (gate_grad - jnp.sum(prob * gate_grad, axis=-1, keepdims=True))
    high, low = split_low(grad_logits)
    grad_ffn = total[:, :width] + (dot(high, router[...]) + dot(low, router[...]))
    hidden = hidden_ref[...]
    inverse = norm_stats(hidden)
    normed = hidden * inverse
    ffn = (normed * post_norm[...]).astype(BF16)
    grad = cot[...].astype(F32) + norm_backward(grad_ffn, normed, inverse, post_norm[...])
    grad = grad.astype(BF16)
    low_out[...] = grad
    router_part = (contract_first(high, ffn) + contract_first(low, ffn)).astype(BF16)
    post = jnp.sum(grad_ffn * normed, axis=0, keepdims=True)
    post = jnp.where(row_index((16, width)) == 0, post, 0.0).astype(BF16)
    quarter = hidden.shape[0]
    scr[:quarter] = grad
    scr[quarter : quarter + experts] = router_part
    scr[quarter + experts :] = post
    wide = lates[0].shape[1]
    for k, out in enumerate(lates):
        out[...] = scr[:, pl.ds(pl.multiple_of((ids[3] ^ k) * wide, wide), wide)]


def block_at(low, k, blocks):
    value = blocks[0].astype(F32)
    for b in range(1, len(blocks)):
        value = jnp.where((low ^ k) == b, blocks[b].astype(F32), value)
    return value.astype(blocks[0].dtype)


def attend_back_kernel(
    count, ids, q, keys, values, p, raw_ref, wo, cos, sin, gain, *refs
):
    pieces, (gq_out, gain_out, kv_out, branch_out, dq_scr) = refs[:4], refs[4:]
    join_rows(ids[1], pieces, branch_out)
    branch_out.send()
    size, rows = q.shape[2], q.shape[1]
    span = branch_out.shape[0] // SEQS
    heads = rows // span
    scaling = 1.0 / math.sqrt(size)
    step = branch_out.shape[1] // 4
    grad_att = contract_last(branch_out[:, :step], wo.part(0))
    for c in range(1, 4):
        grad_att = grad_att + contract_last(branch_out[:, c * step : (c + 1) * step], wo.part(c))
    grad_att = grad_att.astype(BF16)
    gain_sum = jnp.zeros((1, size), F32)
    for s in range(SEQS):
        rows_s = grad_att[s * span : (s + 1) * span]
        for h in range(heads):
            dq_scr[h * span : (h + 1) * span] = rows_s[:, h * size : (h + 1) * size]
        grad_o = dq_scr[...]
        low = p[s]
        grad_p = contract_last(grad_o, values[s])
        weights = low.astype(F32)
        delta = jnp.sum(weights * grad_p, axis=-1, keepdims=True)
        grad_s = (weights * (grad_p - delta)).astype(BF16)
        grad_v = contract_first(low, grad_o).astype(BF16)
        grad_k = (contract_first(grad_s, q[s]) * scaling).astype(BF16)
        for j in range(count):
            kv_out[j, s * span : (s + 1) * span, :size] = grad_k[j * span : (j + 1) * span]
            kv_out[j, s * span : (s + 1) * span, size:] = grad_v[j * span : (j + 1) * span]
        grad_q = dot(grad_s, keys[s]) * scaling
        cosine, sine = cos[s * span : (s + 1) * span], sin[s * span : (s + 1) * span]
        for h in range(heads):
            grad_rot = grad_q[h * span : (h + 1) * span]
            grad_normed = grad_rot * cosine - half_turn(grad_rot) * sine
            raw = raw_ref[s, h * span : (h + 1) * span]
            inverse = norm_stats(raw)
            normed = raw * inverse
            gain_sum = gain_sum + jnp.sum(grad_normed * normed, axis=0, keepdims=True)
            gq_out[s * span : (s + 1) * span, h * size : (h + 1) * size] = norm_backward(
                grad_normed, normed, inverse, gain[...]
            ).astype(BF16)
    gain_out[...] = gain_sum


def query_in_kernel(gq, wq, out):
    out[...] = contract_last(gq[...], wq[...])


def columns_kernel(lows, rows, ids, early, *refs):
    pieces, (col_out, late) = refs[:4], refs[4:]
    wide = col_out.shape[1] // 2
    part = wide // lows
    for k, piece in enumerate(pieces):
        late[ids[3] ^ k] = piece[...]
    quarter = rows
    experts = late.shape[1] - 16 - quarter
    per_row = early.shape[2] // wide
    row = early.shape[1] - 4 // per_row * quarter + ids[3] // per_row * quarter
    here = pl.ds(pl.multiple_of(row, quarter), quarter)
    lane = pl.ds(pl.multiple_of(ids[3] % per_row * wide, wide), wide)

    def place(target_rows, first, values):
        blocks = [values[:, b * part : (b + 1) * part] for b in range(lows)]
        for k in range(lows):
            col_out[target_rows, first + k * part : first + (k + 1) * part] = block_at(
                ids[5], k, blocks
            ).astype(BF16)

    total = jnp.zeros((late.shape[1] - quarter, wide), F32)
    for j in range(4):
        target = slice(j * quarter, (j + 1) * quarter)
        place(target, 0, early[j, here, lane])
        place(target, wide, late[j, :quarter])
        total = total + late[j, quarter:].astype(F32)
    target = slice(4 * quarter, 4 * quarter + experts)
    place(target, 0, total[:experts])
    post = jnp.where(row_index((experts, wide)) == 0, total[experts : experts + 1], 0.0)
    place(target, wide, post)


def grad_in_kernel(ids, from_q, raw_ref, cos, sin, gain, wk, wv, parts, kv_out, gain_out, own_out, send_out, scr):
    size = wk.shape[1]
    total = added([parts[k] for k in range(parts.shape[0])])
    grad_v = total[:, size:].astype(BF16)
    grad_rot = total[:, :size]
    grad_normed = grad_rot * cos[...] - half_turn(grad_rot) * sin[...]
    raw = raw_ref[...]
    inverse = norm_stats(raw)
    normed = raw * inverse
    gain_out[...] = jnp.sum(grad_normed * normed, axis=0, keepdims=True)
    grad_k = norm_backward(grad_normed, normed, inverse, gain[...]).astype(BF16)
    kv_out[:, :size] = grad_k
    kv_out[:, size:] = grad_v
    full = from_q[...] + contract_last(grad_k, wk[...]) + contract_last(grad_v, wv[...])
    scr[...] = full.astype(BF16)
    half = own_out.shape[0]
    for out, core in ((send_out, 1 - ids[1] % 2), (own_out, ids[1] % 2)):
        out[...] = scr[pl.ds(pl.multiple_of(core * half, half), half)]


def half_kernel(own, other, *refs):
    pieces, (out, sums_out, *sends) = refs[:4], refs[4:]
    out[...] = added((own, other)).astype(BF16)
    total = added(pieces)
    experts, part = total.shape[0], sums_out.shape[1]
    wide = total.shape[1] // 2
    for k, target in enumerate((sums_out, *sends)):
        target[:experts] = total[:, k * part : (k + 1) * part].astype(target.dtype)
        target[experts:] = total[:, wide + k * part : wide + (k + 1) * part].astype(target.dtype)


def token_rows_kernel(ids, tok, gain, branch, own, other, rows_out, gain_out):
    half = own.shape[0]
    mine = pl.ds(pl.multiple_of(ids[1] % 2 * half, half), half)
    grad_in = added((own, other))
    wide = tok[mine].astype(F32)
    inverse = norm_stats(wide)
    normed = wide * inverse
    rows_out[...] = (
        branch[mine].astype(F32) + norm_backward(grad_in, normed, inverse, gain[...])
    ).astype(BF16)
    gain_out[...] = 0.5 * jnp.sum(grad_in * normed, axis=0, keepdims=True)


def sums_kernel(parts, router_out, post_out, q_out, k_out, gain_out):
    devices = parts.shape[0]
    experts, step = router_out.shape[0], router_out.shape[1] // devices
    base = experts // 2
    total = parts[0].astype(F32)[base:]
    for d in range(1, devices):
        total = total + parts[d].astype(F32)[base:]
    q_out[...] = total[1:2]
    k_out[...] = total[2:3]
    part = gain_out.shape[1]
    for j in range(-(-part // 128)):
        lanes = min(128, part)
        gain_out[:, j * 128 : j * 128 + lanes] = total[3 + j : 4 + j, :lanes]
    group = 128 // step
    for g in range(devices // group):
        held = range(g * group, (g + 1) * group)
        here = slice(g * 128, (g + 1) * 128)
        wide = [parts[d].astype(F32) for d in held]
        router_out[:base, here] = jnp.concatenate([w[:base, :step] for w in wide], axis=1)
        router_out[base:, here] = jnp.concatenate(
            [w[:base, 64 : 64 + step] for w in wide], axis=1
        )
        post_out[:, here] = jnp.concatenate([w[base : base + 1, :step] for w in wide], axis=1)


def join_kernel(ids, own, other, gain_part, q_gain, k_gain, *refs):
    sums, (out, parts_low, parts_out) = refs[:-3], refs[-3:]
    total = added(sums)
    wa_count = lax.axis_size("wa")
    experts, part = total.shape[0] // 2, total.shape[1]
    step = part // wa_count
    mine = total[:, :step]
    for w in range(1, wa_count):
        mine = jnp.where(ids[1] == w, total[:, w * step : (w + 1) * step], mine)
    router_part, post = mine[:experts], mine[experts : experts + 1]
    base = experts // 2
    parts_out[...] = jnp.zeros(parts_out.shape, F32)
    for d in range(parts_out.shape[0]):
        parts_out[d, :base, :step] = router_part[:base]
        parts_out[d, :base, 64 : 64 + step] = router_part[base:]
        parts_out[d, base : base + 1, :step] = post
        parts_out[d, base + 1 : base + 2] = q_gain[...]
        parts_out[d, base + 2 : base + 3] = k_gain[...]
        first = d // wa_count * part
        for j in range(-(-part // 128)):
            lanes = min(128, part)
            parts_out[d, base + 3 + j : base + 4 + j, :lanes] = gain_part[
                :, first + j * 128 : first + j * 128 + lanes
            ]
    parts_low[...] = parts_out[...].astype(BF16)
    parts_low.send()
    half = own.shape[0]
    for source, core in ((own, ids[1] % 2), (other, 1 - ids[1] % 2)):
        out[pl.ds(pl.multiple_of(core * half, half), half)] = source[...]


def token_order(wa, pieces, count, first, scr):
    part = scr.shape[1]
    wa_count = len(pieces)
    quarter = scr.shape[0] // (wa_count * count)
    for k, piece in enumerate(pieces):
        for c in range(count):
            row = pl.multiple_of((c * wa_count + (wa ^ k)) * quarter, quarter)
            scr[pl.ds(row, quarter)] = piece[c * quarter : (c + 1) * quarter, first : first + part]
    return scr[...]


def out_weight_kernel(ids, attended, *refs):
    pieces, (out, *sends) = refs[:4], refs[4:-2]
    scr, att_scr = refs[-2:]
    part, wide, rows = out.shape[1], scr.shape[1], scr.shape[0] // 4
    columns = token_order(ids[1], pieces, 4, wide, scr)
    for j in range(4):
        att_scr[j * rows : (j + 1) * rows] = attended[j, :rows]
    partial = contract_first(att_scr[...], columns)
    for k, target in enumerate((out, *sends)):
        target[...] = partial[:, k * part : (k + 1) * part].astype(target.dtype)


def in_weight_kernel(ids, queries, *refs):
    pieces, (own, *sends) = refs[:4], refs[4:-1]
    left, part = refs[-1], own.shape[0]
    partial = contract_first(token_order(ids[1], pieces, 4, 0, left), queries[...])
    for k, send in enumerate(sends, start=1):
        send[...] = partial[k * part : (k + 1) * part].astype(BF16)
        send.send()
    own[...] = partial[:part]


def kv_weight_kernel(ids, *refs):
    kvs, refs, rows = refs[:4], refs[4:-1], refs[-1]
    count = kvs[0].shape[0]
    for k, piece in enumerate(kvs):
        rows[pl.ds(pl.multiple_of((ids[3] ^ k) * count, count), count)] = piece[...]
    in_weight_kernel(ids, rows, *refs)


def last_kernel(lows, parts, hidden, out_own, wo_own, wq_own, kv_own, *refs):
    outs, refs = refs[:3], refs[3:]
    wos, wqs, kvs = [refs[j * (lows - 1) : (j + 1) * (lows - 1)] for j in range(3)]
    refs = refs[3 * (lows - 1) :]
    output, wo_out, wq_out, wk_out, wv_out = refs[:5]
    wo_out[...] = added((wo_own, *wos))
    wo_out.send()
    wq_out[...] = added((wq_own, *wqs))
    wq_out.send()
    total = added((kv_own, *kvs))
    size = wk_out.shape[1]
    wk_out[...] = total[:, :size]
    wv_out[...] = total[:, size:]
    output[...] = (hidden[...] + added((out_own, *outs))).astype(BF16)
    sums_kernel(parts, *refs[5:])


def bind(body, *sizes):
    return lambda *refs: body(*sizes, *refs)


def on_device(
    tokens,
    positions,
    routes,
    query_weight,
    key_matrix,
    value_matrix,
    out_weight,
    query_gain,
    key_gain,
    input_norm,
    post_norm,
    router,
    gate_weight,
    up_weight,
    down_weight,
    cotangent,
):
    lead_count, low_count = lax.axis_size("lead"), lax.axis_size("low")
    ctx_count = lead_count * low_count
    wa_count = lax.axis_size("wa")
    lead_id = lax.axis_index("lead")
    wa_id = lax.axis_index("wa")
    ctx_id = lead_id * low_count + lax.axis_index("low")
    plane_id = lax.axis_index("low") * wa_count + wa_id
    low_id = lax.axis_index("low")
    ids = jnp.stack([ctx_id, wa_id, ctx_id * wa_count + wa_id, lead_id, plane_id, low_id]).astype(I32)
    row_count, width = tokens.shape
    span = row_count // SEQS
    quarter = row_count // wa_count
    size = query_gain.shape[0]
    local_width = query_weight.shape[1]
    heads = local_width // size
    length = span * ctx_count
    experts = router.shape[1]
    top = routes.shape[1]
    hidden_units = gate_weight.shape[2]
    devices = ctx_count * wa_count
    planes = low_count * wa_count
    part = width // ctx_count
    capacity = max(2, (5 * quarter * top + 4 * experts - 1) // (4 * experts))
    group = -(-4 * capacity // 16) * 16 if planes > 8 else 4 * capacity
    slot_rows = planes * group
    extra = -(-2 * experts // 128) * 128
    everywhere, plane, blocks = ("lead", "low", "wa"), ("low", "wa"), ("lead", "low")
    gate_weight, up_weight, down_weight = gate_weight[0], up_weight[0], down_weight[0]
    input_norm, post_norm = input_norm[None], post_norm[None]
    query_gain, key_gain = query_gain[None], key_gain[None]

    halves = np.arange(size) % (size // 2)
    rates = np.exp(halves * (-2.0 * math.log(1000000.0) / size)).astype(np.float32)
    attention_input, kv_own, keys_raw, cosine, sine = vcall(
        kv_kernel,
        [
            ((row_count, width), BF16),
            ((row_count, 2 * size), BF16, "near"),
            ((row_count, size), F32),
            ((row_count, size), F32),
            ((row_count, size), F32),
        ],
        tokens, input_norm, key_matrix, value_matrix, positions[None], jnp.asarray(rates)[None],
        key_gain,
        flops=4 * row_count * width * size,
    )
    kv_all = exchange([kv_own] * ctx_count, blocks)

    q_heads, queries_raw = vcall(
        query_kernel,
        [
            ((SEQS, heads * span, size), BF16),
            ((SEQS, heads * span, size), F32),
        ],
        attention_input, query_weight, cosine, sine, query_gain,
        flops=2 * row_count * width * local_width,
    )

    (cot_send,) = vcall(
        pack_kernel,
        [((quarter, width + 128), BF16, "near")],
        cotangent, routes.T,
        after=[q_heads],
    )
    cot_pieces = exchange([cot_send] * 4, "lead")

    keys_seq, values_seq, weights_low, attended_low, *branch = vcall(
        bind(attend_kernel, ctx_count),
        [
            ((SEQS, length, size), BF16),
            ((SEQS, length, size), BF16),
            ((SEQS, heads * span, length), BF16),
            ((row_count, local_width), BF16),
        ]
        + [((quarter, width), BF16, "near")] * wa_count,
        ids, q_heads, positions[None], out_weight, *near(kv_all),
        scratch=[pltpu.VMEM((row_count, width), BF16)],
        flops=2 * row_count * width * local_width + 4 * row_count * local_width * length,
        megabytes=48,
    )
    branch = exchange(branch, "wa")

    inner = np.arange(slot_rows) % group
    columns = np.zeros((8, slot_rows), np.int32)
    columns[0] = np.arange(slot_rows) // group
    columns[1] = np.minimum(inner // capacity, 3)
    columns[2] = np.where(inner < 4 * capacity, inner % capacity, -5)
    chosen, *cot_groups = vcall(
        bind(route_kernel, experts, top, planes),
        [((row_count, slot_rows), BF16)] + [((group, width), BF16)] * planes,
        ids, jnp.asarray(columns), *near(cot_pieces),
        after=[branch[0]],
        scratch=[
            pltpu.VMEM((4 * quarter, width + 128), BF16),
            pltpu.VMEM((slot_rows, width), F32),
        ],
        flops=2 * slot_rows * row_count * width,
    )
    send, hidden, probs = vcall(
        hidden_kernel,
        [
            ((quarter, width + extra), BF16, "near"),
            ((quarter, width), F32),
            ((quarter, experts), F32),
        ],
        ids, tokens, routes.T, post_norm, router.T, *near(branch),
        after=[chosen],
        flops=2 * quarter * width * experts,
    )

    cot_groups = exchange(cot_groups, plane)
    cot_rows, grad_raw = vcall(
        bind(cot_rows_kernel, planes),
        [((slot_rows, width), BF16), ((slot_rows, hidden_units), F32)],
        ids, down_weight, *cot_groups,
        scratch=[pltpu.VMEM((slot_rows, width), F32)],
        flops=2 * slot_rows * hidden_units * width,
    )

    rows_in, early_rows = vcall(
        pick_kernel,
        [
            ((slot_rows, width + extra), BF16),
            ((row_count + width // local_width * quarter, local_width), BF16),
        ],
        ids, chosen, attended_low, attention_input, *near(exchange([send] * 4, "lead")),
        after=cot_groups[1:],
        scratch=[pltpu.VMEM((row_count, width + extra), BF16)],
        flops=2 * slot_rows * row_count * width,
    )
    rows_in = swap(rows_in, plane)
    early_all = gather(early_rows, "lead").reshape(4, -1, local_width)
    activation, grad_gate_part, grad_up_part, row_prob, back = vcall(
        bind(expert_kernel, experts),
        [
            ((slot_rows, hidden_units), BF16),
            ((slot_rows, hidden_units), BF16),
            ((slot_rows, hidden_units), BF16),
            ((slot_rows, 128), F32),
            ((slot_rows, width + extra), BF16),
        ],
        ids, gate_weight, up_weight, grad_raw, Near(rows_in),
        split={1: 3, 2: 3},
        flops=8 * slot_rows * hidden_units * width,
        megabytes=48,
    )

    grad_gate_weight, grad_up_weight, grad_down_weight = vcall(
        expert_weights_kernel,
        [
            ((width, hidden_units), F32),
            ((width, hidden_units), F32),
            ((hidden_units, width), F32),
        ],
        rows_in, grad_gate_part, grad_up_part, activation, cot_rows, row_prob,
        split={-1: 4, -2: 4, -3: 3},
        flops=6 * slot_rows * hidden_units * width,
        megabytes=40,
    )

    def to_tokens(rows, after):
        return vcall(
            combine_kernel,
            [((quarter, rows.shape[1]), F32, "near")]
            + [((quarter, rows.shape[1]), BF16, "near")] * 3,
            ids, chosen, Near(rows),
            after=after,
            scratch=[pltpu.VMEM((row_count, rows.shape[1]), F32)],
            flops=2 * slot_rows * row_count * width,
        )

    back = swap(back, plane)
    back_pieces = exchange(to_tokens(back, [grad_gate_weight, early_all]), "lead")
    (out_rows,) = vcall(
        out_rows_kernel,
        [((slot_rows, width), BF16)],
        activation, down_weight, row_prob,
        after=back_pieces[1:],
        flops=2 * slot_rows * hidden_units * width,
    )
    out_made = out_rows
    out_rows = swap(out_rows, plane)
    grad_low, *late_rows = vcall(
        grad_hidden_kernel,
        [
            ((quarter, width), BF16, "near"),
        ]
        + [((quarter + experts + 16, width // 4), BF16, "near")] * 4,
        ids, hidden, probs, router.T, cotangent, post_norm, *near(back_pieces),
        scratch=[pltpu.VMEM((quarter + experts + 16, width), BF16)],
        flops=4 * quarter * width * experts,
    )

    grad_pieces = exchange([grad_low] * wa_count, "wa")
    late_all = exchange(late_rows, "lead")
    grad_queries, query_gain_part, kv_parts, grad_branch = vcall(
        bind(attend_back_kernel, ctx_count),
        [
            ((row_count, local_width), BF16),
            ((1, size), F32),
            ((ctx_count, row_count, 2 * size), BF16),
            ((row_count, width), BF16),
        ],
        ids, q_heads, keys_seq, values_seq, weights_low, queries_raw, out_weight,
        cosine, sine, query_gain, *near(grad_pieces),
        split={6: 4},
        after=late_all[1:] + [out_made],
        scratch=[pltpu.VMEM((heads * span, size), BF16)],
        flops=2 * row_count * width * local_width + 8 * row_count * local_width * length,
        megabytes=48,
    )
    kv_parts = swap(kv_parts, blocks)
    queries_all = gather(grad_queries, "lead")
    (from_queries,) = vcall(
        query_in_kernel,
        [((row_count, width), F32)],
        grad_queries, query_weight,
        flops=2 * row_count * width * local_width,
    )
    (weight_columns,) = vcall(
        bind(columns_kernel, low_count, quarter),
        [((4 * quarter + experts, 2 * low_count * part), BF16)],
        ids, early_all, *late_all,
        after=[from_queries],
        scratch=[pltpu.VMEM((4, quarter + experts + 16, width // 4), BF16)],
    )
    grad_kv, key_gain_part, grad_in_own, grad_in_send = vcall(
        grad_in_kernel,
        [
            ((row_count, 2 * size), BF16, "near"),
            ((1, size), F32),
            ((row_count // 2, width), BF16, "near"),
            ((row_count // 2, width), BF16, "near"),
        ],
        ids, from_queries, keys_raw, cosine, sine, key_gain, key_matrix, value_matrix, Near(kv_parts),
        scratch=[pltpu.VMEM((row_count, width), BF16)],
        flops=4 * row_count * width * size,
    )
    column_pieces = gather_wa_pieces(weight_columns)
    grad_in_half, sums_own, *sends = vcall(
        half_kernel,
        [((row_count // 2, width), BF16, "near"), ((2 * experts, part), F32)]
        + [((2 * experts, part), BF16, "near")] * (low_count - 1),
        Near(grad_in_own), Near(xor_permute(grad_in_send, "wa", 1)),
        *[Rows(piece, 4 * quarter, experts) for piece in column_pieces],
    )
    out_sums = to_tokens(out_rows, [grad_in_half])
    out_pieces = exchange(out_sums, "lead")
    sums = [sums_own] + [xor_permute(sends[k - 1], "low", k) for k in range(1, low_count)]
    grad_kv_all = exchange([grad_kv] * 4, "lead")
    out_weight_own, *sends = vcall(
        out_weight_kernel,
        [((local_width, part), F32)] + [((local_width, part), BF16)] * (low_count - 1),
        ids, early_all, *column_pieces,
        after=[grad_in_half],
        scratch=[
            pltpu.VMEM((4 * row_count, low_count * part), BF16),
            pltpu.VMEM((4 * row_count, local_width), BF16),
        ],
        flops=8 * row_count * low_count * local_width * part,
    )
    others = [xor_permute(sends[k - 1], "low", k) for k in range(1, low_count)]
    weight_own, *sends = vcall(
        in_weight_kernel,
        [((part, local_width), F32)] + [((part, local_width), BF16)] * (low_count - 1),
        ids, queries_all, *column_pieces,
        after=[grad_in_half],
        scratch=[pltpu.VMEM((4 * row_count, low_count * part), BF16)],
        flops=8 * row_count * low_count * local_width * part,
    )
    weight_others = [xor_permute(sends[k - 1], "low", k) for k in range(1, low_count)]
    token_rows, grad_input_part = vcall(
        token_rows_kernel,
        [((row_count // 2, width), BF16, "near"), ((1, width), F32)],
        ids, tokens, input_norm, grad_branch,
        Near(grad_in_half), Near(xor_permute(grad_in_half, "wa", 2)),
        after=[out_weight_own, weight_own] + grad_kv_all[1:],
    )
    sum_rows = -(-(experts // 2 + 3 + -(-part // 128)) // 16) * 16
    grad_tokens, small_parts = vcall(
        join_kernel,
        [
            ((row_count, width), BF16),
            ((devices, sum_rows, 128), BF16),
        ],
        ids, Near(token_rows), Near(xor_permute(token_rows, "wa", 1)),
        grad_input_part, query_gain_part, key_gain_part,
        *sums,
        after=others + [out_sums[0]],
        scratch=[pltpu.VMEM((devices, sum_rows, 128), F32)],
    )

    kv_weight_own, *sends = vcall(
        kv_weight_kernel,
        [((part, 2 * size), F32)] + [((part, 2 * size), BF16)] * (low_count - 1),
        ids, *grad_kv_all, *column_pieces,
        after=[small_parts],
        scratch=[
            pltpu.VMEM((4 * row_count, low_count * part), BF16),
            pltpu.VMEM((4 * row_count, 2 * size), BF16),
        ],
        flops=8 * row_count * low_count * 2 * size * part,
    )
    kv_others = [xor_permute(sends[k - 1], "low", k) for k in range(1, low_count)]
    (
        output, grad_out_weight, grad_query_weight, grad_key_weight, grad_value_weight,
        grad_router, grad_post_norm, grad_query_gain, grad_key_gain, grad_input_norm,
    ) = vcall(
        bind(last_kernel, low_count),
        [
            ((quarter, width), BF16),
            ((local_width, part), F32),
            ((part, local_width), F32),
            ((part, size), F32),
            ((part, size), F32),
            ((experts, width), F32),
            ((1, width), F32),
            ((1, size), F32),
            ((1, size), F32),
            ((1, part), F32),
        ],
        Near(swap(small_parts, everywhere)), hidden, out_sums[0], out_weight_own, weight_own,
        kv_weight_own, *out_pieces[1:], *others, *weight_others, *near(kv_others),
    )
    return (
        output,
        grad_tokens,
        grad_query_weight,
        grad_key_weight,
        grad_value_weight,
        grad_out_weight,
        grad_query_gain[0],
        grad_key_gain[0],
        grad_input_norm[0],
        grad_post_norm[0],
        grad_router.T,
        grad_gate_weight[None],
        grad_up_weight[None],
        grad_down_weight[None],
    )


def solution(mesh):
    ctx_count, wa_count = mesh.devices.shape
    finer = Mesh(mesh.devices.reshape(4, ctx_count // 4, wa_count), ("lead", "low", "wa"))
    return jax.shard_map(
        on_device,
        mesh=finer,
        in_specs=(
            P(("lead", "low"), None),
            P(("lead", "low")),
            P(("lead", "low", "wa"), None),
            P(None, "wa"),
            P(None, "wa"),
            P(None, "wa"),
            P("wa", None),
            P(),
            P(),
            P(),
            P(),
            P(),
            P(("lead", "low", "wa"), None, None),
            P(("lead", "low", "wa"), None, None),
            P(("lead", "low", "wa"), None, None),
            P(("lead", "low", "wa"), None),
        ),
        out_specs=(
            P(("lead", "low", "wa"), None),
            P(("lead", "low"), None),
            P(("lead", "low"), "wa"),
            P(("lead", "low"), "wa"),
            P(("lead", "low"), "wa"),
            P("wa", ("lead", "low")),
            P(),
            P(),
            P(("lead", "low")),
            P(),
            P(),
            P(("lead", "low", "wa"), None, None),
            P(("lead", "low", "wa"), None, None),
            P(("lead", "low", "wa"), None, None),
        ),
        check_vma=False,
    )
```

profile of v0, /device:TPU:0, one launch (start us, length us, event | category | flops | bytes accessed | tf_op | source)
XLA Modules:
  0.0 267.7 jit_solution(5048703231630282721)
XLA Ops:
  7.2 3.2 %shard_map.281 = (bf16[128,2048]{1,0:T(8,128)(2,1)}, bf16[128,256]{1,0:T(8,128)(2,1)S(1)}, f32[128,128]{1,0:T(8,128)}, f32[128,128]{1,0:T(8,128)}, f32[128,128]{1,0:T(8,128)}) custom-call(bf16[128,2048]{1,0:T(8,128)(2,1)} %refs_1_.8, f32[1,2048]{1,0:T(1,128)} %bitcast.47, bf16[2048,128]{1,0:T(8,128)(2,1)} %refs_6_.3, bf16[2048,128]{1,0:T(8,128)(2,1)} %refs_7_.1, ...), custom_call_target="tpu_custom_call" | custom-call | flops 134217728 | bytes 2369024 | tf_op jit(solution)/shard_map/pallas_call | solution.py:216
  10.3 3.0 %collective-permute-start = (bf16[128,256]{1,0:T(8,128)(2,1)S(1)}, bf16[128,256]{1,0:T(8,128)(2,1)S(1)}, u32[]{:S(2)}, u32[]{:S(2)}) collective-permute-start(bf16[128,256]{1,0:T(8,128)(2,1)S(1)} %get-tuple-element.101.refs_4_), channel_id=1, source_target_pairs={{0,4},{4,0},{8,12},{12,8},{16,20},{20,16},{24,28},{28,24},{1,5},{5... | collective-permute-start | bytes 196616 | tf_op jit(solution)/shard_map/ppermute | solution.py:56
  14.9 3.0 %collective-permute-start.3 = (bf16[128,256]{1,0:T(8,128)(2,1)S(1)}, bf16[128,256]{1,0:T(8,128)(2,1)S(1)}, u32[]{:S(2)}, u32[]{:S(2)}) collective-permute-start(bf16[128,256]{1,0:T(8,128)(2,1)S(1)} %get-tuple-element.101.refs_4_), channel_id=1, source_target_pairs={{0,16},{4,20},{8,24},{12,28},{16,0},{20,4},{24,8},{28,12},{1,17},{... | collective-permute-start | bytes 196616 | tf_op jit(solution)/shard_map/ppermute | solution.py:56
  19.2 3.6 %collective-permute-start.5 = (bf16[128,256]{1,0:T(8,128)(2,1)S(1)}, bf16[128,256]{1,0:T(8,128)(2,1)S(1)}, u32[]{:S(2)}, u32[]{:S(2)}) collective-permute-start(bf16[128,256]{1,0:T(8,128)(2,1)S(1)} %get-tuple-element.101.refs_4_), channel_id=1, source_target_pairs={{0,24},{4,28},{8,16},{12,20},{16,8},{20,12},{24,0},{28,4},{1,25},{... | collective-permute-start | bytes 196616 | tf_op jit(solution)/shard_map/ppermute | solution.py:56
  22.8 4.9 %shard_map.282 = (bf16[2,512,128]{2,1,0:T(8,128)(2,1)}, f32[2,512,128]{2,1,0:T(8,128)}) custom-call(bf16[128,2048]{1,0:T(8,128)(2,1)} %get-tuple-element.97.refs_0_.refs_3_, bf16[2048,1024]{1,0:T(8,128)(2,1)} %refs_1_.7, f32[128,128]{1,0:T(8,128)} %get-tuple-element.98.refs_2_.refs_7_.refs_3_, f32[128,128]{1,0:T(8,128)} %get-tuple-element.99.refs_3_.refs_8_.refs_4_, ...), custom_call_target="tpu_custom_call" | custom-call | flops 536870912 | bytes 5636608 | tf_op jit(solution)/shard_map/pallas_call | solution.py:216
  29.0 4.3 %collective-permute-start.11 = (bf16[32,2176]{1,0:T(8,128)(2,1)S(1)}, bf16[32,2176]{1,0:T(8,128)(2,1)S(1)}, u32[]{:S(2)}, u32[]{:S(2)}) collective-permute-start(bf16[32,2176]{1,0:T(8,128)(2,1)S(1)} %shard_map.284.refs_2_), channel_id=1, source_target_pairs={{0,16},{8,24},{16,0},{24,8},{1,17},{9,25},{17,1},{25,9},{2,18},{10... | collective-permute-start | bytes 417800 | tf_op jit(solution)/shard_map/ppermute | solution.py:56
  33.4 4.0 %shard_map.283 = (bf16[2,512,128]{2,1,0:T(8,128)(2,1)}, bf16[2,512,128]{2,1,0:T(8,128)(2,1)}, bf16[2,512,512]{2,1,0:T(8,128)(2,1)}, bf16[128,1024]{1,0:T(8,128)(...) custom-call(s32[6]{0:T(128)S(1)} %stack.27.refs_0_, ...), custom_call_target="tpu_custom_call" | custom-call | flops 805306368 | bytes 6816256 | tf_op jit(solution)/shard_map/pallas_call | solution.py:216
  39.9 2.3 collective-permute-done.11.refs_4_
  42.2 3.1 %shard_map.285 = (bf16[128,320]{1,0:T(8,128)(2,1)}, bf16[40,2048]{1,0:T(8,128)(2,1)}, bf16[40,2048]{1,0:T(8,128)(2,1)}, bf16[40,2048]{1,0:T(8,128)(2,1)}, bf16[4...) custom-call(s32[6]{0:T(128)S(1)} %stack.27.refs_0_, ...), custom_call_target="tpu_custom_call" | custom-call | flops 167772160 | bytes 1402880 | tf_op jit(solution)/shard_map/pallas_call | solution.py:216
  49.0 2.5 collective-permute-start.18
  54.8 3.0 %shard_map.286 = (bf16[32,2176]{1,0:T(8,128)(2,1)S(1)}, f32[32,2048]{1,0:T(8,128)}, f32[32,32]{1,0:T(8,128)}) custom-call(s32[6]{0:T(128)S(1)} %stack.27.refs_0_, bf16[128,2048]{1,0:T(8,128)(2,1)} %refs_1_.8, s32[8,32]{1,0:T(8,128)} %bitcast.50, f32[1,2048]{1,0:T(1,128)} %bitcast.45, bf16[32,2048]{1,0:T(8,128)(2,1)} %bitcast.43, ...), custom_call_target="tpu_custom_call" | custom-call | flops 4194304 | bytes 1070080 | tf_op jit(solution)/shard_map/pallas_call | solution.py:216
  57.9 2.1 collective-permute-start.20
  61.1 2.8 %collective-permute-done.17.refs_7_.refs_12_ = bf16[40,2048]{1,0:T(8,128)(2,1)S(1)} collective-permute-done((bf16[40,2048]{1,0:T(8,128)(2,1)}, bf16[40,2048]{1,0:T(8,128)(2,1)S(1)}, u32[]{:S(2)}, u32[]{:S(2)}) %collective-permute-start.17) | collective-permute-done | bytes 163872 | tf_op jit(solution)/shard_map/ppermute | solution.py:56
  63.9 2.4 collective-permute-start.22
  66.3 7.0 %collective-permute-done.21.refs_6_ = bf16[32,2176]{1,0:T(8,128)(2,1)S(1)} collective-permute-done((bf16[32,2176]{1,0:T(8,128)(2,1)S(1)}, bf16[32,2176]{1,0:T(8,128)(2,1)S(1)}, u32[]{:S(2)}, u32[]{:S(2)}) %collective-permute-start.21) | collective-permute-done | bytes 139296 | tf_op jit(solution)/shard_map/ppermute | solution.py:56
  73.4 3.3 %shard_map.288 = (bf16[320,2176]{1,0:T(8,128)(2,1)}, bf16[192,1024]{1,0:T(8,128)(2,1)}) custom-call(s32[6]{0:T(128)S(1)} %stack.27.refs_0_, bf16[128,320]{1,0:T(8,128)(2,1)} %get-tuple-element.110.refs_9_.refs_1_, bf16[128,1024]{1,0:T(8,128)(2,1)} %get-tuple-element.122.refs_2_, bf16[128,2048]{1,0:T(8,128)(2,1)} %get-tuple-element.97.refs_0_.refs_3_, ...), custom_call_target="tpu_custom_call" | custom-call | flops 167772160 | bytes 2654208 | tf_op jit(solution)/shard_map/pallas_call | solution.py:216
  76.7 3.6 %all-to-all-start = ((bf16[8,40,2176]{2,1,0:T(8,128)(2,1)}), bf16[8,40,2176]{2,1,0:T(8,128)(2,1)S(1)}, u32[]{:S(2)}, u32[]{:S(2)}) async-start(bf16[8,40,2176]{2,1,0:T(8,128)(2,1)} %bitcast.41), calls=%async_computation | async-start | bytes 2785280 | tf_op jit(solution)/shard_map/all_to_all | solution.py:83
  81.0 5.2 %shard_map.287 = (bf16[320,2048]{1,0:T(8,128)(2,1)}, f32[320,768]{1,0:T(8,128)}) custom-call(s32[6]{0:T(128)S(1)} %stack.27.refs_0_, bf16[768,2048]{1,0:T(8,128)(2,1)} %bitcast.38, bf16[40,2048]{1,0:T(8,128)(2,1)} %get-tuple-element.113.refs_2_, bf16[40,2048]{1,0:T(8,128)(2,1)} %copy-done.15, bf16[40,2048]{1,0:T(8,128)(2,1)} %copy-done.16, ...), custom_call_target="tpu_custom_call" | custom-call | flops 1006632960 | bytes 6750208 | tf_op jit(solution)/shard_map/pallas_call | solution.py:216
  86.3 13.1 %all-to-all-done = bf16[8,40,2176]{2,1,0:T(8,128)(2,1)S(1)} async-done(((bf16[8,40,2176]{2,1,0:T(8,128)(2,1)}), bf16[8,40,2176]{2,1,0:T(8,128)(2,1)S(1)}, u32[]{:S(2)}, u32[]{:S(2)}) %all-to-all-start) | async-done | bytes 1392672 | tf_op jit(solution)/shard_map/all_to_all | solution.py:83
  99.3 10.7 %shard_map.289 = (bf16[320,768]{1,0:T(8,128)(2,1)}, bf16[320,768]{1,0:T(8,128)(2,1)}, bf16[320,768]{1,0:T(8,128)(2,1)}, f32[320,128]{1,0:T(8,128)}, bf16[320,2176]{1,0:T(8,128)(2,1)}) custom-call(s32[6]{0:T(128)S(1)} %stack.27.refs_0_, bf16[2048,768]{1,0:T(8,128)(2,1)} %bitcast.57, bf16[2048,768]{1,0:T(8,128)(2,1)} %bitcast.58, ...), custom_call_target="tpu_custom_call" | custom-call | flops 4026531840 | bytes 10305536 | tf_op jit(solution)/shard_map/pallas_call | solution.py:216
  110.0 3.8 %all-to-all-start.1 = ((bf16[8,40,2176]{2,1,0:T(8,128)(2,1)}), bf16[8,40,2176]{2,1,0:T(8,128)(2,1)S(1)}, u32[]{:S(2)}, u32[]{:S(2)}) async-start(bf16[8,40,2176]{2,1,0:T(8,128)(2,1)} %bitcast.42), calls=%async_computation.1 | async-start | bytes 2785280 | tf_op jit(solution)/shard_map/all_to_all | solution.py:83
  113.8 10.1 %shard_map.290 = (f32[2048,768]{1,0:T(8,128)}, f32[2048,768]{1,0:T(8,128)}, f32[768,2048]{1,0:T(8,128)}) custom-call(bf16[320,2176]{1,0:T(8,128)(2,1)} %bitcast.34, bf16[320,768]{1,0:T(8,128)(2,1)} %get-tuple-element.126.refs_1_, bf16[320,768]{1,0:T(8,128)(2,1)} %get-tuple-element.127.refs_2_, bf16[320,768]{1,0:T(8,128)(2,1)} %get-tuple-element.128.refs_3_.refs_0_, ...), custom_call_target="tpu_custom_call" | custom-call | flops 3019898880 | bytes 23216128 | tf_op jit(solution)/shard_map/pallas_call | solution.py:216
  123.9 8.7 %all-to-all-done.1 = bf16[8,40,2176]{2,1,0:T(8,128)(2,1)S(1)} async-done(((bf16[8,40,2176]{2,1,0:T(8,128)(2,1)}), bf16[8,40,2176]{2,1,0:T(8,128)(2,1)S(1)}, u32[]{:S(2)}, u32[]{:S(2)}) %all-to-all-start.1) | async-done | bytes 1392672 | tf_op jit(solution)/shard_map/all_to_all | solution.py:83
  134.6 3.6 %collective-permute-start.23 = (bf16[32,2176]{1,0:T(8,128)(2,1)S(1)}, bf16[32,2176]{1,0:T(8,128)(2,1)S(1)}, u32[]{:S(2)}, u32[]{:S(2)}) collective-permute-start(bf16[32,2176]{1,0:T(8,128)(2,1)S(1)} %get-tuple-element.134), channel_id=1, source_target_pairs={{0,8},{8,0},{16,24},{24,16},{1,9},{9,1},{17,25},{25,17},{2,10},{10... | collective-permute-start | bytes 417800 | tf_op jit(solution)/shard_map/ppermute | solution.py:56
  140.6 2.2 collective-permute-done.23.refs_7_.refs_3_
  142.8 5.9 %collective-permute-done.24.refs_8_.refs_4_ = bf16[32,2176]{1,0:T(8,128)(2,1)S(1)} collective-permute-done((bf16[32,2176]{1,0:T(8,128)(2,1)S(1)}, bf16[32,2176]{1,0:T(8,128)(2,1)S(1)}, u32[]{:S(2)}, u32[]{:S(2)}) %collective-permute-start.24) | collective-permute-done | bytes 139296 | tf_op jit(solution)/shard_map/ppermute | solution.py:56
  148.7 2.2 shard_map.292
  150.9 2.1 collective-permute-start.29
  153.0 3.7 %collective-permute-start.27 = (bf16[32,2048]{1,0:T(8,128)(2,1)S(1)}, bf16[32,2048]{1,0:T(8,128)(2,1)S(1)}, u32[]{:S(2)}, u32[]{:S(2)}) collective-permute-start(bf16[32,2048]{1,0:T(8,128)(2,1)S(1)} %get-tuple-element.137.refs_10_), channel_id=1, source_target_pairs={{0,2},{1,3},{2,0},{3,1},{4,6},{5,7},{6,4},{7,5},{8,10},{9,11},{10,... | collective-permute-start | bytes 393224 | tf_op jit(solution)/shard_map/ppermute | solution.py:56
  159.3 4.7 %shard_map.293.refs_17_ = bf16[320,2048]{1,0:T(8,128)(2,1)} custom-call(bf16[320,768]{1,0:T(8,128)(2,1)} %get-tuple-element.128.refs_3_.refs_0_, bf16[768,2048]{1,0:T(8,128)(2,1)} %bitcast.39, f32[320,128]{1,0:T(8,128)} %get-tuple-element.130.refs_5_.refs_2_, bf16[32,2176]{1,0:T(8,128)(2,1)} %copy-done.4, bf16[32,2176]{1,0:T(8,128)(2,1)} %copy-done.5, ...), custom_call_target="tpu_custom_call" | custom-call | flops 1006632960 | bytes 5111808 | tf_op jit(solution)/shard_map/pallas_call | solution.py:216
  166.2 9.0 %shard_map.294 = (bf16[128,1024]{1,0:T(8,128)(2,1)}, f32[1,128]{1,0:T(1,128)}, bf16[8,128,256]{2,1,0:T(8,128)(2,1)}, bf16[128,2048]{1,0:T(8,128)(2,1)}) custom-call(s32[6]{0:T(128)S(1)} %stack.27.refs_0_, bf16[2,512,128]{2,1,0:T(8,128)(2,1)} %get-tuple-element.100.refs_1_.refs_2_, bf16[2,512,128]{2,1,0:T(8,128)(2,1)} %get-tuple-element.102.refs_2_, ...), custom_call_target="tpu_custom_call" | custom-call | flops 1073741824 | bytes 7996416 | tf_op jit(solution)/shard_map/pallas_call | solution.py:216
  175.2 4.2 %all-to-all-start.2 = ((bf16[8,128,256]{2,1,0:T(8,128)(2,1)}), bf16[8,128,256]{2,1,0:T(8,128)(2,1)S(1)}, u32[]{:S(2)}, u32[]{:S(2)}) async-start(bf16[8,128,256]{2,1,0:T(8,128)(2,1)} %get-tuple-element.144), calls=%async_computation.2 | async-start | bytes 1048576 | tf_op jit(solution)/shard_map/all_to_all | solution.py:83
  180.2 4.8 %shard_map.295.refs_1_.refs_6_ = f32[128,2048]{1,0:T(8,128)} custom-call(bf16[128,1024]{1,0:T(8,128)(2,1)} %get-tuple-element.142.refs_0_, bf16[2048,1024]{1,0:T(8,128)(2,1)} %refs_1_.7), custom_call_target="tpu_custom_call" | custom-call | flops 536870912 | bytes 5505024 | tf_op jit(solution)/shard_map/pallas_call | solution.py:216
  185.0 3.0 %shard_map.297.refs_2_.refs_5_ = bf16[160,1024]{1,0:T(8,128)(2,1)} custom-call(s32[6]{0:T(128)S(1)} %stack.27.refs_0_, bf16[4,192,1024]{2,1,0:T(8,128)(2,1)} %bitcast.36, bf16[80,512]{1,0:T(8,128)(2,1)} %copy-done.9, bf16[80,512]{1,0:T(8,128)(2,1)} %copy-done.23, bf16[80,512]{1,0:T(8,128)(2,1)} %copy-done.24, bf16[80,512]{1,0:T(8,128)(2,1)} %copy-done.25, ...), custom_call_target="tpu_custom_call" | custom-call | bytes 2228224 | tf_op jit(solution)/shard_map/pallas_call | solution.py:216
  189.9 4.2 %all-to-all-done.2.refs_8_ = bf16[8,128,256]{2,1,0:T(8,128)(2,1)S(1)} async-done(((bf16[8,128,256]{2,1,0:T(8,128)(2,1)}), bf16[8,128,256]{2,1,0:T(8,128)(2,1)S(1)}, u32[]{:S(2)}, u32[]{:S(2)}) %all-to-all-start.2) | async-done | bytes 524320 | tf_op jit(solution)/shard_map/all_to_all | solution.py:83
  194.1 4.2 %all-to-all-start.3 = ((bf16[8,40,2048]{2,1,0:T(8,128)(2,1)}), bf16[8,40,2048]{2,1,0:T(8,128)(2,1)S(1)}, u32[]{:S(2)}, u32[]{:S(2)}) async-start(bf16[8,40,2048]{2,1,0:T(8,128)(2,1)} %bitcast.21), calls=%async_computation.3 | async-start | bytes 2621440 | tf_op jit(solution)/shard_map/all_to_all | solution.py:83
  198.9 3.1 %shard_map.296 = (bf16[128,256]{1,0:T(8,128)(2,1)S(1)}, f32[1,128]{1,0:T(1,128)}, bf16[64,2048]{1,0:T(8,128)(2,1)S(1)}, bf16[64,2048]{1,0:T(8,128)(2,1)S(1)}) custom-call(s32[6]{0:T(128)S(1)} %stack.27.refs_0_, f32[128,2048]{1,0:T(8,128)} %shard_map.295.refs_1_.refs_6_, f32[128,128]{1,0:T(8,128)} %get-tuple-element.143.refs_2_, ...), custom_call_target="tpu_custom_call" | custom-call | flops 134217728 | bytes 2884608 | tf_op jit(solution)/shard_map/pallas_call | solution.py:216
  207.2 4.3 %shard_map.299 = (f32[1024,256]{1,0:T(8,128)}, bf16[1024,256]{1,0:T(8,128)(2,1)}) custom-call(s32[6]{0:T(128)S(1)} %stack.27.refs_0_, bf16[4,192,1024]{2,1,0:T(8,128)(2,1)} %bitcast.37, bf16[160,1024]{1,0:T(8,128)(2,1)} %shard_map.297.refs_2_.refs_5_, bf16[160,1024]{1,0:T(8,128)(2,1)} %copy-done.12, bf16[160,1024]{1,0:T(8,128)(2,1)} %copy-done.11, ...), custom_call_target="tpu_custom_call" | custom-call | flops 536870912 | bytes 4456448 | tf_op jit(solution)/shard_map/pallas_call | solution.py:216
  213.7 2.4 collective-permute-start.38
  217.5 4.1 %shard_map.300 = (f32[256,1024]{1,0:T(8,128)}, bf16[256,1024]{1,0:T(8,128)(2,1)}) custom-call(s32[6]{0:T(128)S(1)} %stack.27.refs_0_, bf16[512,1024]{1,0:T(8,128)(2,1)} %all-gather.5.cloned.1.call-done.refs_1_, bf16[160,1024]{1,0:T(8,128)(2,1)} %shard_map.297.refs_2_.refs_5_, bf16[160,1024]{1,0:T(8,128)(2,1)} %copy-done.12, bf16[160,1024]{1,0:T(8,128)(2,1)} %copy-done.11, ...), custom_call_target="tpu_custom_call" | custom-call | flops 536870912 | bytes 3932160 | tf_op jit(solution)/shard_map/pallas_call | solution.py:216
  223.8 2.7 %shard_map.301 = (bf16[64,2048]{1,0:T(8,128)(2,1)S(1)}, f32[1,2048]{1,0:T(1,128)}) custom-call(s32[6]{0:T(128)S(1)} %stack.27.refs_0_, bf16[128,2048]{1,0:T(8,128)(2,1)} %refs_1_.8, f32[1,2048]{1,0:T(1,128)} %bitcast.48, bf16[128,2048]{1,0:T(8,128)(2,1)} %get-tuple-element.141.refs_3_, bf16[64,2048]{1,0:T(8,128)(2,1)S(1)} %copy-done.1, ...), custom_call_target="tpu_custom_call" | custom-call | bytes 1327104 | tf_op jit(solution)/shard_map/pallas_call | solution.py:216
  232.1 2.8 %shard_map.303 = (bf16[128,2048]{1,0:T(8,128)(2,1)}, bf16[32,32,128]{2,1,0:T(8,128)(2,1)}) custom-call(s32[6]{0:T(128)S(1)} %stack.27.refs_0_, bf16[64,2048]{1,0:T(8,128)(2,1)S(1)} %get-tuple-element.152.refs_1_, bf16[64,2048]{1,0:T(8,128)(2,1)S(1)} %collective-permute-done.40.refs_2_, f32[1,2048]{1,0:T(1,128)} %get-tuple-element.153.refs_3_, ...), custom_call_target="tpu_custom_call" | custom-call | bytes 893952 | tf_op jit(solution)/shard_map/pallas_call | solution.py:216
  234.9 2.9 %all-to-all-start.4 = ((bf16[32,32,128]{2,1,0:T(8,128)(2,1)}), bf16[32,32,128]{2,1,0:T(8,128)(2,1)S(1)}, u32[]{:S(2)}, u32[]{:S(2)}) async-start(bf16[32,32,128]{2,1,0:T(8,128)(2,1)} %get-tuple-element.160.refs_9_), calls=%async_computation.4 | async-start | bytes 524288 | tf_op jit(solution)/shard_map/all_to_all | solution.py:83
  239.7 2.4 collective-permute-start.44
  242.3 3.1 %shard_map.304 = (f32[256,256]{1,0:T(8,128)}, bf16[256,256]{1,0:T(8,128)(2,1)}) custom-call(s32[6]{0:T(128)S(1)} %stack.27.refs_0_, bf16[128,256]{1,0:T(8,128)(2,1)} %copy-done.10, bf16[128,256]{1,0:T(8,128)(2,1)} %copy-done.26, bf16[128,256]{1,0:T(8,128)(2,1)} %copy-done.27, bf16[128,256]{1,0:T(8,128)(2,1)} %copy-done.28, ...), custom_call_target="tpu_custom_call" | custom-call | flops 134217728 | bytes 1966080 | tf_op jit(solution)/shard_map/pallas_call | solution.py:216
  247.3 2.8 %collective-permute-done.43.refs_6_ = bf16[32,2048]{1,0:T(8,128)(2,1)S(1)} collective-permute-done((bf16[32,2048]{1,0:T(8,128)(2,1)S(1)}, bf16[32,2048]{1,0:T(8,128)(2,1)S(1)}, u32[]{:S(2)}, u32[]{:S(2)}) %collective-permute-start.43) | collective-permute-done | bytes 131104 | tf_op jit(solution)/shard_map/ppermute | solution.py:56
  250.1 6.0 %collective-permute-done.44.refs_7_ = bf16[32,2048]{1,0:T(8,128)(2,1)S(1)} collective-permute-done((bf16[32,2048]{1,0:T(8,128)(2,1)S(1)}, bf16[32,2048]{1,0:T(8,128)(2,1)S(1)}, u32[]{:S(2)}, u32[]{:S(2)}) %collective-permute-start.44) | collective-permute-done | bytes 131104 | tf_op jit(solution)/shard_map/ppermute | solution.py:56
  257.0 3.8 %shard_map.305 = (bf16[32,2048]{1,0:T(8,128)(2,1)}, f32[1024,256]{1,0:T(8,128)}, f32[256,1024]{1,0:T(8,128)}, f32[256,128]{1,0:T(8,128)}, f32[256,128]{1,0:T(8,1...) custom-call(bf16[32,32,128]{2,1,0:T(8,128)(2,1)S(1)} %all-to-all-don, ...), custom_call_target="tpu_custom_call" | custom-call | bytes 7088128 | tf_op jit(solution)/shard_map/pallas_call | solution.py:216
  (156 shorter events, 49.2 us)
Async XLA Ops:
  10.3 8.9 %collective-permute-start = (bf16[128,256]{1,0:T(8,128)(2,1)S(1)}, bf16[128,256]{1,0:T(8,128)(2,1)S(1)}, u32[]{:S(2)}, u32[]{:S(2)}) collective-permute-start(bf16[128,256]{1,0:T(8,128)(2,1)S(1)} %get-tuple-element.101.refs_4_), channel_id=1, source_target_pairs={{0,4},{4,0},{8,12},{12,8},{16,20},{20,16},{24,28},{28,24},{1,5},{5... | collective-permute-start | bytes 196616 | tf_op jit(solution)/shard_map/ppermute | solution.py:56
  13.4 9.5 %collective-permute-start.1 = (bf16[128,256]{1,0:T(8,128)(2,1)S(1)}, bf16[128,256]{1,0:T(8,128)(2,1)S(1)}, u32[]{:S(2)}, u32[]{:S(2)}) collective-permute-start(bf16[128,256]{1,0:T(8,128)(2,1)S(1)} %get-tuple-element.101.refs_4_), channel_id=1, source_target_pairs={{0,8},{4,12},{8,0},{12,4},{16,24},{20,28},{24,16},{28,20},{1,9},{5... | collective-permute-start | bytes 196616 | tf_op jit(solution)/shard_map/ppermute | solution.py:56
  14.9 13.8 %collective-permute-start.2 = (bf16[128,256]{1,0:T(8,128)(2,1)S(1)}, bf16[128,256]{1,0:T(8,128)(2,1)S(1)}, u32[]{:S(2)}, u32[]{:S(2)}) collective-permute-start(bf16[128,256]{1,0:T(8,128)(2,1)S(1)} %get-tuple-element.101.refs_4_), channel_id=1, source_target_pairs={{0,12},{4,8},{8,4},{12,0},{16,28},{20,24},{24,20},{28,16},{1,13},{... | collective-permute-start | bytes 196616 | tf_op jit(solution)/shard_map/ppermute | solution.py:56
  14.9 14.0 %collective-permute-start.3 = (bf16[128,256]{1,0:T(8,128)(2,1)S(1)}, bf16[128,256]{1,0:T(8,128)(2,1)S(1)}, u32[]{:S(2)}, u32[]{:S(2)}) collective-permute-start(bf16[128,256]{1,0:T(8,128)(2,1)S(1)} %get-tuple-element.101.refs_4_), channel_id=1, source_target_pairs={{0,16},{4,20},{8,24},{12,28},{16,0},{20,4},{24,8},{28,12},{1,17},{... | collective-permute-start | bytes 196616 | tf_op jit(solution)/shard_map/ppermute | solution.py:56
  17.9 15.4 %collective-permute-start.4 = (bf16[128,256]{1,0:T(8,128)(2,1)S(1)}, bf16[128,256]{1,0:T(8,128)(2,1)S(1)}, u32[]{:S(2)}, u32[]{:S(2)}) collective-permute-start(bf16[128,256]{1,0:T(8,128)(2,1)S(1)} %get-tuple-element.101.refs_4_), channel_id=1, source_target_pairs={{0,20},{4,16},{8,28},{12,24},{16,4},{20,0},{24,12},{28,8},{1,21},{... | collective-permute-start | bytes 196616 | tf_op jit(solution)/shard_map/ppermute | solution.py:56
  19.2 14.1 %collective-permute-start.5 = (bf16[128,256]{1,0:T(8,128)(2,1)S(1)}, bf16[128,256]{1,0:T(8,128)(2,1)S(1)}, u32[]{:S(2)}, u32[]{:S(2)}) collective-permute-start(bf16[128,256]{1,0:T(8,128)(2,1)S(1)} %get-tuple-element.101.refs_4_), channel_id=1, source_target_pairs={{0,24},{4,28},{8,16},{12,20},{16,8},{20,12},{24,0},{28,4},{1,25},{... | collective-permute-start | bytes 196616 | tf_op jit(solution)/shard_map/ppermute | solution.py:56
  22.8 10.5 %collective-permute-start.6 = (bf16[128,256]{1,0:T(8,128)(2,1)S(1)}, bf16[128,256]{1,0:T(8,128)(2,1)S(1)}, u32[]{:S(2)}, u32[]{:S(2)}) collective-permute-start(bf16[128,256]{1,0:T(8,128)(2,1)S(1)} %get-tuple-element.101.refs_4_), channel_id=1, source_target_pairs={{0,28},{4,24},{8,20},{12,16},{16,12},{20,8},{24,4},{28,0},{1,29},{... | collective-permute-start | bytes 196616 | tf_op jit(solution)/shard_map/ppermute | solution.py:56
  28.8 10.8 %collective-permute-start.10 = (bf16[32,2176]{1,0:T(8,128)(2,1)S(1)}, bf16[32,2176]{1,0:T(8,128)(2,1)S(1)}, u32[]{:S(2)}, u32[]{:S(2)}) collective-permute-start(bf16[32,2176]{1,0:T(8,128)(2,1)S(1)} %shard_map.284.refs_2_), channel_id=1, source_target_pairs={{0,8},{8,0},{16,24},{24,16},{1,9},{9,1},{17,25},{25,17},{2,10},{10... | collective-permute-start | bytes 417800 | tf_op jit(solution)/shard_map/ppermute | solution.py:56
  29.0 13.2 %collective-permute-start.11 = (bf16[32,2176]{1,0:T(8,128)(2,1)S(1)}, bf16[32,2176]{1,0:T(8,128)(2,1)S(1)}, u32[]{:S(2)}, u32[]{:S(2)}) collective-permute-start(bf16[32,2176]{1,0:T(8,128)(2,1)S(1)} %shard_map.284.refs_2_), channel_id=1, source_target_pairs={{0,16},{8,24},{16,0},{24,8},{1,17},{9,25},{17,1},{25,9},{2,18},{10... | collective-permute-start | bytes 417800 | tf_op jit(solution)/shard_map/ppermute | solution.py:56
  33.3 8.9 %collective-permute-start.12 = (bf16[32,2176]{1,0:T(8,128)(2,1)S(1)}, bf16[32,2176]{1,0:T(8,128)(2,1)S(1)}, u32[]{:S(2)}, u32[]{:S(2)}) collective-permute-start(bf16[32,2176]{1,0:T(8,128)(2,1)S(1)} %shard_map.284.refs_2_), channel_id=1, source_target_pairs={{0,24},{8,16},{16,8},{24,0},{1,25},{9,17},{17,9},{25,1},{2,26},{10... | collective-permute-start | bytes 417800 | tf_op jit(solution)/shard_map/ppermute | solution.py:56
  38.0 9.0 %collective-permute-start.7 = (bf16[32,2048]{1,0:T(8,128)(2,1)S(1)}, bf16[32,2048]{1,0:T(8,128)(2,1)S(1)}, u32[]{:S(2)}, u32[]{:S(2)}) collective-permute-start(bf16[32,2048]{1,0:T(8,128)(2,1)S(1)} %get-tuple-element.107), channel_id=1, source_target_pairs={{0,1},{1,0},{2,3},{3,2},{4,5},{5,4},{6,7},{7,6},{8,9},{9,8},{10,11... | collective-permute-start | bytes 393224 | tf_op jit(solution)/shard_map/ppermute | solution.py:56
  38.0 9.3 %collective-permute-start.8 = (bf16[32,2048]{1,0:T(8,128)(2,1)S(1)}, bf16[32,2048]{1,0:T(8,128)(2,1)S(1)}, u32[]{:S(2)}, u32[]{:S(2)}) collective-permute-start(bf16[32,2048]{1,0:T(8,128)(2,1)S(1)} %get-tuple-element.108), channel_id=1, source_target_pairs={{0,2},{1,3},{2,0},{3,1},{4,6},{5,7},{6,4},{7,5},{8,10},{9,11},{10,... | collective-permute-start | bytes 393224 | tf_op jit(solution)/shard_map/ppermute | solution.py:56
  39.6 9.2 %collective-permute-start.9 = (bf16[32,2048]{1,0:T(8,128)(2,1)S(1)}, bf16[32,2048]{1,0:T(8,128)(2,1)S(1)}, u32[]{:S(2)}, u32[]{:S(2)}) collective-permute-start(bf16[32,2048]{1,0:T(8,128)(2,1)S(1)} %get-tuple-element.109), channel_id=1, source_target_pairs={{0,3},{1,2},{2,1},{3,0},{4,7},{5,6},{6,5},{7,4},{8,11},{9,10},{10,... | collective-permute-start | bytes 393224 | tf_op jit(solution)/shard_map/ppermute | solution.py:56
  45.4 7.3 %collective-permute-start.14 = (bf16[40,2048]{1,0:T(8,128)(2,1)}, bf16[40,2048]{1,0:T(8,128)(2,1)S(1)}, u32[]{:S(2)}, u32[]{:S(2)}) collective-permute-start(bf16[40,2048]{1,0:T(8,128)(2,1)} %get-tuple-element.115), channel_id=1, source_target_pairs={{0,2},{1,3},{2,0},{3,1},{4,6},{5,7},{6,4},{7,5},{8,10},{9,11},{10,... | collective-permute-start | bytes 491528 | tf_op jit(solution)/shard_map/ppermute | solution.py:56
  47.0 10.9 %collective-permute-start.15 = (bf16[40,2048]{1,0:T(8,128)(2,1)}, bf16[40,2048]{1,0:T(8,128)(2,1)S(1)}, u32[]{:S(2)}, u32[]{:S(2)}) collective-permute-start(bf16[40,2048]{1,0:T(8,128)(2,1)} %get-tuple-element.116), channel_id=1, source_target_pairs={{0,3},{1,2},{2,1},{3,0},{4,7},{5,6},{6,5},{7,4},{8,11},{9,10},{10,... | collective-permute-start | bytes 491528 | tf_op jit(solution)/shard_map/ppermute | solution.py:56
  47.3 12.7 %collective-permute-start.16 = (bf16[40,2048]{1,0:T(8,128)(2,1)}, bf16[40,2048]{1,0:T(8,128)(2,1)S(1)}, u32[]{:S(2)}, u32[]{:S(2)}) collective-permute-start(bf16[40,2048]{1,0:T(8,128)(2,1)} %get-tuple-element.117), channel_id=1, source_target_pairs={{0,4},{1,5},{2,6},{3,7},{4,0},{5,1},{6,2},{7,3},{8,12},{9,13},{10,... | collective-permute-start | bytes 491528 | tf_op jit(solution)/shard_map/ppermute | solution.py:56
  48.8 15.1 %collective-permute-start.17 = (bf16[40,2048]{1,0:T(8,128)(2,1)}, bf16[40,2048]{1,0:T(8,128)(2,1)S(1)}, u32[]{:S(2)}, u32[]{:S(2)}) collective-permute-start(bf16[40,2048]{1,0:T(8,128)(2,1)} %get-tuple-element.118), channel_id=1, source_target_pairs={{0,5},{1,4},{2,7},{3,6},{4,1},{5,0},{6,3},{7,2},{8,13},{9,12},{10,... | collective-permute-start | bytes 491528 | tf_op jit(solution)/shard_map/ppermute | solution.py:56
  49.0 17.3 %collective-permute-start.18 = (bf16[40,2048]{1,0:T(8,128)(2,1)}, bf16[40,2048]{1,0:T(8,128)(2,1)S(1)}, u32[]{:S(2)}, u32[]{:S(2)}) collective-permute-start(bf16[40,2048]{1,0:T(8,128)(2,1)} %get-tuple-element.119), channel_id=1, source_target_pairs={{0,6},{1,7},{2,4},{3,5},{4,2},{5,3},{6,0},{7,1},{8,14},{9,15},{10,... | collective-permute-start | bytes 491528 | tf_op jit(solution)/shard_map/ppermute | solution.py:56
  52.7 13.6 %collective-permute-start.19 = (bf16[40,2048]{1,0:T(8,128)(2,1)}, bf16[40,2048]{1,0:T(8,128)(2,1)S(1)}, u32[]{:S(2)}, u32[]{:S(2)}) collective-permute-start(bf16[40,2048]{1,0:T(8,128)(2,1)} %get-tuple-element.120), channel_id=1, source_target_pairs={{0,7},{1,6},{2,5},{3,4},{4,3},{5,2},{6,1},{7,0},{8,15},{9,14},{10,... | collective-permute-start | bytes 491528 | tf_op jit(solution)/shard_map/ppermute | solution.py:56
  57.9 8.5 %collective-permute-start.20 = (bf16[32,2176]{1,0:T(8,128)(2,1)S(1)}, bf16[32,2176]{1,0:T(8,128)(2,1)S(1)}, u32[]{:S(2)}, u32[]{:S(2)}) collective-permute-start(bf16[32,2176]{1,0:T(8,128)(2,1)S(1)} %get-tuple-element.123.refs_4_), channel_id=1, source_target_pairs={{0,8},{8,0},{16,24},{24,16},{1,9},{9,1},{17,25},{25,17},{2,10},{10... | collective-permute-start | bytes 417800 | tf_op jit(solution)/shard_map/ppermute | solution.py:56
  60.0 13.4 %collective-permute-start.21 = (bf16[32,2176]{1,0:T(8,128)(2,1)S(1)}, bf16[32,2176]{1,0:T(8,128)(2,1)S(1)}, u32[]{:S(2)}, u32[]{:S(2)}) collective-permute-start(bf16[32,2176]{1,0:T(8,128)(2,1)S(1)} %get-tuple-element.123.refs_4_), channel_id=1, source_target_pairs={{0,16},{8,24},{16,0},{24,8},{1,17},{9,25},{17,1},{25,9},{2,18},{10... | collective-permute-start | bytes 417800 | tf_op jit(solution)/shard_map/ppermute | solution.py:56
  63.9 9.5 %collective-permute-start.22 = (bf16[32,2176]{1,0:T(8,128)(2,1)S(1)}, bf16[32,2176]{1,0:T(8,128)(2,1)S(1)}, u32[]{:S(2)}, u32[]{:S(2)}) collective-permute-start(bf16[32,2176]{1,0:T(8,128)(2,1)S(1)} %get-tuple-element.123.refs_4_), channel_id=1, source_target_pairs={{0,24},{8,16},{16,8},{24,0},{1,25},{9,17},{17,9},{25,1},{2,26},{10... | collective-permute-start | bytes 417800 | tf_op jit(solution)/shard_map/ppermute | solution.py:56
  76.7 22.6 %all-to-all-start = ((bf16[8,40,2176]{2,1,0:T(8,128)(2,1)}), bf16[8,40,2176]{2,1,0:T(8,128)(2,1)S(1)}, u32[]{:S(2)}, u32[]{:S(2)}) async-start(bf16[8,40,2176]{2,1,0:T(8,128)(2,1)} %bitcast.41), calls=%async_computation | async-start | bytes 2785280 | tf_op jit(solution)/shard_map/all_to_all | solution.py:83
  80.3 43.6 %all-gather.3.cloned.1.call-start = ((), (), s32[]{:S(2)}) async-start(), calls=%async_computation.5 | async-start | bytes 1966080 | tf_op jit(solution)/shard_map/all_gather | solution.py:79
  110.0 22.6 %all-to-all-start.1 = ((bf16[8,40,2176]{2,1,0:T(8,128)(2,1)}), bf16[8,40,2176]{2,1,0:T(8,128)(2,1)S(1)}, u32[]{:S(2)}, u32[]{:S(2)}) async-start(bf16[8,40,2176]{2,1,0:T(8,128)(2,1)} %bitcast.42), calls=%async_computation.1 | async-start | bytes 2785280 | tf_op jit(solution)/shard_map/all_to_all | solution.py:83
  134.6 8.2 %collective-permute-start.23 = (bf16[32,2176]{1,0:T(8,128)(2,1)S(1)}, bf16[32,2176]{1,0:T(8,128)(2,1)S(1)}, u32[]{:S(2)}, u32[]{:S(2)}) collective-permute-start(bf16[32,2176]{1,0:T(8,128)(2,1)S(1)} %get-tuple-element.134), channel_id=1, source_target_pairs={{0,8},{8,0},{16,24},{24,16},{1,9},{9,1},{17,25},{25,17},{2,10},{10... | collective-permute-start | bytes 417800 | tf_op jit(solution)/shard_map/ppermute | solution.py:56
  138.2 10.5 %collective-permute-start.24 = (bf16[32,2176]{1,0:T(8,128)(2,1)S(1)}, bf16[32,2176]{1,0:T(8,128)(2,1)S(1)}, u32[]{:S(2)}, u32[]{:S(2)}) collective-permute-start(bf16[32,2176]{1,0:T(8,128)(2,1)S(1)} %get-tuple-element.135), channel_id=1, source_target_pairs={{0,16},{8,24},{16,0},{24,8},{1,17},{9,25},{17,1},{25,9},{2,18},{10... | collective-permute-start | bytes 417800 | tf_op jit(solution)/shard_map/ppermute | solution.py:56
  139.2 9.5 %collective-permute-start.25 = (bf16[32,2176]{1,0:T(8,128)(2,1)S(1)}, bf16[32,2176]{1,0:T(8,128)(2,1)S(1)}, u32[]{:S(2)}, u32[]{:S(2)}) collective-permute-start(bf16[32,2176]{1,0:T(8,128)(2,1)S(1)} %get-tuple-element.136), channel_id=1, source_target_pairs={{0,24},{8,16},{16,8},{24,0},{1,25},{9,17},{17,9},{25,1},{2,26},{10... | collective-permute-start | bytes 417800 | tf_op jit(solution)/shard_map/ppermute | solution.py:56
  150.9 7.0 %collective-permute-start.29 = (bf16[80,512]{1,0:T(8,128)(2,1)S(1)}, bf16[80,512]{1,0:T(8,128)(2,1)S(1)}, u32[]{:S(2)}, u32[]{:S(2)}) collective-permute-start(bf16[80,512]{1,0:T(8,128)(2,1)S(1)} %get-tuple-element.138), channel_id=1, source_target_pairs={{0,8},{8,0},{16,24},{24,16},{1,9},{9,1},{17,25},{25,17},{2,10},{10... | collective-permute-start | bytes 245768 | tf_op jit(solution)/shard_map/ppermute | solution.py:56
  153.0 12.6 %collective-permute-start.26 = (bf16[32,2048]{1,0:T(8,128)(2,1)S(1)}, bf16[32,2048]{1,0:T(8,128)(2,1)S(1)}, u32[]{:S(2)}, u32[]{:S(2)}) collective-permute-start(bf16[32,2048]{1,0:T(8,128)(2,1)S(1)} %get-tuple-element.137.refs_10_), channel_id=1, source_target_pairs={{0,1},{1,0},{2,3},{3,2},{4,5},{5,4},{6,7},{7,6},{8,9},{9,8},{10,11... | collective-permute-start | bytes 393224 | tf_op jit(solution)/shard_map/ppermute | solution.py:56
  153.0 12.6 %collective-permute-start.27 = (bf16[32,2048]{1,0:T(8,128)(2,1)S(1)}, bf16[32,2048]{1,0:T(8,128)(2,1)S(1)}, u32[]{:S(2)}, u32[]{:S(2)}) collective-permute-start(bf16[32,2048]{1,0:T(8,128)(2,1)S(1)} %get-tuple-element.137.refs_10_), channel_id=1, source_target_pairs={{0,2},{1,3},{2,0},{3,1},{4,6},{5,7},{6,4},{7,5},{8,10},{9,11},{10,... | collective-permute-start | bytes 393224 | tf_op jit(solution)/shard_map/ppermute | solution.py:56
  156.7 8.8 %collective-permute-start.28 = (bf16[32,2048]{1,0:T(8,128)(2,1)S(1)}, bf16[32,2048]{1,0:T(8,128)(2,1)S(1)}, u32[]{:S(2)}, u32[]{:S(2)}) collective-permute-start(bf16[32,2048]{1,0:T(8,128)(2,1)S(1)} %get-tuple-element.137.refs_10_), channel_id=1, source_target_pairs={{0,3},{1,2},{2,1},{3,0},{4,7},{5,6},{6,5},{7,4},{8,11},{9,10},{10,... | collective-permute-start | bytes 393224 | tf_op jit(solution)/shard_map/ppermute | solution.py:56
  156.9 8.7 %collective-permute-start.30 = (bf16[80,512]{1,0:T(8,128)(2,1)S(1)}, bf16[80,512]{1,0:T(8,128)(2,1)S(1)}, u32[]{:S(2)}, u32[]{:S(2)}) collective-permute-start(bf16[80,512]{1,0:T(8,128)(2,1)S(1)} %get-tuple-element.139), channel_id=1, source_target_pairs={{0,16},{8,24},{16,0},{24,8},{1,17},{9,25},{17,1},{25,9},{2,18},{10... | collective-permute-start | bytes 245768 | tf_op jit(solution)/shard_map/ppermute | solution.py:56
  157.9 7.7 %collective-permute-start.31 = (bf16[80,512]{1,0:T(8,128)(2,1)S(1)}, bf16[80,512]{1,0:T(8,128)(2,1)S(1)}, u32[]{:S(2)}, u32[]{:S(2)}) collective-permute-start(bf16[80,512]{1,0:T(8,128)(2,1)S(1)} %get-tuple-element.140), channel_id=1, source_target_pairs={{0,24},{8,16},{16,8},{24,0},{1,25},{9,17},{17,9},{25,1},{2,26},{10... | collective-permute-start | bytes 245768 | tf_op jit(solution)/shard_map/ppermute | solution.py:56
  175.2 18.9 %all-to-all-start.2 = ((bf16[8,128,256]{2,1,0:T(8,128)(2,1)}), bf16[8,128,256]{2,1,0:T(8,128)(2,1)S(1)}, u32[]{:S(2)}, u32[]{:S(2)}) async-start(bf16[8,128,256]{2,1,0:T(8,128)(2,1)} %get-tuple-element.144), calls=%async_computation.2 | async-start | bytes 1048576 | tf_op jit(solution)/shard_map/all_to_all | solution.py:83
  179.4 38.0 %all-gather.5.cloned.1.call-start = ((), (), s32[]{:S(2)}) async-start(), calls=%async_computation.6 | async-start | bytes 1310720 | tf_op jit(solution)/shard_map/all_gather | solution.py:79
  187.9 10.9 %collective-permute-start.34 = (bf16[160,1024]{1,0:T(8,128)(2,1)}, bf16[160,1024]{1,0:T(8,128)(2,1)S(1)}, u32[]{:S(2)}, u32[]{:S(2)}) collective-permute-start(bf16[160,1024]{1,0:T(8,128)(2,1)} %shard_map.297.refs_2_.refs_5_), channel_id=1, source_target_pairs={{0,2},{1,3},{2,0},{3,1},{4,6},{5,7},{6,4},{7,5},{8,10},{9,11},{10,... | collective-permute-start | bytes 983048 | tf_op jit(solution)/shard_map/ppermute | solution.py:56
  194.1 34.6 %all-to-all-start.3 = ((bf16[8,40,2048]{2,1,0:T(8,128)(2,1)}), bf16[8,40,2048]{2,1,0:T(8,128)(2,1)S(1)}, u32[]{:S(2)}, u32[]{:S(2)}) async-start(bf16[8,40,2048]{2,1,0:T(8,128)(2,1)} %bitcast.21), calls=%async_computation.3 | async-start | bytes 2621440 | tf_op jit(solution)/shard_map/all_to_all | solution.py:83
  205.3 16.9 %collective-permute-start.36 = (bf16[64,2048]{1,0:T(8,128)(2,1)S(1)}, bf16[64,2048]{1,0:T(8,128)(2,1)S(1)}, u32[]{:S(2)}, u32[]{:S(2)}) collective-permute-start(bf16[64,2048]{1,0:T(8,128)(2,1)S(1)} %get-tuple-element.148.refs_6_.refs_4_.refs_3_), channel_id=1, source_target_pairs={{0,2},{1,3},{2,0},{3,1},{4,6},{5,7},{6,4},{7,5},{8,10},{9,11},{10,... | collective-permute-start | bytes 786440 | tf_op jit(solution)/shard_map/ppermute | solution.py:56
  211.5 19.8 %collective-permute-start.42 = (bf16[1024,256]{1,0:T(8,128)(2,1)}, bf16[1024,256]{1,0:T(8,128)(2,1)S(1)}, u32[]{:S(2)}, u32[]{:S(2)}) collective-permute-start(bf16[1024,256]{1,0:T(8,128)(2,1)} %get-tuple-element.158), channel_id=1, source_target_pairs={{0,4},{4,0},{1,5},{5,1},{2,6},{6,2},{3,7},{7,3},{8,12},{12,8},{9,1... | collective-permute-start | bytes 1572872 | tf_op jit(solution)/shard_map/ppermute | solution.py:56
  213.1 8.5 %collective-permute-start.37 = (bf16[128,256]{1,0:T(8,128)(2,1)S(1)}, bf16[128,256]{1,0:T(8,128)(2,1)S(1)}, u32[]{:S(2)}, u32[]{:S(2)}) collective-permute-start(bf16[128,256]{1,0:T(8,128)(2,1)S(1)} %get-tuple-element.151.refs_1_), channel_id=1, source_target_pairs={{0,8},{8,0},{16,24},{24,16},{1,9},{9,1},{17,25},{25,17},{2,10},{10... | collective-permute-start | bytes 196616 | tf_op jit(solution)/shard_map/ppermute | solution.py:56
  213.7 8.0 %collective-permute-start.38 = (bf16[128,256]{1,0:T(8,128)(2,1)S(1)}, bf16[128,256]{1,0:T(8,128)(2,1)S(1)}, u32[]{:S(2)}, u32[]{:S(2)}) collective-permute-start(bf16[128,256]{1,0:T(8,128)(2,1)S(1)} %get-tuple-element.151.refs_1_), channel_id=1, source_target_pairs={{0,16},{8,24},{16,0},{24,8},{1,17},{9,25},{17,1},{25,9},{2,18},{10... | collective-permute-start | bytes 196616 | tf_op jit(solution)/shard_map/ppermute | solution.py:56
  227.2 28.9 %collective-permute-start.46 = (bf16[256,1024]{1,0:T(8,128)(2,1)}, bf16[256,1024]{1,0:T(8,128)(2,1)S(1)}, u32[]{:S(2)}, u32[]{:S(2)}) collective-permute-start(bf16[256,1024]{1,0:T(8,128)(2,1)} %get-tuple-element.165), channel_id=1, source_target_pairs={{0,4},{4,0},{1,5},{5,1},{2,6},{6,2},{3,7},{7,3},{8,12},{12,8},{9,1... | collective-permute-start | bytes 1572872 | tf_op jit(solution)/shard_map/ppermute | solution.py:56
  234.9 21.2 %all-to-all-start.4 = ((bf16[32,32,128]{2,1,0:T(8,128)(2,1)}), bf16[32,32,128]{2,1,0:T(8,128)(2,1)S(1)}, u32[]{:S(2)}, u32[]{:S(2)}) async-start(bf16[32,32,128]{2,1,0:T(8,128)(2,1)} %get-tuple-element.160.refs_9_), calls=%async_computation.4 | async-start | bytes 524288 | tf_op jit(solution)/shard_map/all_to_all | solution.py:83
  237.8 12.2 %collective-permute-start.43 = (bf16[32,2048]{1,0:T(8,128)(2,1)S(1)}, bf16[32,2048]{1,0:T(8,128)(2,1)S(1)}, u32[]{:S(2)}, u32[]{:S(2)}) collective-permute-start(bf16[32,2048]{1,0:T(8,128)(2,1)S(1)} %get-tuple-element.162), channel_id=1, source_target_pairs={{0,8},{8,0},{16,24},{24,16},{1,9},{9,1},{17,25},{25,17},{2,10},{10... | collective-permute-start | bytes 393224 | tf_op jit(solution)/shard_map/ppermute | solution.py:56
  239.7 16.4 %collective-permute-start.44 = (bf16[32,2048]{1,0:T(8,128)(2,1)S(1)}, bf16[32,2048]{1,0:T(8,128)(2,1)S(1)}, u32[]{:S(2)}, u32[]{:S(2)}) collective-permute-start(bf16[32,2048]{1,0:T(8,128)(2,1)S(1)} %get-tuple-element.163), channel_id=1, source_target_pairs={{0,16},{8,24},{16,0},{24,8},{1,17},{9,25},{17,1},{25,9},{2,18},{10... | collective-permute-start | bytes 393224 | tf_op jit(solution)/shard_map/ppermute | solution.py:56
  242.1 14.0 %collective-permute-start.45 = (bf16[32,2048]{1,0:T(8,128)(2,1)S(1)}, bf16[32,2048]{1,0:T(8,128)(2,1)S(1)}, u32[]{:S(2)}, u32[]{:S(2)}) collective-permute-start(bf16[32,2048]{1,0:T(8,128)(2,1)S(1)} %get-tuple-element.164), channel_id=1, source_target_pairs={{0,24},{8,16},{16,8},{24,0},{1,25},{9,17},{17,9},{25,1},{2,26},{10... | collective-permute-start | bytes 393224 | tf_op jit(solution)/shard_map/ppermute | solution.py:56
  245.4 10.7 %collective-permute-start.47 = (bf16[256,256]{1,0:T(8,128)(2,1)}, bf16[256,256]{1,0:T(8,128)(2,1)S(1)}, u32[]{:S(2)}, u32[]{:S(2)}) collective-permute-start(bf16[256,256]{1,0:T(8,128)(2,1)} %get-tuple-element.166), channel_id=1, source_target_pairs={{0,4},{4,0},{1,5},{5,1},{2,6},{6,2},{3,7},{7,3},{8,12},{12,8},{9,1... | collective-permute-start | bytes 393224 | tf_op jit(solution)/shard_map/ppermute | solution.py:56
  (40 other events, 242.3 us)
Sparse Core Ops, SparseCore 0:
  82.7 39.6 all-gather.2
  181.8 29.7 all-gather.4
where the time goes:
time: 269 us; the launch traced here: 268 us
  Pallas kernels  101 us (38%)
  starting transfers between devices  84.8 us (32%)
  waiting for transfers between devices  60.6 us (23%)
  between operations  14.7 us (5%)
  local copies, waits for them, and re-layouts  6.22 us (2%)
    pallas_call x25, Pallas kernels, vcall(): pl.pallas_call(kernel, out_shape=[jax.ShapeDtypeStruct(s, d) if c else pl...  101 us
    ppermute x48, starting transfers between devices, xor_permute(): return lax.ppermute(value, axis, [(i, i ^ offset) for i in range(count)])  65.6 us
    ppermute x48, waiting for transfers between devices, xor_permute(): return lax.ppermute(value, axis, [(i, i ^ offset) for i in range(count)])  33.6 us
    all_to_all x5, waiting for transfers between devices, swap(): return lax.all_to_all(value, axes, split_axis=0, concat_axis=0, tiled=True)  26 us
    all_to_all x5, starting transfers between devices, swap(): return lax.all_to_all(value, axes, split_axis=0, concat_axis=0, tiled=True)  18.7 us
    unnamed x66, local copies, waits for them, and re-layouts  6.13 us
  transfers between devices with their start and end apart: 55, of which 14 were waited for; matrix products, arithmetic and copies ran while one was open for 0% of the time, Pallas kernels for 29%

commit v1 on v0

--- a/solution.py
+++ b/solution.py
@@ -135,7 +135,7 @@
     return [Near(value) for value in values]
 
 
-def vcall(body, outs, *operands, scratch=(), after=(), split=None, flops=0, megabytes=24):
+def vcall(body, outs, *operands, scratch=(), after=(), split=None, loose=(), flops=0, megabytes=24):
     split = split or {}
     close = [isinstance(o, Near) for o in operands]
     ranges = {i: (o.first, o.count) for i, o in enumerate(operands) if isinstance(o, Rows)}
@@ -153,11 +153,12 @@
     sizes = [o.size * o.dtype.itemsize for o in arrays]
     in_parts = [split.get(i, 1) for i in places]
     out_parts = [split.get(-1 - i, 1) for i in far_outs]
+    out_parts = [len(p) if isinstance(p, tuple) else p for p in out_parts]
     count = len(arrays)
 
     def kernel(*refs):
         given = list(refs[: len(operands)])
-        rest = refs[len(operands) + len(after) :]
+        rest = refs[len(operands) + len(after) + len(loose) :]
         results, rest = rest[: len(outs)], rest[len(outs) :]
         inner = count + len(far_outs)
         buffers, sems, own = rest[:inner], rest[inner], rest[inner + 1 :]
@@ -189,8 +190,11 @@
             copies = []
             for c in range(parts):
                 step = result.shape[0] // parts
-                if parts > 1:
+                cuts = split.get(-1 - i)
+                if isinstance(cuts, tuple) or parts > 1:
                     piece = pl.ds(c * step, step)
+                    if isinstance(cuts, tuple):
+                        piece = (slice(None), pl.ds(*cuts[c]))
                     copy = pltpu.make_async_copy(source.at[piece], result.at[piece], sems.at[used])
                 else:
                     copy = pltpu.make_async_copy(source, result, sems.at[used])
@@ -225,7 +229,8 @@
             else (pl.BlockSpec(memory_space=pltpu.VMEM) if c else in_hbm)
             for o, c in zip(operands, close)
         ]
-        + [in_hbm] * len(after),
+        + [in_hbm] * len(after)
+        + [pl.BlockSpec(memory_space=pl.ANY)] * len(loose),
         out_specs=[pl.BlockSpec(memory_space=pltpu.VMEM) if c else in_hbm for c in close_out],
         scratch_shapes=[pltpu.VMEM(o.shape, o.dtype) for o in arrays]
         + [pltpu.VMEM(*outs[i]) for i in far_outs]
@@ -233,7 +238,7 @@
         + list(scratch),
         compiler_params=pltpu.CompilerParams(vmem_limit_bytes=megabytes << 20),
         cost_estimate=pl.CostEstimate(flops=flops, bytes_accessed=moved, transcendentals=0),
-    )(*[pinned(o) if i in places else o for i, o in enumerate(operands)], *[pinned(o) for o in after])
+    )(*[pinned(o) if i in places else o for i, o in enumerate(operands)], *[pinned(o) for o in after], *loose)
 
 
 def as_column(row):
@@ -485,11 +490,14 @@
         du_out[:, here] = (grad_act * lifted).astype(BF16)
     for out in (act_out, dg_out, du_out, prob_out):
         out.send()
-    grad_in = contract_last(dg_out[...], wg[...]) + contract_last(du_out[...], wu[...])
-    back[:, :width] = grad_in.astype(BF16)
     high = gate_grad.astype(BF16).astype(F32)
     tail = jnp.where(mine_high, high, jnp.where(mine_low, gate_grad - high, 0.0))
     back[:, width:] = tail.astype(BF16)
+    for c in range(4):
+        here = slice(c * width // 4, (c + 1) * width // 4)
+        grad_in = contract_last(dg_out[...], wg[here]) + contract_last(du_out[...], wu[here])
+        back[:, here] = grad_in.astype(BF16)
+        back.send(c)
 
 
 def expert_weights_kernel(rows, dg, du, act, cot_rows, prob, gate_out, up_out, down_out):
@@ -964,7 +972,7 @@
             ((slot_rows, width + extra), BF16),
         ],
         ids, gate_weight, up_weight, grad_raw, Near(rows_in),
-        split={1: 3, 2: 3},
+        split={1: 3, 2: 3, -5: tuple((c * width // 4, width // 4 + (extra if c == 3 else 0)) for c in range(4))},
         flops=8 * slot_rows * hidden_units * width,
         megabytes=48,
     )
@@ -982,10 +990,10 @@
         megabytes=40,
     )
 
-    def to_tokens(rows, after):
+    def to_tokens(rows, after, place):
         return vcall(
             combine_kernel,
-            [((quarter, rows.shape[1]), F32, "near")]
+            [((quarter, rows.shape[1]), F32, *place)]
             + [((quarter, rows.shape[1]), BF16, "near")] * 3,
             ids, chosen, Near(rows),
             after=after,
@@ -994,7 +1002,7 @@
         )
 
     back = swap(back, plane)
-    back_pieces = exchange(to_tokens(back, [grad_gate_weight, early_all]), "lead")
+    back_pieces = exchange(to_tokens(back, [grad_gate_weight, early_all], ["near"]), "lead")
     (out_rows,) = vcall(
         out_rows_kernel,
         [((slot_rows, width), BF16)],
@@ -1028,7 +1036,8 @@
         ids, q_heads, keys_seq, values_seq, weights_low, queries_raw, out_weight,
         cosine, sine, query_gain, *near(grad_pieces),
         split={6: 4},
-        after=late_all[1:] + [out_made],
+        after=[out_made],
+        loose=late_all[1:],
         scratch=[pltpu.VMEM((heads * span, size), BF16)],
         flops=2 * row_count * width * local_width + 8 * row_count * local_width * length,
         megabytes=48,
@@ -1044,7 +1053,7 @@
     (weight_columns,) = vcall(
         bind(columns_kernel, low_count, quarter),
         [((4 * quarter + experts, 2 * low_count * part), BF16)],
-        ids, early_all, *late_all,
+        ids, early_all, *near(late_all),
         after=[from_queries],
         scratch=[pltpu.VMEM((4, quarter + experts + 16, width // 4), BF16)],
     )
@@ -1068,7 +1077,7 @@
         Near(grad_in_own), Near(xor_permute(grad_in_send, "wa", 1)),
         *[Rows(piece, 4 * quarter, experts) for piece in column_pieces],
     )
-    out_sums = to_tokens(out_rows, [grad_in_half])
+    out_sums = to_tokens(out_rows, [grad_in_half], [])
     out_pieces = exchange(out_sums, "lead")
     sums = [sums_own] + [xor_permute(sends[k - 1], "low", k) for k in range(1, low_count)]
     grad_kv_all = exchange([grad_kv] * 4, "lead")
@@ -1098,7 +1107,8 @@
         [((row_count // 2, width), BF16, "near"), ((1, width), F32)],
         ids, tokens, input_norm, grad_branch,
         Near(grad_in_half), Near(xor_permute(grad_in_half, "wa", 2)),
-        after=[out_weight_own, weight_own] + grad_kv_all[1:],
+        after=[out_weight_own, weight_own],
+        loose=grad_kv_all[1:],
     )
     sum_rows = -(-(experts // 2 + 3 + -(-part // 128)) // 16) * 16
     grad_tokens, small_parts = vcall(
@@ -1110,14 +1120,15 @@
         ids, Near(token_rows), Near(xor_permute(token_rows, "wa", 1)),
         grad_input_part, query_gain_part, key_gain_part,
         *sums,
-        after=others + [out_sums[0]],
+        after=[out_sums[0]],
+        loose=others,
         scratch=[pltpu.VMEM((devices, sum_rows, 128), F32)],
     )
 
     kv_weight_own, *sends = vcall(
         kv_weight_kernel,
         [((part, 2 * size), F32)] + [((part, 2 * size), BF16)] * (low_count - 1),
-        ids, *grad_kv_all, *column_pieces,
+        ids, *near(grad_kv_all), *column_pieces,
         after=[small_parts],
         scratch=[
             pltpu.VMEM((4 * row_count, low_count * part), BF16),
@@ -1144,7 +1155,7 @@
             ((1, part), F32),
         ],
         Near(swap(small_parts, everywhere)), hidden, out_sums[0], out_weight_own, weight_own,
-        kv_weight_own, *out_pieces[1:], *others, *weight_others, *near(kv_others),
+        kv_weight_own, *out_pieces[1:], *near(others + weight_others + kv_others),
     )
     return (
         output,

time: 269 us -> 266 us (0.989)
  local copies, waits for them, and re-layouts: 6.22 us -> 3.33 us
    unnamed x66 -> x42, local copies, waits for them, and re-layouts: 6.13 us -> 3.25 us
  transfers between devices with their start and end apart: 55 -> 55, of which waited for: 14 -> 14; matrix products, arithmetic and copies ran while one was open for 0% -> 0% of each run, Pallas kernels for 29% -> 30%
where the time goes in v1:
time: 266 us; the launch traced here: 265 us
  Pallas kernels  102 us (38%)
  starting transfers between devices  84.8 us (32%)
  waiting for transfers between devices  60.8 us (23%)
  between operations  14.6 us (5%)
  local copies, waits for them, and re-layouts  3.33 us (1%)
    pallas_call x25, Pallas kernels, vcall(): pl.pallas_call(kernel, out_shape=[jax.ShapeDtypeStruct(s, d) if c else pl...  102 us
    ppermute x48, starting transfers between devices, xor_permute(): return lax.ppermute(value, axis, [(i, i ^ offset) for i in range(count)])  65.6 us
    ppermute x48, waiting for transfers between devices, xor_permute(): return lax.ppermute(value, axis, [(i, i ^ offset) for i in range(count)])  33.6 us
    all_to_all x5, waiting for transfers between devices, swap(): return lax.all_to_all(value, axes, split_axis=0, concat_axis=0, tiled=True)  26.2 us
    all_to_all x5, starting transfers between devices, swap(): return lax.all_to_all(value, axes, split_axis=0, concat_axis=0, tiled=True)  18.6 us
  transfers between devices with their start and end apart: 55, of which 14 were waited for; matrix products, arithmetic and copies ran while one was open for 0% of the time, Pallas kernels for 30%

profile of v1, /device:TPU:0, one launch (start us, length us, event | category | flops | bytes accessed | tf_op | source)
XLA Modules:
  0.0 265.1 jit_solution(11215950716393720629)
XLA Ops:
  7.2 3.1 %shard_map.281 = (bf16[128,2048]{1,0:T(8,128)(2,1)}, bf16[128,256]{1,0:T(8,128)(2,1)S(1)}, f32[128,128]{1,0:T(8,128)}, f32[128,128]{1,0:T(8,128)}, f32[128,128]{1,0:T(8,128)}) custom-call(bf16[128,2048]{1,0:T(8,128)(2,1)} %refs_1_.8, f32[1,2048]{1,0:T(1,128)} %bitcast.48, bf16[2048,128]{1,0:T(8,128)(2,1)} %refs_6_.3, bf16[2048,128]{1,0:T(8,128)(2,1)} %refs_7_.1, ...), custom_call_target="tpu_custom_call" | custom-call | flops 134217728 | bytes 2369024 | tf_op jit(solution)/shard_map/pallas_call | solution.py:220
  10.3 3.0 %collective-permute-start = (bf16[128,256]{1,0:T(8,128)(2,1)S(1)}, bf16[128,256]{1,0:T(8,128)(2,1)S(1)}, u32[]{:S(2)}, u32[]{:S(2)}) collective-permute-start(bf16[128,256]{1,0:T(8,128)(2,1)S(1)} %get-tuple-element.101.refs_4_), channel_id=1, source_target_pairs={{0,4},{4,0},{8,12},{12,8},{16,20},{20,16},{24,28},{28,24},{1,5},{5... | collective-permute-start | bytes 196616 | tf_op jit(solution)/shard_map/ppermute | solution.py:56
  14.9 3.0 %collective-permute-start.3 = (bf16[128,256]{1,0:T(8,128)(2,1)S(1)}, bf16[128,256]{1,0:T(8,128)(2,1)S(1)}, u32[]{:S(2)}, u32[]{:S(2)}) collective-permute-start(bf16[128,256]{1,0:T(8,128)(2,1)S(1)} %get-tuple-element.101.refs_4_), channel_id=1, source_target_pairs={{0,16},{4,20},{8,24},{12,28},{16,0},{20,4},{24,8},{28,12},{1,17},{... | collective-permute-start | bytes 196616 | tf_op jit(solution)/shard_map/ppermute | solution.py:56
  19.2 3.6 %collective-permute-start.5 = (bf16[128,256]{1,0:T(8,128)(2,1)S(1)}, bf16[128,256]{1,0:T(8,128)(2,1)S(1)}, u32[]{:S(2)}, u32[]{:S(2)}) collective-permute-start(bf16[128,256]{1,0:T(8,128)(2,1)S(1)} %get-tuple-element.101.refs_4_), channel_id=1, source_target_pairs={{0,24},{4,28},{8,16},{12,20},{16,8},{20,12},{24,0},{28,4},{1,25},{... | collective-permute-start | bytes 196616 | tf_op jit(solution)/shard_map/ppermute | solution.py:56
  22.8 4.8 %shard_map.282 = (bf16[2,512,128]{2,1,0:T(8,128)(2,1)}, f32[2,512,128]{2,1,0:T(8,128)}) custom-call(bf16[128,2048]{1,0:T(8,128)(2,1)} %get-tuple-element.97.refs_0_.refs_3_, bf16[2048,1024]{1,0:T(8,128)(2,1)} %refs_1_.7, f32[128,128]{1,0:T(8,128)} %get-tuple-element.98.refs_2_.refs_7_.refs_3_, f32[128,128]{1,0:T(8,128)} %get-tuple-element.99.refs_3_.refs_8_.refs_4_, ...), custom_call_target="tpu_custom_call" | custom-call | flops 536870912 | bytes 5636608 | tf_op jit(solution)/shard_map/pallas_call | solution.py:220
  28.9 4.3 %collective-permute-start.11 = (bf16[32,2176]{1,0:T(8,128)(2,1)S(1)}, bf16[32,2176]{1,0:T(8,128)(2,1)S(1)}, u32[]{:S(2)}, u32[]{:S(2)}) collective-permute-start(bf16[32,2176]{1,0:T(8,128)(2,1)S(1)} %shard_map.284.refs_2_), channel_id=1, source_target_pairs={{0,16},{8,24},{16,0},{24,8},{1,17},{9,25},{17,1},{25,9},{2,18},{10... | collective-permute-start | bytes 417800 | tf_op jit(solution)/shard_map/ppermute | solution.py:56
  33.3 4.0 %shard_map.283 = (bf16[2,512,128]{2,1,0:T(8,128)(2,1)}, bf16[2,512,128]{2,1,0:T(8,128)(2,1)}, bf16[2,512,512]{2,1,0:T(8,128)(2,1)}, bf16[128,1024]{1,0:T(8,128)(...) custom-call(s32[6]{0:T(128)S(1)} %stack.27.refs_0_, ...), custom_call_target="tpu_custom_call" | custom-call | flops 805306368 | bytes 6816256 | tf_op jit(solution)/shard_map/pallas_call | solution.py:220
  39.8 2.3 collective-permute-done.11.refs_4_
  42.2 3.1 %shard_map.285 = (bf16[128,320]{1,0:T(8,128)(2,1)}, bf16[40,2048]{1,0:T(8,128)(2,1)}, bf16[40,2048]{1,0:T(8,128)(2,1)}, bf16[40,2048]{1,0:T(8,128)(2,1)}, bf16[4...) custom-call(s32[6]{0:T(128)S(1)} %stack.27.refs_0_, ...), custom_call_target="tpu_custom_call" | custom-call | flops 167772160 | bytes 1402880 | tf_op jit(solution)/shard_map/pallas_call | solution.py:220
  49.0 2.4 collective-permute-start.18
  54.8 3.0 %shard_map.286 = (bf16[32,2176]{1,0:T(8,128)(2,1)S(1)}, f32[32,2048]{1,0:T(8,128)}, f32[32,32]{1,0:T(8,128)}) custom-call(s32[6]{0:T(128)S(1)} %stack.27.refs_0_, bf16[128,2048]{1,0:T(8,128)(2,1)} %refs_1_.8, s32[8,32]{1,0:T(8,128)} %bitcast.51, f32[1,2048]{1,0:T(1,128)} %bitcast.46, bf16[32,2048]{1,0:T(8,128)(2,1)} %bitcast.44, ...), custom_call_target="tpu_custom_call" | custom-call | flops 4194304 | bytes 1070080 | tf_op jit(solution)/shard_map/pallas_call | solution.py:220
  61.0 2.8 %collective-permute-done.17.refs_7_.refs_12_ = bf16[40,2048]{1,0:T(8,128)(2,1)S(1)} collective-permute-done((bf16[40,2048]{1,0:T(8,128)(2,1)}, bf16[40,2048]{1,0:T(8,128)(2,1)S(1)}, u32[]{:S(2)}, u32[]{:S(2)}) %collective-permute-start.17) | collective-permute-done | bytes 163872 | tf_op jit(solution)/shard_map/ppermute | solution.py:56
  63.9 2.4 collective-permute-start.22
  66.3 7.0 %collective-permute-done.21.refs_6_ = bf16[32,2176]{1,0:T(8,128)(2,1)S(1)} collective-permute-done((bf16[32,2176]{1,0:T(8,128)(2,1)S(1)}, bf16[32,2176]{1,0:T(8,128)(2,1)S(1)}, u32[]{:S(2)}, u32[]{:S(2)}) %collective-permute-start.21) | collective-permute-done | bytes 139296 | tf_op jit(solution)/shard_map/ppermute | solution.py:56
  73.4 3.3 %shard_map.288 = (bf16[320,2176]{1,0:T(8,128)(2,1)}, bf16[192,1024]{1,0:T(8,128)(2,1)}) custom-call(s32[6]{0:T(128)S(1)} %stack.27.refs_0_, bf16[128,320]{1,0:T(8,128)(2,1)} %get-tuple-element.110.refs_9_.refs_1_, bf16[128,1024]{1,0:T(8,128)(2,1)} %get-tuple-element.122.refs_2_, bf16[128,2048]{1,0:T(8,128)(2,1)} %get-tuple-element.97.refs_0_.refs_3_, ...), custom_call_target="tpu_custom_call" | custom-call | flops 167772160 | bytes 2654208 | tf_op jit(solution)/shard_map/pallas_call | solution.py:220
  76.7 3.6 %all-to-all-start = ((bf16[8,40,2176]{2,1,0:T(8,128)(2,1)}), bf16[8,40,2176]{2,1,0:T(8,128)(2,1)S(1)}, u32[]{:S(2)}, u32[]{:S(2)}) async-start(bf16[8,40,2176]{2,1,0:T(8,128)(2,1)} %bitcast.42), calls=%async_computation | async-start | bytes 2785280 | tf_op jit(solution)/shard_map/all_to_all | solution.py:83
  81.0 5.2 %shard_map.287 = (bf16[320,2048]{1,0:T(8,128)(2,1)}, f32[320,768]{1,0:T(8,128)}) custom-call(s32[6]{0:T(128)S(1)} %stack.27.refs_0_, bf16[768,2048]{1,0:T(8,128)(2,1)} %bitcast.38, bf16[40,2048]{1,0:T(8,128)(2,1)} %get-tuple-element.113.refs_2_, bf16[40,2048]{1,0:T(8,128)(2,1)} %copy-done.11, bf16[40,2048]{1,0:T(8,128)(2,1)} %copy-done.12, ...), custom_call_target="tpu_custom_call" | custom-call | flops 1006632960 | bytes 6750208 | tf_op jit(solution)/shard_map/pallas_call | solution.py:220
  86.3 13.1 %all-to-all-done = bf16[8,40,2176]{2,1,0:T(8,128)(2,1)S(1)} async-done(((bf16[8,40,2176]{2,1,0:T(8,128)(2,1)}), bf16[8,40,2176]{2,1,0:T(8,128)(2,1)S(1)}, u32[]{:S(2)}, u32[]{:S(2)}) %all-to-all-start) | async-done | bytes 1392672 | tf_op jit(solution)/shard_map/all_to_all | solution.py:83
  99.3 10.4 %shard_map.289 = (bf16[320,768]{1,0:T(8,128)(2,1)}, bf16[320,768]{1,0:T(8,128)(2,1)}, bf16[320,768]{1,0:T(8,128)(2,1)}, f32[320,128]{1,0:T(8,128)}, bf16[320,2176]{1,0:T(8,128)(2,1)}) custom-call(s32[6]{0:T(128)S(1)} %stack.27.refs_0_, bf16[2048,768]{1,0:T(8,128)(2,1)} %bitcast.58, bf16[2048,768]{1,0:T(8,128)(2,1)} %bitcast.59, ...), custom_call_target="tpu_custom_call" | custom-call | flops 4026531840 | bytes 10305536 | tf_op jit(solution)/shard_map/pallas_call | solution.py:220
  109.7 3.8 %all-to-all-start.1 = ((bf16[8,40,2176]{2,1,0:T(8,128)(2,1)}), bf16[8,40,2176]{2,1,0:T(8,128)(2,1)S(1)}, u32[]{:S(2)}, u32[]{:S(2)}) async-start(bf16[8,40,2176]{2,1,0:T(8,128)(2,1)} %bitcast.43), calls=%async_computation.1 | async-start | bytes 2785280 | tf_op jit(solution)/shard_map/all_to_all | solution.py:83
  113.5 10.1 %shard_map.290 = (f32[2048,768]{1,0:T(8,128)}, f32[2048,768]{1,0:T(8,128)}, f32[768,2048]{1,0:T(8,128)}) custom-call(bf16[320,2176]{1,0:T(8,128)(2,1)} %bitcast.34, bf16[320,768]{1,0:T(8,128)(2,1)} %get-tuple-element.126.refs_1_, bf16[320,768]{1,0:T(8,128)(2,1)} %get-tuple-element.127.refs_2_, bf16[320,768]{1,0:T(8,128)(2,1)} %get-tuple-element.128.refs_3_.refs_0_, ...), custom_call_target="tpu_custom_call" | custom-call | flops 3019898880 | bytes 23216128 | tf_op jit(solution)/shard_map/pallas_call | solution.py:220
  123.6 8.7 %all-to-all-done.1 = bf16[8,40,2176]{2,1,0:T(8,128)(2,1)S(1)} async-done(((bf16[8,40,2176]{2,1,0:T(8,128)(2,1)}), bf16[8,40,2176]{2,1,0:T(8,128)(2,1)S(1)}, u32[]{:S(2)}, u32[]{:S(2)}) %all-to-all-start.1) | async-done | bytes 1392672 | tf_op jit(solution)/shard_map/all_to_all | solution.py:83
  134.3 3.6 %collective-permute-start.23 = (bf16[32,2176]{1,0:T(8,128)(2,1)S(1)}, bf16[32,2176]{1,0:T(8,128)(2,1)S(1)}, u32[]{:S(2)}, u32[]{:S(2)}) collective-permute-start(bf16[32,2176]{1,0:T(8,128)(2,1)S(1)} %get-tuple-element.134), channel_id=1, source_target_pairs={{0,8},{8,0},{16,24},{24,16},{1,9},{9,1},{17,25},{25,17},{2,10},{10... | collective-permute-start | bytes 417800 | tf_op jit(solution)/shard_map/ppermute | solution.py:56
  140.3 2.2 collective-permute-done.23.refs_7_.refs_3_
  142.6 5.8 %collective-permute-done.24.refs_8_.refs_4_ = bf16[32,2176]{1,0:T(8,128)(2,1)S(1)} collective-permute-done((bf16[32,2176]{1,0:T(8,128)(2,1)S(1)}, bf16[32,2176]{1,0:T(8,128)(2,1)S(1)}, u32[]{:S(2)}, u32[]{:S(2)}) %collective-permute-start.24) | collective-permute-done | bytes 139296 | tf_op jit(solution)/shard_map/ppermute | solution.py:56
  148.4 2.1 shard_map.292
  152.7 3.7 %collective-permute-start.27 = (bf16[32,2048]{1,0:T(8,128)(2,1)S(1)}, bf16[32,2048]{1,0:T(8,128)(2,1)S(1)}, u32[]{:S(2)}, u32[]{:S(2)}) collective-permute-start(bf16[32,2048]{1,0:T(8,128)(2,1)S(1)} %get-tuple-element.137.refs_10_), channel_id=1, source_target_pairs={{0,2},{1,3},{2,0},{3,1},{4,6},{5,7},{6,4},{7,5},{8,10},{9,11},{10,... | collective-permute-start | bytes 393224 | tf_op jit(solution)/shard_map/ppermute | solution.py:56
  159.0 4.7 %shard_map.293.refs_14_ = bf16[320,2048]{1,0:T(8,128)(2,1)} custom-call(bf16[320,768]{1,0:T(8,128)(2,1)} %get-tuple-element.128.refs_3_.refs_0_, bf16[768,2048]{1,0:T(8,128)(2,1)} %bitcast.39, f32[320,128]{1,0:T(8,128)} %get-tuple-element.130.refs_5_.refs_2_, bf16[32,2176]{1,0:T(8,128)(2,1)} %copy-done.3, bf16[32,2176]{1,0:T(8,128)(2,1)} %copy-done.4, ...), custom_call_target="tpu_custom_call" | custom-call | flops 1006632960 | bytes 5111808 | tf_op jit(solution)/shard_map/pallas_call | solution.py:220
  165.3 9.0 %shard_map.294 = (bf16[128,1024]{1,0:T(8,128)(2,1)}, f32[1,128]{1,0:T(1,128)}, bf16[8,128,256]{2,1,0:T(8,128)(2,1)}, bf16[128,2048]{1,0:T(8,128)(2,1)}) custom-call(s32[6]{0:T(128)S(1)} %stack.27.refs_0_, bf16[2,512,128]{2,1,0:T(8,128)(2,1)} %get-tuple-element.100.refs_1_.refs_2_, bf16[2,512,128]{2,1,0:T(8,128)(2,1)} %get-tuple-element.102.refs_2_, ...), custom_call_target="tpu_custom_call" | custom-call | flops 1073741824 | bytes 7996416 | tf_op jit(solution)/shard_map/pallas_call | solution.py:220
  174.3 4.3 %all-to-all-start.2 = ((bf16[8,128,256]{2,1,0:T(8,128)(2,1)}), bf16[8,128,256]{2,1,0:T(8,128)(2,1)S(1)}, u32[]{:S(2)}, u32[]{:S(2)}) async-start(bf16[8,128,256]{2,1,0:T(8,128)(2,1)} %get-tuple-element.144), calls=%async_computation.2 | async-start | bytes 1048576 | tf_op jit(solution)/shard_map/all_to_all | solution.py:83
  179.3 4.8 %shard_map.295.refs_1_.refs_6_ = f32[128,2048]{1,0:T(8,128)} custom-call(bf16[128,1024]{1,0:T(8,128)(2,1)} %get-tuple-element.142.refs_0_, bf16[2048,1024]{1,0:T(8,128)(2,1)} %refs_1_.7), custom_call_target="tpu_custom_call" | custom-call | flops 536870912 | bytes 5505024 | tf_op jit(solution)/shard_map/pallas_call | solution.py:220
  184.1 2.8 %shard_map.297.refs_2_.refs_5_ = bf16[160,1024]{1,0:T(8,128)(2,1)} custom-call(s32[6]{0:T(128)S(1)} %stack.27.refs_0_, bf16[4,192,1024]{2,1,0:T(8,128)(2,1)} %bitcast.36, bf16[80,512]{1,0:T(8,128)(2,1)S(1)} %get-tuple-element.147.refs_2_, bf16[80,512]{1,0:T(8,128)(2,1)S(1)} %collective-permute-done.29.refs_15_.refs_3_, ...), custom_call_target="tpu_custom_call" | custom-call | bytes 1900544 | tf_op jit(solution)/shard_map/pallas_call | solution.py:220
  188.8 4.4 %all-to-all-done.2.refs_8_ = bf16[8,128,256]{2,1,0:T(8,128)(2,1)S(1)} async-done(((bf16[8,128,256]{2,1,0:T(8,128)(2,1)}), bf16[8,128,256]{2,1,0:T(8,128)(2,1)S(1)}, u32[]{:S(2)}, u32[]{:S(2)}) %all-to-all-start.2) | async-done | bytes 524320 | tf_op jit(solution)/shard_map/all_to_all | solution.py:83
  193.2 4.2 %all-to-all-start.3 = ((bf16[8,40,2048]{2,1,0:T(8,128)(2,1)}), bf16[8,40,2048]{2,1,0:T(8,128)(2,1)S(1)}, u32[]{:S(2)}, u32[]{:S(2)}) async-start(bf16[8,40,2048]{2,1,0:T(8,128)(2,1)} %bitcast.40), calls=%async_computation.3 | async-start | bytes 2621440 | tf_op jit(solution)/shard_map/all_to_all | solution.py:83
  198.0 3.1 %shard_map.296 = (bf16[128,256]{1,0:T(8,128)(2,1)S(1)}, f32[1,128]{1,0:T(1,128)}, bf16[64,2048]{1,0:T(8,128)(2,1)S(1)}, bf16[64,2048]{1,0:T(8,128)(2,1)S(1)}) custom-call(s32[6]{0:T(128)S(1)} %stack.27.refs_0_, f32[128,2048]{1,0:T(8,128)} %shard_map.295.refs_1_.refs_6_, f32[128,128]{1,0:T(8,128)} %get-tuple-element.143.refs_2_, ...), custom_call_target="tpu_custom_call" | custom-call | flops 134217728 | bytes 2884608 | tf_op jit(solution)/shard_map/pallas_call | solution.py:220
  202.7 2.2 shard_map.298
  206.9 4.3 %shard_map.299 = (f32[1024,256]{1,0:T(8,128)}, bf16[1024,256]{1,0:T(8,128)(2,1)}) custom-call(s32[6]{0:T(128)S(1)} %stack.27.refs_0_, bf16[4,192,1024]{2,1,0:T(8,128)(2,1)} %bitcast.37, bf16[160,1024]{1,0:T(8,128)(2,1)} %shard_map.297.refs_2_.refs_5_, bf16[160,1024]{1,0:T(8,128)(2,1)} %copy-done.9, bf16[160,1024]{1,0:T(8,128)(2,1)} %copy-done.8, ...), custom_call_target="tpu_custom_call" | custom-call | flops 536870912 | bytes 4456448 | tf_op jit(solution)/shard_map/pallas_call | solution.py:220
  213.1 2.4 collective-permute-start.38
  217.2 4.1 %shard_map.300 = (f32[256,1024]{1,0:T(8,128)}, bf16[256,1024]{1,0:T(8,128)(2,1)}) custom-call(s32[6]{0:T(128)S(1)} %stack.27.refs_0_, bf16[512,1024]{1,0:T(8,128)(2,1)} %all-gather.5.cloned.1.call-done.refs_1_, bf16[160,1024]{1,0:T(8,128)(2,1)} %shard_map.297.refs_2_.refs_5_, bf16[160,1024]{1,0:T(8,128)(2,1)} %copy-done.9, bf16[160,1024]{1,0:T(8,128)(2,1)} %copy-done.8, ...), custom_call_target="tpu_custom_call" | custom-call | flops 536870912 | bytes 3932160 | tf_op jit(solution)/shard_map/pallas_call | solution.py:220
  222.6 2.7 %shard_map.301 = (bf16[64,2048]{1,0:T(8,128)(2,1)S(1)}, f32[1,2048]{1,0:T(1,128)}) custom-call(s32[6]{0:T(128)S(1)} %stack.27.refs_0_, bf16[128,2048]{1,0:T(8,128)(2,1)} %refs_1_.8, f32[1,2048]{1,0:T(1,128)} %bitcast.49, bf16[128,2048]{1,0:T(8,128)(2,1)} %get-tuple-element.141.refs_3_, bf16[64,2048]{1,0:T(8,128)(2,1)S(1)} %copy-done.1, ...), custom_call_target="tpu_custom_call" | custom-call | bytes 1327104 | tf_op jit(solution)/shard_map/pallas_call | solution.py:220
  227.5 2.6 shard_map.302
  230.2 2.8 %shard_map.303 = (bf16[128,2048]{1,0:T(8,128)(2,1)}, bf16[32,32,128]{2,1,0:T(8,128)(2,1)}) custom-call(s32[6]{0:T(128)S(1)} %stack.27.refs_0_, bf16[64,2048]{1,0:T(8,128)(2,1)S(1)} %get-tuple-element.152.refs_1_, bf16[64,2048]{1,0:T(8,128)(2,1)S(1)} %collective-permute-done.40.refs_2_, f32[1,2048]{1,0:T(1,128)} %get-tuple-element.153.refs_3_, ...), custom_call_target="tpu_custom_call" | custom-call | bytes 893952 | tf_op jit(solution)/shard_map/pallas_call | solution.py:220
  233.0 2.8 %all-to-all-start.4 = ((bf16[32,32,128]{2,1,0:T(8,128)(2,1)}), bf16[32,32,128]{2,1,0:T(8,128)(2,1)S(1)}, u32[]{:S(2)}, u32[]{:S(2)}) async-start(bf16[32,32,128]{2,1,0:T(8,128)(2,1)} %get-tuple-element.160.refs_9_), calls=%async_computation.4 | async-start | bytes 524288 | tf_op jit(solution)/shard_map/all_to_all | solution.py:83
  237.7 2.4 collective-permute-start.44
  240.3 3.0 %shard_map.304 = (f32[256,256]{1,0:T(8,128)}, bf16[256,256]{1,0:T(8,128)(2,1)}) custom-call(s32[6]{0:T(128)S(1)} %stack.27.refs_0_, bf16[128,256]{1,0:T(8,128)(2,1)S(1)} %get-tuple-element.151.refs_1_, bf16[128,256]{1,0:T(8,128)(2,1)S(1)} %collective-permute-done.37.refs_8_.refs_2_, bf16[128,256]{1,0:T(8,128)(2,1)S(1)} %collective-permute-done.38.refs_9_.refs_3_, ...), custom_call_target="tpu_custom_call" | custom-call | flops 134217728 | bytes 1703936 | tf_op jit(solution)/shard_map/pallas_call | solution.py:220
  245.1 3.0 %collective-permute-done.43.refs_6_ = bf16[32,2048]{1,0:T(8,128)(2,1)S(1)} collective-permute-done((bf16[32,2048]{1,0:T(8,128)(2,1)S(1)}, bf16[32,2048]{1,0:T(8,128)(2,1)S(1)}, u32[]{:S(2)}, u32[]{:S(2)}) %collective-permute-start.43) | collective-permute-done | bytes 131104 | tf_op jit(solution)/shard_map/ppermute | solution.py:56
  248.1 6.0 %collective-permute-done.44.refs_7_ = bf16[32,2048]{1,0:T(8,128)(2,1)S(1)} collective-permute-done((bf16[32,2048]{1,0:T(8,128)(2,1)S(1)}, bf16[32,2048]{1,0:T(8,128)(2,1)S(1)}, u32[]{:S(2)}, u32[]{:S(2)}) %collective-permute-start.44) | collective-permute-done | bytes 131104 | tf_op jit(solution)/shard_map/ppermute | solution.py:56
  254.8 3.5 %shard_map.305 = (bf16[32,2048]{1,0:T(8,128)(2,1)}, f32[1024,256]{1,0:T(8,128)}, f32[256,1024]{1,0:T(8,128)}, f32[256,128]{1,0:T(8,128)}, f32[256,128]{1,0:T(8,1...) custom-call(bf16[32,32,128]{2,1,0:T(8,128)(2,1)S(1)} %all-to-all-don, ...), custom_call_target="tpu_custom_call" | custom-call | bytes 6039552 | tf_op jit(solution)/shard_map/pallas_call | solution.py:220
  (132 shorter events, 46.9 us)
Async XLA Ops:
  10.3 8.9 %collective-permute-start = (bf16[128,256]{1,0:T(8,128)(2,1)S(1)}, bf16[128,256]{1,0:T(8,128)(2,1)S(1)}, u32[]{:S(2)}, u32[]{:S(2)}) collective-permute-start(bf16[128,256]{1,0:T(8,128)(2,1)S(1)} %get-tuple-element.101.refs_4_), channel_id=1, source_target_pairs={{0,4},{4,0},{8,12},{12,8},{16,20},{20,16},{24,28},{28,24},{1,5},{5... | collective-permute-start | bytes 196616 | tf_op jit(solution)/shard_map/ppermute | solution.py:56
  13.4 9.5 %collective-permute-start.1 = (bf16[128,256]{1,0:T(8,128)(2,1)S(1)}, bf16[128,256]{1,0:T(8,128)(2,1)S(1)}, u32[]{:S(2)}, u32[]{:S(2)}) collective-permute-start(bf16[128,256]{1,0:T(8,128)(2,1)S(1)} %get-tuple-element.101.refs_4_), channel_id=1, source_target_pairs={{0,8},{4,12},{8,0},{12,4},{16,24},{20,28},{24,16},{28,20},{1,9},{5... | collective-permute-start | bytes 196616 | tf_op jit(solution)/shard_map/ppermute | solution.py:56
  14.9 13.8 %collective-permute-start.2 = (bf16[128,256]{1,0:T(8,128)(2,1)S(1)}, bf16[128,256]{1,0:T(8,128)(2,1)S(1)}, u32[]{:S(2)}, u32[]{:S(2)}) collective-permute-start(bf16[128,256]{1,0:T(8,128)(2,1)S(1)} %get-tuple-element.101.refs_4_), channel_id=1, source_target_pairs={{0,12},{4,8},{8,4},{12,0},{16,28},{20,24},{24,20},{28,16},{1,13},{... | collective-permute-start | bytes 196616 | tf_op jit(solution)/shard_map/ppermute | solution.py:56
  14.9 14.0 %collective-permute-start.3 = (bf16[128,256]{1,0:T(8,128)(2,1)S(1)}, bf16[128,256]{1,0:T(8,128)(2,1)S(1)}, u32[]{:S(2)}, u32[]{:S(2)}) collective-permute-start(bf16[128,256]{1,0:T(8,128)(2,1)S(1)} %get-tuple-element.101.refs_4_), channel_id=1, source_target_pairs={{0,16},{4,20},{8,24},{12,28},{16,0},{20,4},{24,8},{28,12},{1,17},{... | collective-permute-start | bytes 196616 | tf_op jit(solution)/shard_map/ppermute | solution.py:56
  17.9 15.3 %collective-permute-start.4 = (bf16[128,256]{1,0:T(8,128)(2,1)S(1)}, bf16[128,256]{1,0:T(8,128)(2,1)S(1)}, u32[]{:S(2)}, u32[]{:S(2)}) collective-permute-start(bf16[128,256]{1,0:T(8,128)(2,1)S(1)} %get-tuple-element.101.refs_4_), channel_id=1, source_target_pairs={{0,20},{4,16},{8,28},{12,24},{16,4},{20,0},{24,12},{28,8},{1,21},{... | collective-permute-start | bytes 196616 | tf_op jit(solution)/shard_map/ppermute | solution.py:56
  19.2 14.1 %collective-permute-start.5 = (bf16[128,256]{1,0:T(8,128)(2,1)S(1)}, bf16[128,256]{1,0:T(8,128)(2,1)S(1)}, u32[]{:S(2)}, u32[]{:S(2)}) collective-permute-start(bf16[128,256]{1,0:T(8,128)(2,1)S(1)} %get-tuple-element.101.refs_4_), channel_id=1, source_target_pairs={{0,24},{4,28},{8,16},{12,20},{16,8},{20,12},{24,0},{28,4},{1,25},{... | collective-permute-start | bytes 196616 | tf_op jit(solution)/shard_map/ppermute | solution.py:56
  22.8 10.5 %collective-permute-start.6 = (bf16[128,256]{1,0:T(8,128)(2,1)S(1)}, bf16[128,256]{1,0:T(8,128)(2,1)S(1)}, u32[]{:S(2)}, u32[]{:S(2)}) collective-permute-start(bf16[128,256]{1,0:T(8,128)(2,1)S(1)} %get-tuple-element.101.refs_4_), channel_id=1, source_target_pairs={{0,28},{4,24},{8,20},{12,16},{16,12},{20,8},{24,4},{28,0},{1,29},{... | collective-permute-start | bytes 196616 | tf_op jit(solution)/shard_map/ppermute | solution.py:56
  28.8 10.9 %collective-permute-start.10 = (bf16[32,2176]{1,0:T(8,128)(2,1)S(1)}, bf16[32,2176]{1,0:T(8,128)(2,1)S(1)}, u32[]{:S(2)}, u32[]{:S(2)}) collective-permute-start(bf16[32,2176]{1,0:T(8,128)(2,1)S(1)} %shard_map.284.refs_2_), channel_id=1, source_target_pairs={{0,8},{8,0},{16,24},{24,16},{1,9},{9,1},{17,25},{25,17},{2,10},{10... | collective-permute-start | bytes 417800 | tf_op jit(solution)/shard_map/ppermute | solution.py:56
  28.9 13.2 %collective-permute-start.11 = (bf16[32,2176]{1,0:T(8,128)(2,1)S(1)}, bf16[32,2176]{1,0:T(8,128)(2,1)S(1)}, u32[]{:S(2)}, u32[]{:S(2)}) collective-permute-start(bf16[32,2176]{1,0:T(8,128)(2,1)S(1)} %shard_map.284.refs_2_), channel_id=1, source_target_pairs={{0,16},{8,24},{16,0},{24,8},{1,17},{9,25},{17,1},{25,9},{2,18},{10... | collective-permute-start | bytes 417800 | tf_op jit(solution)/shard_map/ppermute | solution.py:56
  33.3 8.9 %collective-permute-start.12 = (bf16[32,2176]{1,0:T(8,128)(2,1)S(1)}, bf16[32,2176]{1,0:T(8,128)(2,1)S(1)}, u32[]{:S(2)}, u32[]{:S(2)}) collective-permute-start(bf16[32,2176]{1,0:T(8,128)(2,1)S(1)} %shard_map.284.refs_2_), channel_id=1, source_target_pairs={{0,24},{8,16},{16,8},{24,0},{1,25},{9,17},{17,9},{25,1},{2,26},{10... | collective-permute-start | bytes 417800 | tf_op jit(solution)/shard_map/ppermute | solution.py:56
  38.0 9.0 %collective-permute-start.7 = (bf16[32,2048]{1,0:T(8,128)(2,1)S(1)}, bf16[32,2048]{1,0:T(8,128)(2,1)S(1)}, u32[]{:S(2)}, u32[]{:S(2)}) collective-permute-start(bf16[32,2048]{1,0:T(8,128)(2,1)S(1)} %get-tuple-element.107), channel_id=1, source_target_pairs={{0,1},{1,0},{2,3},{3,2},{4,5},{5,4},{6,7},{7,6},{8,9},{9,8},{10,11... | collective-permute-start | bytes 393224 | tf_op jit(solution)/shard_map/ppermute | solution.py:56
  38.0 9.3 %collective-permute-start.8 = (bf16[32,2048]{1,0:T(8,128)(2,1)S(1)}, bf16[32,2048]{1,0:T(8,128)(2,1)S(1)}, u32[]{:S(2)}, u32[]{:S(2)}) collective-permute-start(bf16[32,2048]{1,0:T(8,128)(2,1)S(1)} %get-tuple-element.108), channel_id=1, source_target_pairs={{0,2},{1,3},{2,0},{3,1},{4,6},{5,7},{6,4},{7,5},{8,10},{9,11},{10,... | collective-permute-start | bytes 393224 | tf_op jit(solution)/shard_map/ppermute | solution.py:56
  39.6 9.1 %collective-permute-start.9 = (bf16[32,2048]{1,0:T(8,128)(2,1)S(1)}, bf16[32,2048]{1,0:T(8,128)(2,1)S(1)}, u32[]{:S(2)}, u32[]{:S(2)}) collective-permute-start(bf16[32,2048]{1,0:T(8,128)(2,1)S(1)} %get-tuple-element.109), channel_id=1, source_target_pairs={{0,3},{1,2},{2,1},{3,0},{4,7},{5,6},{6,5},{7,4},{8,11},{9,10},{10,... | collective-permute-start | bytes 393224 | tf_op jit(solution)/shard_map/ppermute | solution.py:56
  45.4 7.3 %collective-permute-start.14 = (bf16[40,2048]{1,0:T(8,128)(2,1)}, bf16[40,2048]{1,0:T(8,128)(2,1)S(1)}, u32[]{:S(2)}, u32[]{:S(2)}) collective-permute-start(bf16[40,2048]{1,0:T(8,128)(2,1)} %get-tuple-element.115), channel_id=1, source_target_pairs={{0,2},{1,3},{2,0},{3,1},{4,6},{5,7},{6,4},{7,5},{8,10},{9,11},{10,... | collective-permute-start | bytes 491528 | tf_op jit(solution)/shard_map/ppermute | solution.py:56
  46.9 10.9 %collective-permute-start.15 = (bf16[40,2048]{1,0:T(8,128)(2,1)}, bf16[40,2048]{1,0:T(8,128)(2,1)S(1)}, u32[]{:S(2)}, u32[]{:S(2)}) collective-permute-start(bf16[40,2048]{1,0:T(8,128)(2,1)} %get-tuple-element.116), channel_id=1, source_target_pairs={{0,3},{1,2},{2,1},{3,0},{4,7},{5,6},{6,5},{7,4},{8,11},{9,10},{10,... | collective-permute-start | bytes 491528 | tf_op jit(solution)/shard_map/ppermute | solution.py:56
  47.2 12.7 %collective-permute-start.16 = (bf16[40,2048]{1,0:T(8,128)(2,1)}, bf16[40,2048]{1,0:T(8,128)(2,1)S(1)}, u32[]{:S(2)}, u32[]{:S(2)}) collective-permute-start(bf16[40,2048]{1,0:T(8,128)(2,1)} %get-tuple-element.117), channel_id=1, source_target_pairs={{0,4},{1,5},{2,6},{3,7},{4,0},{5,1},{6,2},{7,3},{8,12},{9,13},{10,... | collective-permute-start | bytes 491528 | tf_op jit(solution)/shard_map/ppermute | solution.py:56
  48.8 15.1 %collective-permute-start.17 = (bf16[40,2048]{1,0:T(8,128)(2,1)}, bf16[40,2048]{1,0:T(8,128)(2,1)S(1)}, u32[]{:S(2)}, u32[]{:S(2)}) collective-permute-start(bf16[40,2048]{1,0:T(8,128)(2,1)} %get-tuple-element.118), channel_id=1, source_target_pairs={{0,5},{1,4},{2,7},{3,6},{4,1},{5,0},{6,3},{7,2},{8,13},{9,12},{10,... | collective-permute-start | bytes 491528 | tf_op jit(solution)/shard_map/ppermute | solution.py:56
  49.0 17.3 %collective-permute-start.18 = (bf16[40,2048]{1,0:T(8,128)(2,1)}, bf16[40,2048]{1,0:T(8,128)(2,1)S(1)}, u32[]{:S(2)}, u32[]{:S(2)}) collective-permute-start(bf16[40,2048]{1,0:T(8,128)(2,1)} %get-tuple-element.119), channel_id=1, source_target_pairs={{0,6},{1,7},{2,4},{3,5},{4,2},{5,3},{6,0},{7,1},{8,14},{9,15},{10,... | collective-permute-start | bytes 491528 | tf_op jit(solution)/shard_map/ppermute | solution.py:56
  52.7 13.6 %collective-permute-start.19 = (bf16[40,2048]{1,0:T(8,128)(2,1)}, bf16[40,2048]{1,0:T(8,128)(2,1)S(1)}, u32[]{:S(2)}, u32[]{:S(2)}) collective-permute-start(bf16[40,2048]{1,0:T(8,128)(2,1)} %get-tuple-element.120), channel_id=1, source_target_pairs={{0,7},{1,6},{2,5},{3,4},{4,3},{5,2},{6,1},{7,0},{8,15},{9,14},{10,... | collective-permute-start | bytes 491528 | tf_op jit(solution)/shard_map/ppermute | solution.py:56
  57.9 8.5 %collective-permute-start.20 = (bf16[32,2176]{1,0:T(8,128)(2,1)S(1)}, bf16[32,2176]{1,0:T(8,128)(2,1)S(1)}, u32[]{:S(2)}, u32[]{:S(2)}) collective-permute-start(bf16[32,2176]{1,0:T(8,128)(2,1)S(1)} %get-tuple-element.123.refs_4_), channel_id=1, source_target_pairs={{0,8},{8,0},{16,24},{24,16},{1,9},{9,1},{17,25},{25,17},{2,10},{10... | collective-permute-start | bytes 417800 | tf_op jit(solution)/shard_map/ppermute | solution.py:56
  60.0 13.4 %collective-permute-start.21 = (bf16[32,2176]{1,0:T(8,128)(2,1)S(1)}, bf16[32,2176]{1,0:T(8,128)(2,1)S(1)}, u32[]{:S(2)}, u32[]{:S(2)}) collective-permute-start(bf16[32,2176]{1,0:T(8,128)(2,1)S(1)} %get-tuple-element.123.refs_4_), channel_id=1, source_target_pairs={{0,16},{8,24},{16,0},{24,8},{1,17},{9,25},{17,1},{25,9},{2,18},{10... | collective-permute-start | bytes 417800 | tf_op jit(solution)/shard_map/ppermute | solution.py:56
  63.9 9.5 %collective-permute-start.22 = (bf16[32,2176]{1,0:T(8,128)(2,1)S(1)}, bf16[32,2176]{1,0:T(8,128)(2,1)S(1)}, u32[]{:S(2)}, u32[]{:S(2)}) collective-permute-start(bf16[32,2176]{1,0:T(8,128)(2,1)S(1)} %get-tuple-element.123.refs_4_), channel_id=1, source_target_pairs={{0,24},{8,16},{16,8},{24,0},{1,25},{9,17},{17,9},{25,1},{2,26},{10... | collective-permute-start | bytes 417800 | tf_op jit(solution)/shard_map/ppermute | solution.py:56
  76.7 22.6 %all-to-all-start = ((bf16[8,40,2176]{2,1,0:T(8,128)(2,1)}), bf16[8,40,2176]{2,1,0:T(8,128)(2,1)S(1)}, u32[]{:S(2)}, u32[]{:S(2)}) async-start(bf16[8,40,2176]{2,1,0:T(8,128)(2,1)} %bitcast.42), calls=%async_computation | async-start | bytes 2785280 | tf_op jit(solution)/shard_map/all_to_all | solution.py:83
  80.3 43.3 %all-gather.3.cloned.1.call-start = ((), (), s32[]{:S(2)}) async-start(), calls=%async_computation.5 | async-start | bytes 1966080 | tf_op jit(solution)/shard_map/all_gather | solution.py:79
  109.7 22.6 %all-to-all-start.1 = ((bf16[8,40,2176]{2,1,0:T(8,128)(2,1)}), bf16[8,40,2176]{2,1,0:T(8,128)(2,1)S(1)}, u32[]{:S(2)}, u32[]{:S(2)}) async-start(bf16[8,40,2176]{2,1,0:T(8,128)(2,1)} %bitcast.43), calls=%async_computation.1 | async-start | bytes 2785280 | tf_op jit(solution)/shard_map/all_to_all | solution.py:83
  134.3 8.3 %collective-permute-start.23 = (bf16[32,2176]{1,0:T(8,128)(2,1)S(1)}, bf16[32,2176]{1,0:T(8,128)(2,1)S(1)}, u32[]{:S(2)}, u32[]{:S(2)}) collective-permute-start(bf16[32,2176]{1,0:T(8,128)(2,1)S(1)} %get-tuple-element.134), channel_id=1, source_target_pairs={{0,8},{8,0},{16,24},{24,16},{1,9},{9,1},{17,25},{25,17},{2,10},{10... | collective-permute-start | bytes 417800 | tf_op jit(solution)/shard_map/ppermute | solution.py:56
  137.9 10.5 %collective-permute-start.24 = (bf16[32,2176]{1,0:T(8,128)(2,1)S(1)}, bf16[32,2176]{1,0:T(8,128)(2,1)S(1)}, u32[]{:S(2)}, u32[]{:S(2)}) collective-permute-start(bf16[32,2176]{1,0:T(8,128)(2,1)S(1)} %get-tuple-element.135), channel_id=1, source_target_pairs={{0,16},{8,24},{16,0},{24,8},{1,17},{9,25},{17,1},{25,9},{2,18},{10... | collective-permute-start | bytes 417800 | tf_op jit(solution)/shard_map/ppermute | solution.py:56
  138.9 9.5 %collective-permute-start.25 = (bf16[32,2176]{1,0:T(8,128)(2,1)S(1)}, bf16[32,2176]{1,0:T(8,128)(2,1)S(1)}, u32[]{:S(2)}, u32[]{:S(2)}) collective-permute-start(bf16[32,2176]{1,0:T(8,128)(2,1)S(1)} %get-tuple-element.136), channel_id=1, source_target_pairs={{0,24},{8,16},{16,8},{24,0},{1,25},{9,17},{17,9},{25,1},{2,26},{10... | collective-permute-start | bytes 417800 | tf_op jit(solution)/shard_map/ppermute | solution.py:56
  150.6 7.0 %collective-permute-start.29 = (bf16[80,512]{1,0:T(8,128)(2,1)S(1)}, bf16[80,512]{1,0:T(8,128)(2,1)S(1)}, u32[]{:S(2)}, u32[]{:S(2)}) collective-permute-start(bf16[80,512]{1,0:T(8,128)(2,1)S(1)} %get-tuple-element.138), channel_id=1, source_target_pairs={{0,8},{8,0},{16,24},{24,16},{1,9},{9,1},{17,25},{25,17},{2,10},{10... | collective-permute-start | bytes 245768 | tf_op jit(solution)/shard_map/ppermute | solution.py:56
  152.7 12.6 %collective-permute-start.26 = (bf16[32,2048]{1,0:T(8,128)(2,1)S(1)}, bf16[32,2048]{1,0:T(8,128)(2,1)S(1)}, u32[]{:S(2)}, u32[]{:S(2)}) collective-permute-start(bf16[32,2048]{1,0:T(8,128)(2,1)S(1)} %get-tuple-element.137.refs_10_), channel_id=1, source_target_pairs={{0,1},{1,0},{2,3},{3,2},{4,5},{5,4},{6,7},{7,6},{8,9},{9,8},{10,11... | collective-permute-start | bytes 393224 | tf_op jit(solution)/shard_map/ppermute | solution.py:56
  152.7 12.6 %collective-permute-start.27 = (bf16[32,2048]{1,0:T(8,128)(2,1)S(1)}, bf16[32,2048]{1,0:T(8,128)(2,1)S(1)}, u32[]{:S(2)}, u32[]{:S(2)}) collective-permute-start(bf16[32,2048]{1,0:T(8,128)(2,1)S(1)} %get-tuple-element.137.refs_10_), channel_id=1, source_target_pairs={{0,2},{1,3},{2,0},{3,1},{4,6},{5,7},{6,4},{7,5},{8,10},{9,11},{10,... | collective-permute-start | bytes 393224 | tf_op jit(solution)/shard_map/ppermute | solution.py:56
  156.4 8.8 %collective-permute-start.28 = (bf16[32,2048]{1,0:T(8,128)(2,1)S(1)}, bf16[32,2048]{1,0:T(8,128)(2,1)S(1)}, u32[]{:S(2)}, u32[]{:S(2)}) collective-permute-start(bf16[32,2048]{1,0:T(8,128)(2,1)S(1)} %get-tuple-element.137.refs_10_), channel_id=1, source_target_pairs={{0,3},{1,2},{2,1},{3,0},{4,7},{5,6},{6,5},{7,4},{8,11},{9,10},{10,... | collective-permute-start | bytes 393224 | tf_op jit(solution)/shard_map/ppermute | solution.py:56
  156.6 8.7 %collective-permute-start.30 = (bf16[80,512]{1,0:T(8,128)(2,1)S(1)}, bf16[80,512]{1,0:T(8,128)(2,1)S(1)}, u32[]{:S(2)}, u32[]{:S(2)}) collective-permute-start(bf16[80,512]{1,0:T(8,128)(2,1)S(1)} %get-tuple-element.139), channel_id=1, source_target_pairs={{0,16},{8,24},{16,0},{24,8},{1,17},{9,25},{17,1},{25,9},{2,18},{10... | collective-permute-start | bytes 245768 | tf_op jit(solution)/shard_map/ppermute | solution.py:56
  157.6 7.7 %collective-permute-start.31 = (bf16[80,512]{1,0:T(8,128)(2,1)S(1)}, bf16[80,512]{1,0:T(8,128)(2,1)S(1)}, u32[]{:S(2)}, u32[]{:S(2)}) collective-permute-start(bf16[80,512]{1,0:T(8,128)(2,1)S(1)} %get-tuple-element.140), channel_id=1, source_target_pairs={{0,24},{8,16},{16,8},{24,0},{1,25},{9,17},{17,9},{25,1},{2,26},{10... | collective-permute-start | bytes 245768 | tf_op jit(solution)/shard_map/ppermute | solution.py:56
  174.3 19.0 %all-to-all-start.2 = ((bf16[8,128,256]{2,1,0:T(8,128)(2,1)}), bf16[8,128,256]{2,1,0:T(8,128)(2,1)S(1)}, u32[]{:S(2)}, u32[]{:S(2)}) async-start(bf16[8,128,256]{2,1,0:T(8,128)(2,1)} %get-tuple-element.144), calls=%async_computation.2 | async-start | bytes 1048576 | tf_op jit(solution)/shard_map/all_to_all | solution.py:83
  178.5 38.6 %all-gather.5.cloned.1.call-start = ((), (), s32[]{:S(2)}) async-start(), calls=%async_computation.6 | async-start | bytes 1310720 | tf_op jit(solution)/shard_map/all_gather | solution.py:79
  186.8 11.1 %collective-permute-start.34 = (bf16[160,1024]{1,0:T(8,128)(2,1)}, bf16[160,1024]{1,0:T(8,128)(2,1)S(1)}, u32[]{:S(2)}, u32[]{:S(2)}) collective-permute-start(bf16[160,1024]{1,0:T(8,128)(2,1)} %shard_map.297.refs_2_.refs_5_), channel_id=1, source_target_pairs={{0,2},{1,3},{2,0},{3,1},{4,6},{5,7},{6,4},{7,5},{8,10},{9,11},{10,... | collective-permute-start | bytes 983048 | tf_op jit(solution)/shard_map/ppermute | solution.py:56
  193.2 34.3 %all-to-all-start.3 = ((bf16[8,40,2048]{2,1,0:T(8,128)(2,1)}), bf16[8,40,2048]{2,1,0:T(8,128)(2,1)S(1)}, u32[]{:S(2)}, u32[]{:S(2)}) async-start(bf16[8,40,2048]{2,1,0:T(8,128)(2,1)} %bitcast.40), calls=%async_computation.3 | async-start | bytes 2621440 | tf_op jit(solution)/shard_map/all_to_all | solution.py:83
  205.0 16.7 %collective-permute-start.36 = (bf16[64,2048]{1,0:T(8,128)(2,1)S(1)}, bf16[64,2048]{1,0:T(8,128)(2,1)S(1)}, u32[]{:S(2)}, u32[]{:S(2)}) collective-permute-start(bf16[64,2048]{1,0:T(8,128)(2,1)S(1)} %get-tuple-element.148.refs_6_.refs_4_.refs_3_), channel_id=1, source_target_pairs={{0,2},{1,3},{2,0},{3,1},{4,6},{5,7},{6,4},{7,5},{8,10},{9,11},{10,... | collective-permute-start | bytes 786440 | tf_op jit(solution)/shard_map/ppermute | solution.py:56
  211.2 18.9 %collective-permute-start.42 = (bf16[1024,256]{1,0:T(8,128)(2,1)}, bf16[1024,256]{1,0:T(8,128)(2,1)S(1)}, u32[]{:S(2)}, u32[]{:S(2)}) collective-permute-start(bf16[1024,256]{1,0:T(8,128)(2,1)} %get-tuple-element.159), channel_id=1, source_target_pairs={{0,4},{4,0},{1,5},{5,1},{2,6},{6,2},{3,7},{7,3},{8,12},{12,8},{9,1... | collective-permute-start | bytes 1572872 | tf_op jit(solution)/shard_map/ppermute | solution.py:56
  212.8 8.5 %collective-permute-start.37 = (bf16[128,256]{1,0:T(8,128)(2,1)S(1)}, bf16[128,256]{1,0:T(8,128)(2,1)S(1)}, u32[]{:S(2)}, u32[]{:S(2)}) collective-permute-start(bf16[128,256]{1,0:T(8,128)(2,1)S(1)} %get-tuple-element.151.refs_1_), channel_id=1, source_target_pairs={{0,8},{8,0},{16,24},{24,16},{1,9},{9,1},{17,25},{25,17},{2,10},{10... | collective-permute-start | bytes 196616 | tf_op jit(solution)/shard_map/ppermute | solution.py:56
  213.1 8.2 %collective-permute-start.38 = (bf16[128,256]{1,0:T(8,128)(2,1)S(1)}, bf16[128,256]{1,0:T(8,128)(2,1)S(1)}, u32[]{:S(2)}, u32[]{:S(2)}) collective-permute-start(bf16[128,256]{1,0:T(8,128)(2,1)S(1)} %get-tuple-element.151.refs_1_), channel_id=1, source_target_pairs={{0,16},{8,24},{16,0},{24,8},{1,17},{9,25},{17,1},{25,9},{2,18},{10... | collective-permute-start | bytes 196616 | tf_op jit(solution)/shard_map/ppermute | solution.py:56
  226.1 28.1 %collective-permute-start.46 = (bf16[256,1024]{1,0:T(8,128)(2,1)}, bf16[256,1024]{1,0:T(8,128)(2,1)S(1)}, u32[]{:S(2)}, u32[]{:S(2)}) collective-permute-start(bf16[256,1024]{1,0:T(8,128)(2,1)} %get-tuple-element.165), channel_id=1, source_target_pairs={{0,4},{4,0},{1,5},{5,1},{2,6},{6,2},{3,7},{7,3},{8,12},{12,8},{9,1... | collective-permute-start | bytes 1572872 | tf_op jit(solution)/shard_map/ppermute | solution.py:56
  233.0 21.1 %all-to-all-start.4 = ((bf16[32,32,128]{2,1,0:T(8,128)(2,1)}), bf16[32,32,128]{2,1,0:T(8,128)(2,1)S(1)}, u32[]{:S(2)}, u32[]{:S(2)}) async-start(bf16[32,32,128]{2,1,0:T(8,128)(2,1)} %get-tuple-element.160.refs_9_), calls=%async_computation.4 | async-start | bytes 524288 | tf_op jit(solution)/shard_map/all_to_all | solution.py:83
  235.8 12.2 %collective-permute-start.43 = (bf16[32,2048]{1,0:T(8,128)(2,1)S(1)}, bf16[32,2048]{1,0:T(8,128)(2,1)S(1)}, u32[]{:S(2)}, u32[]{:S(2)}) collective-permute-start(bf16[32,2048]{1,0:T(8,128)(2,1)S(1)} %get-tuple-element.162), channel_id=1, source_target_pairs={{0,8},{8,0},{16,24},{24,16},{1,9},{9,1},{17,25},{25,17},{2,10},{10... | collective-permute-start | bytes 393224 | tf_op jit(solution)/shard_map/ppermute | solution.py:56
  237.7 16.4 %collective-permute-start.44 = (bf16[32,2048]{1,0:T(8,128)(2,1)S(1)}, bf16[32,2048]{1,0:T(8,128)(2,1)S(1)}, u32[]{:S(2)}, u32[]{:S(2)}) collective-permute-start(bf16[32,2048]{1,0:T(8,128)(2,1)S(1)} %get-tuple-element.163), channel_id=1, source_target_pairs={{0,16},{8,24},{16,0},{24,8},{1,17},{9,25},{17,1},{25,9},{2,18},{10... | collective-permute-start | bytes 393224 | tf_op jit(solution)/shard_map/ppermute | solution.py:56
  240.1 14.0 %collective-permute-start.45 = (bf16[32,2048]{1,0:T(8,128)(2,1)S(1)}, bf16[32,2048]{1,0:T(8,128)(2,1)S(1)}, u32[]{:S(2)}, u32[]{:S(2)}) collective-permute-start(bf16[32,2048]{1,0:T(8,128)(2,1)S(1)} %get-tuple-element.164), channel_id=1, source_target_pairs={{0,24},{8,16},{16,8},{24,0},{1,25},{9,17},{17,9},{25,1},{2,26},{10... | collective-permute-start | bytes 393224 | tf_op jit(solution)/shard_map/ppermute | solution.py:56
  243.2 10.9 %collective-permute-start.47 = (bf16[256,256]{1,0:T(8,128)(2,1)}, bf16[256,256]{1,0:T(8,128)(2,1)S(1)}, u32[]{:S(2)}, u32[]{:S(2)}) collective-permute-start(bf16[256,256]{1,0:T(8,128)(2,1)} %get-tuple-element.166), channel_id=1, source_target_pairs={{0,4},{4,0},{1,5},{5,1},{2,6},{6,2},{3,7},{7,3},{8,12},{12,8},{9,1... | collective-permute-start | bytes 393224 | tf_op jit(solution)/shard_map/ppermute | solution.py:56
  (28 other events, 193.8 us)
Sparse Core Ops, SparseCore 0:
  82.7 39.6 all-gather.2
  180.9 29.7 all-gather.4

commit v2 on v1

--- a/solution.py
+++ b/solution.py
@@ -921,7 +921,7 @@
         bind(route_kernel, experts, top, planes),
         [((row_count, slot_rows), BF16)] + [((group, width), BF16)] * planes,
         ids, jnp.asarray(columns), *near(cot_pieces),
-        after=[branch[0]],
+        loose=[branch[0]],
         scratch=[
             pltpu.VMEM((4 * quarter, width + 128), BF16),
             pltpu.VMEM((slot_rows, width), F32),
@@ -956,7 +956,7 @@
             ((row_count + width // local_width * quarter, local_width), BF16),
         ],
         ids, chosen, attended_low, attention_input, *near(exchange([send] * 4, "lead")),
-        after=cot_groups[1:],
+        loose=cot_groups[1:],
         scratch=[pltpu.VMEM((row_count, width + extra), BF16)],
         flops=2 * slot_rows * row_count * width,
     )
@@ -990,13 +990,14 @@
         megabytes=40,
     )
 
-    def to_tokens(rows, after, place):
+    def to_tokens(rows, after, place, loose=()):
         return vcall(
             combine_kernel,
             [((quarter, rows.shape[1]), F32, *place)]
             + [((quarter, rows.shape[1]), BF16, "near")] * 3,
             ids, chosen, Near(rows),
             after=after,
+            loose=loose,
             scratch=[pltpu.VMEM((row_count, rows.shape[1]), F32)],
             flops=2 * slot_rows * row_count * width,
         )
@@ -1077,7 +1078,7 @@
         Near(grad_in_own), Near(xor_permute(grad_in_send, "wa", 1)),
         *[Rows(piece, 4 * quarter, experts) for piece in column_pieces],
     )
-    out_sums = to_tokens(out_rows, [grad_in_half], [])
+    out_sums = to_tokens(out_rows, [], [], [grad_in_half])
     out_pieces = exchange(out_sums, "lead")
     sums = [sums_own] + [xor_permute(sends[k - 1], "low", k) for k in range(1, low_count)]
     grad_kv_all = exchange([grad_kv] * 4, "lead")
@@ -1085,7 +1086,7 @@
         out_weight_kernel,
         [((local_width, part), F32)] + [((local_width, part), BF16)] * (low_count - 1),
         ids, early_all, *column_pieces,
-        after=[grad_in_half],
+        loose=[grad_in_half],
         scratch=[
             pltpu.VMEM((4 * row_count, low_count * part), BF16),
             pltpu.VMEM((4 * row_count, local_width), BF16),
@@ -1097,7 +1098,7 @@
         in_weight_kernel,
         [((part, local_width), F32)] + [((part, local_width), BF16)] * (low_count - 1),
         ids, queries_all, *column_pieces,
-        after=[grad_in_half],
+        loose=[grad_in_half],
         scratch=[pltpu.VMEM((4 * row_count, low_count * part), BF16)],
         flops=8 * row_count * low_count * local_width * part,
     )
@@ -1155,7 +1156,7 @@
             ((1, part), F32),
         ],
         Near(swap(small_parts, everywhere)), hidden, out_sums[0], out_weight_own, weight_own,
-        kv_weight_own, *out_pieces[1:], *near(others + weight_others + kv_others),
+        kv_weight_own, *near(out_pieces[1:] + others + weight_others + kv_others),
     )
     return (
         output,

time: 266 us -> 263 us (0.989)
  local copies, waits for them, and re-layouts: 3.33 us -> 0.15 us
    unnamed x42 -> x32, local copies, waits for them, and re-layouts: 3.25 us -> 0.07 us
where the time goes in v2:
time: 263 us; the launch traced here: 262 us
  Pallas kernels  101 us (38%)
  starting transfers between devices  84.6 us (32%)
  waiting for transfers between devices  61.3 us (23%)
  between operations  14.6 us (6%)
    pallas_call x25, Pallas kernels, vcall(): pl.pallas_call(kernel, out_shape=[jax.ShapeDtypeStruct(s, d) if c else pl...  101 us
    ppermute x48, starting transfers between devices, xor_permute(): return lax.ppermute(value, axis, [(i, i ^ offset) for i in range(count)])  65.7 us
    ppermute x48, waiting for transfers between devices, xor_permute(): return lax.ppermute(value, axis, [(i, i ^ offset) for i in range(count)])  34.3 us
    all_to_all x5, waiting for transfers between devices, swap(): return lax.all_to_all(value, axes, split_axis=0, concat_axis=0, tiled=True)  26.1 us
    all_to_all x5, starting transfers between devices, swap(): return lax.all_to_all(value, axes, split_axis=0, concat_axis=0, tiled=True)  18.5 us
  transfers between devices with their start and end apart: 55, of which 14 were waited for; matrix products, arithmetic and copies ran while one was open for 0% of the time, Pallas kernels for 30%

profile of v2, /device:TPU:0, one launch (start us, length us, event | category | flops | bytes accessed | tf_op | source)
XLA Modules:
  0.0 262.2 jit_solution(10637905998051596481)
XLA Ops:
  7.2 3.2 %shard_map.281 = (bf16[128,2048]{1,0:T(8,128)(2,1)}, bf16[128,256]{1,0:T(8,128)(2,1)S(1)}, f32[128,128]{1,0:T(8,128)}, f32[128,128]{1,0:T(8,128)}, f32[128,128]{1,0:T(8,128)}) custom-call(bf16[128,2048]{1,0:T(8,128)(2,1)} %refs_1_.8, f32[1,2048]{1,0:T(1,128)} %bitcast.47, bf16[2048,128]{1,0:T(8,128)(2,1)} %refs_6_.3, bf16[2048,128]{1,0:T(8,128)(2,1)} %refs_7_.1, ...), custom_call_target="tpu_custom_call" | custom-call | flops 134217728 | bytes 2369024 | tf_op jit(solution)/shard_map/pallas_call | solution.py:220
  10.3 3.0 %collective-permute-start = (bf16[128,256]{1,0:T(8,128)(2,1)S(1)}, bf16[128,256]{1,0:T(8,128)(2,1)S(1)}, u32[]{:S(2)}, u32[]{:S(2)}) collective-permute-start(bf16[128,256]{1,0:T(8,128)(2,1)S(1)} %get-tuple-element.101.refs_4_), channel_id=1, source_target_pairs={{0,4},{4,0},{8,12},{12,8},{16,20},{20,16},{24,28},{28,24},{1,5},{5... | collective-permute-start | bytes 196616 | tf_op jit(solution)/shard_map/ppermute | solution.py:56
  14.9 3.0 %collective-permute-start.3 = (bf16[128,256]{1,0:T(8,128)(2,1)S(1)}, bf16[128,256]{1,0:T(8,128)(2,1)S(1)}, u32[]{:S(2)}, u32[]{:S(2)}) collective-permute-start(bf16[128,256]{1,0:T(8,128)(2,1)S(1)} %get-tuple-element.101.refs_4_), channel_id=1, source_target_pairs={{0,16},{4,20},{8,24},{12,28},{16,0},{20,4},{24,8},{28,12},{1,17},{... | collective-permute-start | bytes 196616 | tf_op jit(solution)/shard_map/ppermute | solution.py:56
  19.2 3.6 %collective-permute-start.5 = (bf16[128,256]{1,0:T(8,128)(2,1)S(1)}, bf16[128,256]{1,0:T(8,128)(2,1)S(1)}, u32[]{:S(2)}, u32[]{:S(2)}) collective-permute-start(bf16[128,256]{1,0:T(8,128)(2,1)S(1)} %get-tuple-element.101.refs_4_), channel_id=1, source_target_pairs={{0,24},{4,28},{8,16},{12,20},{16,8},{20,12},{24,0},{28,4},{1,25},{... | collective-permute-start | bytes 196616 | tf_op jit(solution)/shard_map/ppermute | solution.py:56
  22.8 4.9 %shard_map.282 = (bf16[2,512,128]{2,1,0:T(8,128)(2,1)}, f32[2,512,128]{2,1,0:T(8,128)}) custom-call(bf16[128,2048]{1,0:T(8,128)(2,1)} %get-tuple-element.97.refs_0_.refs_3_, bf16[2048,1024]{1,0:T(8,128)(2,1)} %refs_1_.7, f32[128,128]{1,0:T(8,128)} %get-tuple-element.98.refs_2_.refs_7_.refs_3_, f32[128,128]{1,0:T(8,128)} %get-tuple-element.99.refs_3_.refs_8_.refs_4_, ...), custom_call_target="tpu_custom_call" | custom-call | flops 536870912 | bytes 5636608 | tf_op jit(solution)/shard_map/pallas_call | solution.py:220
  29.0 4.3 %collective-permute-start.11 = (bf16[32,2176]{1,0:T(8,128)(2,1)S(1)}, bf16[32,2176]{1,0:T(8,128)(2,1)S(1)}, u32[]{:S(2)}, u32[]{:S(2)}) collective-permute-start(bf16[32,2176]{1,0:T(8,128)(2,1)S(1)} %shard_map.284.refs_2_), channel_id=1, source_target_pairs={{0,16},{8,24},{16,0},{24,8},{1,17},{9,25},{17,1},{25,9},{2,18},{10... | collective-permute-start | bytes 417800 | tf_op jit(solution)/shard_map/ppermute | solution.py:56
  33.4 4.0 %shard_map.283 = (bf16[2,512,128]{2,1,0:T(8,128)(2,1)}, bf16[2,512,128]{2,1,0:T(8,128)(2,1)}, bf16[2,512,512]{2,1,0:T(8,128)(2,1)}, bf16[128,1024]{1,0:T(8,128)(...) custom-call(s32[6]{0:T(128)S(1)} %stack.27.refs_0_, ...), custom_call_target="tpu_custom_call" | custom-call | flops 805306368 | bytes 6816256 | tf_op jit(solution)/shard_map/pallas_call | solution.py:220
  39.3 2.9 %collective-permute-done.11.refs_4_ = bf16[32,2176]{1,0:T(8,128)(2,1)S(1)} collective-permute-done((bf16[32,2176]{1,0:T(8,128)(2,1)S(1)}, bf16[32,2176]{1,0:T(8,128)(2,1)S(1)}, u32[]{:S(2)}, u32[]{:S(2)}) %collective-permute-start.11) | collective-permute-done | bytes 139296 | tf_op jit(solution)/shard_map/ppermute | solution.py:56
  42.2 3.1 %shard_map.285 = (bf16[128,320]{1,0:T(8,128)(2,1)}, bf16[40,2048]{1,0:T(8,128)(2,1)}, bf16[40,2048]{1,0:T(8,128)(2,1)}, bf16[40,2048]{1,0:T(8,128)(2,1)}, bf16[4...) custom-call(s32[6]{0:T(128)S(1)} %stack.27.refs_0_, ...), custom_call_target="tpu_custom_call" | custom-call | flops 167772160 | bytes 1402880 | tf_op jit(solution)/shard_map/pallas_call | solution.py:220
  49.0 2.5 collective-permute-start.18
  53.9 3.0 %shard_map.286 = (bf16[32,2176]{1,0:T(8,128)(2,1)S(1)}, f32[32,2048]{1,0:T(8,128)}, f32[32,32]{1,0:T(8,128)}) custom-call(s32[6]{0:T(128)S(1)} %stack.27.refs_0_, bf16[128,2048]{1,0:T(8,128)(2,1)} %refs_1_.8, s32[8,32]{1,0:T(8,128)} %bitcast.50, f32[1,2048]{1,0:T(1,128)} %bitcast.45, bf16[32,2048]{1,0:T(8,128)(2,1)} %bitcast.43, ...), custom_call_target="tpu_custom_call" | custom-call | flops 4194304 | bytes 1070080 | tf_op jit(solution)/shard_map/pallas_call | solution.py:220
  60.2 3.7 %collective-permute-done.17.refs_7_.refs_12_ = bf16[40,2048]{1,0:T(8,128)(2,1)S(1)} collective-permute-done((bf16[40,2048]{1,0:T(8,128)(2,1)}, bf16[40,2048]{1,0:T(8,128)(2,1)S(1)}, u32[]{:S(2)}, u32[]{:S(2)}) %collective-permute-start.17) | collective-permute-done | bytes 163872 | tf_op jit(solution)/shard_map/ppermute | solution.py:56
  63.9 2.4 collective-permute-start.22
  66.4 6.1 %collective-permute-done.21.refs_6_ = bf16[32,2176]{1,0:T(8,128)(2,1)S(1)} collective-permute-done((bf16[32,2176]{1,0:T(8,128)(2,1)S(1)}, bf16[32,2176]{1,0:T(8,128)(2,1)S(1)}, u32[]{:S(2)}, u32[]{:S(2)}) %collective-permute-start.21) | collective-permute-done | bytes 139296 | tf_op jit(solution)/shard_map/ppermute | solution.py:56
  72.5 3.3 %shard_map.288 = (bf16[320,2176]{1,0:T(8,128)(2,1)}, bf16[192,1024]{1,0:T(8,128)(2,1)}) custom-call(s32[6]{0:T(128)S(1)} %stack.27.refs_0_, bf16[128,320]{1,0:T(8,128)(2,1)} %get-tuple-element.110.refs_9_.refs_1_, bf16[128,1024]{1,0:T(8,128)(2,1)} %get-tuple-element.122.refs_2_, bf16[128,2048]{1,0:T(8,128)(2,1)} %get-tuple-element.97.refs_0_.refs_3_, ...), custom_call_target="tpu_custom_call" | custom-call | flops 167772160 | bytes 2654208 | tf_op jit(solution)/shard_map/pallas_call | solution.py:220
  75.8 3.6 %all-to-all-start = ((bf16[8,40,2176]{2,1,0:T(8,128)(2,1)}), bf16[8,40,2176]{2,1,0:T(8,128)(2,1)S(1)}, u32[]{:S(2)}, u32[]{:S(2)}) async-start(bf16[8,40,2176]{2,1,0:T(8,128)(2,1)} %bitcast.41), calls=%async_computation | async-start | bytes 2785280 | tf_op jit(solution)/shard_map/all_to_all | solution.py:83
  80.1 5.2 %shard_map.287 = (bf16[320,2048]{1,0:T(8,128)(2,1)}, f32[320,768]{1,0:T(8,128)}) custom-call(s32[6]{0:T(128)S(1)} %stack.27.refs_0_, bf16[768,2048]{1,0:T(8,128)(2,1)} %bitcast.38, bf16[40,2048]{1,0:T(8,128)(2,1)} %get-tuple-element.113.refs_2_, bf16[40,2048]{1,0:T(8,128)(2,1)} %copy-done.1, bf16[40,2048]{1,0:T(8,128)(2,1)} %copy-done.2, ...), custom_call_target="tpu_custom_call" | custom-call | flops 1006632960 | bytes 6750208 | tf_op jit(solution)/shard_map/pallas_call | solution.py:220
  85.4 13.0 %all-to-all-done = bf16[8,40,2176]{2,1,0:T(8,128)(2,1)S(1)} async-done(((bf16[8,40,2176]{2,1,0:T(8,128)(2,1)}), bf16[8,40,2176]{2,1,0:T(8,128)(2,1)S(1)}, u32[]{:S(2)}, u32[]{:S(2)}) %all-to-all-start) | async-done | bytes 1392672 | tf_op jit(solution)/shard_map/all_to_all | solution.py:83
  98.4 10.4 %shard_map.289 = (bf16[320,768]{1,0:T(8,128)(2,1)}, bf16[320,768]{1,0:T(8,128)(2,1)}, bf16[320,768]{1,0:T(8,128)(2,1)}, f32[320,128]{1,0:T(8,128)}, bf16[320,2176]{1,0:T(8,128)(2,1)}) custom-call(s32[6]{0:T(128)S(1)} %stack.27.refs_0_, bf16[2048,768]{1,0:T(8,128)(2,1)} %bitcast.57, bf16[2048,768]{1,0:T(8,128)(2,1)} %bitcast.58, ...), custom_call_target="tpu_custom_call" | custom-call | flops 4026531840 | bytes 10305536 | tf_op jit(solution)/shard_map/pallas_call | solution.py:220
  108.8 3.8 %all-to-all-start.1 = ((bf16[8,40,2176]{2,1,0:T(8,128)(2,1)}), bf16[8,40,2176]{2,1,0:T(8,128)(2,1)S(1)}, u32[]{:S(2)}, u32[]{:S(2)}) async-start(bf16[8,40,2176]{2,1,0:T(8,128)(2,1)} %bitcast.42), calls=%async_computation.1 | async-start | bytes 2785280 | tf_op jit(solution)/shard_map/all_to_all | solution.py:83
  112.6 10.0 %shard_map.290 = (f32[2048,768]{1,0:T(8,128)}, f32[2048,768]{1,0:T(8,128)}, f32[768,2048]{1,0:T(8,128)}) custom-call(bf16[320,2176]{1,0:T(8,128)(2,1)} %bitcast.34, bf16[320,768]{1,0:T(8,128)(2,1)} %get-tuple-element.126.refs_1_, bf16[320,768]{1,0:T(8,128)(2,1)} %get-tuple-element.127.refs_2_, bf16[320,768]{1,0:T(8,128)(2,1)} %get-tuple-element.128.refs_3_.refs_0_, ...), custom_call_target="tpu_custom_call" | custom-call | flops 3019898880 | bytes 23216128 | tf_op jit(solution)/shard_map/pallas_call | solution.py:220
  122.7 8.7 %all-to-all-done.1 = bf16[8,40,2176]{2,1,0:T(8,128)(2,1)S(1)} async-done(((bf16[8,40,2176]{2,1,0:T(8,128)(2,1)}), bf16[8,40,2176]{2,1,0:T(8,128)(2,1)S(1)}, u32[]{:S(2)}, u32[]{:S(2)}) %all-to-all-start.1) | async-done | bytes 1392672 | tf_op jit(solution)/shard_map/all_to_all | solution.py:83
  133.4 3.6 %collective-permute-start.23 = (bf16[32,2176]{1,0:T(8,128)(2,1)S(1)}, bf16[32,2176]{1,0:T(8,128)(2,1)S(1)}, u32[]{:S(2)}, u32[]{:S(2)}) collective-permute-start(bf16[32,2176]{1,0:T(8,128)(2,1)S(1)} %get-tuple-element.134), channel_id=1, source_target_pairs={{0,8},{8,0},{16,24},{24,16},{1,9},{9,1},{17,25},{25,17},{2,10},{10... | collective-permute-start | bytes 417800 | tf_op jit(solution)/shard_map/ppermute | solution.py:56
  139.4 2.2 collective-permute-done.23.refs_7_.refs_3_
  141.6 5.9 %collective-permute-done.24.refs_8_.refs_4_ = bf16[32,2176]{1,0:T(8,128)(2,1)S(1)} collective-permute-done((bf16[32,2176]{1,0:T(8,128)(2,1)S(1)}, bf16[32,2176]{1,0:T(8,128)(2,1)S(1)}, u32[]{:S(2)}, u32[]{:S(2)}) %collective-permute-start.24) | collective-permute-done | bytes 139296 | tf_op jit(solution)/shard_map/ppermute | solution.py:56
  147.5 2.1 shard_map.292
  151.8 3.7 %collective-permute-start.27 = (bf16[32,2048]{1,0:T(8,128)(2,1)S(1)}, bf16[32,2048]{1,0:T(8,128)(2,1)S(1)}, u32[]{:S(2)}, u32[]{:S(2)}) collective-permute-start(bf16[32,2048]{1,0:T(8,128)(2,1)S(1)} %get-tuple-element.137.refs_10_), channel_id=1, source_target_pairs={{0,2},{1,3},{2,0},{3,1},{4,6},{5,7},{6,4},{7,5},{8,10},{9,11},{10,... | collective-permute-start | bytes 393224 | tf_op jit(solution)/shard_map/ppermute | solution.py:56
  158.1 4.7 %shard_map.293.refs_14_ = bf16[320,2048]{1,0:T(8,128)(2,1)} custom-call(bf16[320,768]{1,0:T(8,128)(2,1)} %get-tuple-element.128.refs_3_.refs_0_, bf16[768,2048]{1,0:T(8,128)(2,1)} %bitcast.39, f32[320,128]{1,0:T(8,128)} %get-tuple-element.130.refs_5_.refs_2_, bf16[32,2176]{1,0:T(8,128)(2,1)} %copy-done.8, bf16[32,2176]{1,0:T(8,128)(2,1)} %copy-done.9, ...), custom_call_target="tpu_custom_call" | custom-call | flops 1006632960 | bytes 5111808 | tf_op jit(solution)/shard_map/pallas_call | solution.py:220
  164.3 9.0 %shard_map.294 = (bf16[128,1024]{1,0:T(8,128)(2,1)}, f32[1,128]{1,0:T(1,128)}, bf16[8,128,256]{2,1,0:T(8,128)(2,1)}, bf16[128,2048]{1,0:T(8,128)(2,1)}) custom-call(s32[6]{0:T(128)S(1)} %stack.27.refs_0_, bf16[2,512,128]{2,1,0:T(8,128)(2,1)} %get-tuple-element.100.refs_1_.refs_2_, bf16[2,512,128]{2,1,0:T(8,128)(2,1)} %get-tuple-element.102.refs_2_, ...), custom_call_target="tpu_custom_call" | custom-call | flops 1073741824 | bytes 7996416 | tf_op jit(solution)/shard_map/pallas_call | solution.py:220
  173.3 4.3 %all-to-all-start.2 = ((bf16[8,128,256]{2,1,0:T(8,128)(2,1)}), bf16[8,128,256]{2,1,0:T(8,128)(2,1)S(1)}, u32[]{:S(2)}, u32[]{:S(2)}) async-start(bf16[8,128,256]{2,1,0:T(8,128)(2,1)} %get-tuple-element.144), calls=%async_computation.2 | async-start | bytes 1048576 | tf_op jit(solution)/shard_map/all_to_all | solution.py:83
  178.4 4.8 %shard_map.295.refs_1_.refs_6_ = f32[128,2048]{1,0:T(8,128)} custom-call(bf16[128,1024]{1,0:T(8,128)(2,1)} %get-tuple-element.142.refs_0_, bf16[2048,1024]{1,0:T(8,128)(2,1)} %refs_1_.7), custom_call_target="tpu_custom_call" | custom-call | flops 536870912 | bytes 5505024 | tf_op jit(solution)/shard_map/pallas_call | solution.py:220
  183.1 2.8 %shard_map.297.refs_2_.refs_5_ = bf16[160,1024]{1,0:T(8,128)(2,1)} custom-call(s32[6]{0:T(128)S(1)} %stack.27.refs_0_, bf16[4,192,1024]{2,1,0:T(8,128)(2,1)} %bitcast.36, bf16[80,512]{1,0:T(8,128)(2,1)S(1)} %get-tuple-element.147.refs_2_, bf16[80,512]{1,0:T(8,128)(2,1)S(1)} %collective-permute-done.29.refs_15_.refs_3_, ...), custom_call_target="tpu_custom_call" | custom-call | bytes 1900544 | tf_op jit(solution)/shard_map/pallas_call | solution.py:220
  187.9 4.4 %all-to-all-done.2.refs_8_ = bf16[8,128,256]{2,1,0:T(8,128)(2,1)S(1)} async-done(((bf16[8,128,256]{2,1,0:T(8,128)(2,1)}), bf16[8,128,256]{2,1,0:T(8,128)(2,1)S(1)}, u32[]{:S(2)}, u32[]{:S(2)}) %all-to-all-start.2) | async-done | bytes 524320 | tf_op jit(solution)/shard_map/all_to_all | solution.py:83
  192.3 4.2 %all-to-all-start.3 = ((bf16[8,40,2048]{2,1,0:T(8,128)(2,1)}), bf16[8,40,2048]{2,1,0:T(8,128)(2,1)S(1)}, u32[]{:S(2)}, u32[]{:S(2)}) async-start(bf16[8,40,2048]{2,1,0:T(8,128)(2,1)} %bitcast.21), calls=%async_computation.3 | async-start | bytes 2621440 | tf_op jit(solution)/shard_map/all_to_all | solution.py:83
  197.1 3.1 %shard_map.296 = (bf16[128,256]{1,0:T(8,128)(2,1)S(1)}, f32[1,128]{1,0:T(1,128)}, bf16[64,2048]{1,0:T(8,128)(2,1)S(1)}, bf16[64,2048]{1,0:T(8,128)(2,1)S(1)}) custom-call(s32[6]{0:T(128)S(1)} %stack.27.refs_0_, f32[128,2048]{1,0:T(8,128)} %shard_map.295.refs_1_.refs_6_, f32[128,128]{1,0:T(8,128)} %get-tuple-element.143.refs_2_, ...), custom_call_target="tpu_custom_call" | custom-call | flops 134217728 | bytes 2884608 | tf_op jit(solution)/shard_map/pallas_call | solution.py:220
  201.8 2.2 shard_map.298
  206.0 4.3 %shard_map.299 = (f32[1024,256]{1,0:T(8,128)}, bf16[1024,256]{1,0:T(8,128)(2,1)}) custom-call(s32[6]{0:T(128)S(1)} %stack.27.refs_0_, bf16[4,192,1024]{2,1,0:T(8,128)(2,1)} %bitcast.37, bf16[160,1024]{1,0:T(8,128)(2,1)} %shard_map.297.refs_2_.refs_5_, bf16[160,1024]{1,0:T(8,128)(2,1)} %copy-done.14, bf16[160,1024]{1,0:T(8,128)(2,1)} %copy-done.13, ...), custom_call_target="tpu_custom_call" | custom-call | flops 536870912 | bytes 4456448 | tf_op jit(solution)/shard_map/pallas_call | solution.py:220
  212.2 2.4 collective-permute-start.38
  216.2 4.1 %shard_map.300 = (f32[256,1024]{1,0:T(8,128)}, bf16[256,1024]{1,0:T(8,128)(2,1)}) custom-call(s32[6]{0:T(128)S(1)} %stack.27.refs_0_, bf16[512,1024]{1,0:T(8,128)(2,1)} %all-gather.5.cloned.1.call-done.refs_1_, bf16[160,1024]{1,0:T(8,128)(2,1)} %shard_map.297.refs_2_.refs_5_, bf16[160,1024]{1,0:T(8,128)(2,1)} %copy-done.14, bf16[160,1024]{1,0:T(8,128)(2,1)} %copy-done.13, ...), custom_call_target="tpu_custom_call" | custom-call | flops 536870912 | bytes 3932160 | tf_op jit(solution)/shard_map/pallas_call | solution.py:220
  220.8 2.7 %shard_map.301 = (bf16[64,2048]{1,0:T(8,128)(2,1)S(1)}, f32[1,2048]{1,0:T(1,128)}) custom-call(s32[6]{0:T(128)S(1)} %stack.27.refs_0_, bf16[128,2048]{1,0:T(8,128)(2,1)} %refs_1_.8, f32[1,2048]{1,0:T(1,128)} %bitcast.48, bf16[128,2048]{1,0:T(8,128)(2,1)} %get-tuple-element.141.refs_3_, bf16[64,2048]{1,0:T(8,128)(2,1)S(1)} %get-tuple-element.148.refs_6_.refs_4_.refs_3_, ...), custom_call_target="tpu_custom_call" | custom-call | bytes 1327104 | tf_op jit(solution)/shard_map/pallas_call | solution.py:220
  225.6 2.7 %shard_map.302 = (f32[32,2048]{1,0:T(8,128)}, bf16[32,2048]{1,0:T(8,128)(2,1)S(1)}, bf16[32,2048]{1,0:T(8,128)(2,1)S(1)}, bf16[32,2048]{1,0:T(8,128)(2,1)S(1)}) custom-call(s32[6]{0:T(128)S(1)} %stack.27.refs_0_, bf16[128,320]{1,0:T(8,128)(2,1)} %get-tuple-element.110.refs_9_.refs_1_, bf16[320,2048]{1,0:T(8,128)(2,1)S(1)} %bitcast.32, ...), custom_call_target="tpu_custom_call" | custom-call | flops 167772160 | bytes 737280 | tf_op jit(solution)/shard_map/pallas_call | solution.py:220
  228.4 2.8 %shard_map.303 = (bf16[128,2048]{1,0:T(8,128)(2,1)}, bf16[32,32,128]{2,1,0:T(8,128)(2,1)}) custom-call(s32[6]{0:T(128)S(1)} %stack.27.refs_0_, bf16[64,2048]{1,0:T(8,128)(2,1)S(1)} %get-tuple-element.152.refs_1_, bf16[64,2048]{1,0:T(8,128)(2,1)S(1)} %collective-permute-done.40.refs_2_, f32[1,2048]{1,0:T(1,128)} %get-tuple-element.153.refs_3_, ...), custom_call_target="tpu_custom_call" | custom-call | bytes 893952 | tf_op jit(solution)/shard_map/pallas_call | solution.py:220
  231.2 2.6 all-to-all-start.4
  235.6 2.5 collective-permute-start.44
  238.2 3.0 %shard_map.304 = (f32[256,256]{1,0:T(8,128)}, bf16[256,256]{1,0:T(8,128)(2,1)}) custom-call(s32[6]{0:T(128)S(1)} %stack.27.refs_0_, bf16[128,256]{1,0:T(8,128)(2,1)S(1)} %get-tuple-element.151.refs_1_, bf16[128,256]{1,0:T(8,128)(2,1)S(1)} %collective-permute-done.37.refs_8_.refs_2_, bf16[128,256]{1,0:T(8,128)(2,1)S(1)} %collective-permute-done.38.refs_9_.refs_3_, ...), custom_call_target="tpu_custom_call" | custom-call | flops 134217728 | bytes 1703936 | tf_op jit(solution)/shard_map/pallas_call | solution.py:220
  243.0 3.0 %collective-permute-done.43.refs_6_ = bf16[32,2048]{1,0:T(8,128)(2,1)S(1)} collective-permute-done((bf16[32,2048]{1,0:T(8,128)(2,1)}, bf16[32,2048]{1,0:T(8,128)(2,1)S(1)}, u32[]{:S(2)}, u32[]{:S(2)}) %collective-permute-start.43) | collective-permute-done | bytes 131104 | tf_op jit(solution)/shard_map/ppermute | solution.py:56
  246.0 6.1 %collective-permute-done.44.refs_7_ = bf16[32,2048]{1,0:T(8,128)(2,1)S(1)} collective-permute-done((bf16[32,2048]{1,0:T(8,128)(2,1)}, bf16[32,2048]{1,0:T(8,128)(2,1)S(1)}, u32[]{:S(2)}, u32[]{:S(2)}) %collective-permute-start.44) | collective-permute-done | bytes 131104 | tf_op jit(solution)/shard_map/ppermute | solution.py:56
  252.1 3.3 %shard_map.305 = (bf16[32,2048]{1,0:T(8,128)(2,1)}, f32[1024,256]{1,0:T(8,128)}, f32[256,1024]{1,0:T(8,128)}, f32[256,128]{1,0:T(8,128)}, f32[256,128]{1,0:T(8,1...) custom-call(bf16[32,32,128]{2,1,0:T(8,128)(2,1)S(1)} %all-to-all-don, ...), custom_call_target="tpu_custom_call" | custom-call | bytes 5646336 | tf_op jit(solution)/shard_map/pallas_call | solution.py:220
  (122 shorter events, 43.7 us)
Async XLA Ops:
  10.3 8.9 %collective-permute-start = (bf16[128,256]{1,0:T(8,128)(2,1)S(1)}, bf16[128,256]{1,0:T(8,128)(2,1)S(1)}, u32[]{:S(2)}, u32[]{:S(2)}) collective-permute-start(bf16[128,256]{1,0:T(8,128)(2,1)S(1)} %get-tuple-element.101.refs_4_), channel_id=1, source_target_pairs={{0,4},{4,0},{8,12},{12,8},{16,20},{20,16},{24,28},{28,24},{1,5},{5... | collective-permute-start | bytes 196616 | tf_op jit(solution)/shard_map/ppermute | solution.py:56
  13.4 9.5 %collective-permute-start.1 = (bf16[128,256]{1,0:T(8,128)(2,1)S(1)}, bf16[128,256]{1,0:T(8,128)(2,1)S(1)}, u32[]{:S(2)}, u32[]{:S(2)}) collective-permute-start(bf16[128,256]{1,0:T(8,128)(2,1)S(1)} %get-tuple-element.101.refs_4_), channel_id=1, source_target_pairs={{0,8},{4,12},{8,0},{12,4},{16,24},{20,28},{24,16},{28,20},{1,9},{5... | collective-permute-start | bytes 196616 | tf_op jit(solution)/shard_map/ppermute | solution.py:56
  14.9 13.8 %collective-permute-start.2 = (bf16[128,256]{1,0:T(8,128)(2,1)S(1)}, bf16[128,256]{1,0:T(8,128)(2,1)S(1)}, u32[]{:S(2)}, u32[]{:S(2)}) collective-permute-start(bf16[128,256]{1,0:T(8,128)(2,1)S(1)} %get-tuple-element.101.refs_4_), channel_id=1, source_target_pairs={{0,12},{4,8},{8,4},{12,0},{16,28},{20,24},{24,20},{28,16},{1,13},{... | collective-permute-start | bytes 196616 | tf_op jit(solution)/shard_map/ppermute | solution.py:56
  14.9 14.0 %collective-permute-start.3 = (bf16[128,256]{1,0:T(8,128)(2,1)S(1)}, bf16[128,256]{1,0:T(8,128)(2,1)S(1)}, u32[]{:S(2)}, u32[]{:S(2)}) collective-permute-start(bf16[128,256]{1,0:T(8,128)(2,1)S(1)} %get-tuple-element.101.refs_4_), channel_id=1, source_target_pairs={{0,16},{4,20},{8,24},{12,28},{16,0},{20,4},{24,8},{28,12},{1,17},{... | collective-permute-start | bytes 196616 | tf_op jit(solution)/shard_map/ppermute | solution.py:56
  17.9 15.4 %collective-permute-start.4 = (bf16[128,256]{1,0:T(8,128)(2,1)S(1)}, bf16[128,256]{1,0:T(8,128)(2,1)S(1)}, u32[]{:S(2)}, u32[]{:S(2)}) collective-permute-start(bf16[128,256]{1,0:T(8,128)(2,1)S(1)} %get-tuple-element.101.refs_4_), channel_id=1, source_target_pairs={{0,20},{4,16},{8,28},{12,24},{16,4},{20,0},{24,12},{28,8},{1,21},{... | collective-permute-start | bytes 196616 | tf_op jit(solution)/shard_map/ppermute | solution.py:56
  19.2 14.1 %collective-permute-start.5 = (bf16[128,256]{1,0:T(8,128)(2,1)S(1)}, bf16[128,256]{1,0:T(8,128)(2,1)S(1)}, u32[]{:S(2)}, u32[]{:S(2)}) collective-permute-start(bf16[128,256]{1,0:T(8,128)(2,1)S(1)} %get-tuple-element.101.refs_4_), channel_id=1, source_target_pairs={{0,24},{4,28},{8,16},{12,20},{16,8},{20,12},{24,0},{28,4},{1,25},{... | collective-permute-start | bytes 196616 | tf_op jit(solution)/shard_map/ppermute | solution.py:56
  22.8 10.5 %collective-permute-start.6 = (bf16[128,256]{1,0:T(8,128)(2,1)S(1)}, bf16[128,256]{1,0:T(8,128)(2,1)S(1)}, u32[]{:S(2)}, u32[]{:S(2)}) collective-permute-start(bf16[128,256]{1,0:T(8,128)(2,1)S(1)} %get-tuple-element.101.refs_4_), channel_id=1, source_target_pairs={{0,28},{4,24},{8,20},{12,16},{16,12},{20,8},{24,4},{28,0},{1,29},{... | collective-permute-start | bytes 196616 | tf_op jit(solution)/shard_map/ppermute | solution.py:56
  28.8 10.3 %collective-permute-start.10 = (bf16[32,2176]{1,0:T(8,128)(2,1)S(1)}, bf16[32,2176]{1,0:T(8,128)(2,1)S(1)}, u32[]{:S(2)}, u32[]{:S(2)}) collective-permute-start(bf16[32,2176]{1,0:T(8,128)(2,1)S(1)} %shard_map.284.refs_2_), channel_id=1, source_target_pairs={{0,8},{8,0},{16,24},{24,16},{1,9},{9,1},{17,25},{25,17},{2,10},{10... | collective-permute-start | bytes 417800 | tf_op jit(solution)/shard_map/ppermute | solution.py:56
  29.0 13.2 %collective-permute-start.11 = (bf16[32,2176]{1,0:T(8,128)(2,1)S(1)}, bf16[32,2176]{1,0:T(8,128)(2,1)S(1)}, u32[]{:S(2)}, u32[]{:S(2)}) collective-permute-start(bf16[32,2176]{1,0:T(8,128)(2,1)S(1)} %shard_map.284.refs_2_), channel_id=1, source_target_pairs={{0,16},{8,24},{16,0},{24,8},{1,17},{9,25},{17,1},{25,9},{2,18},{10... | collective-permute-start | bytes 417800 | tf_op jit(solution)/shard_map/ppermute | solution.py:56
  33.3 8.9 %collective-permute-start.12 = (bf16[32,2176]{1,0:T(8,128)(2,1)S(1)}, bf16[32,2176]{1,0:T(8,128)(2,1)S(1)}, u32[]{:S(2)}, u32[]{:S(2)}) collective-permute-start(bf16[32,2176]{1,0:T(8,128)(2,1)S(1)} %shard_map.284.refs_2_), channel_id=1, source_target_pairs={{0,24},{8,16},{16,8},{24,0},{1,25},{9,17},{17,9},{25,1},{2,26},{10... | collective-permute-start | bytes 417800 | tf_op jit(solution)/shard_map/ppermute | solution.py:56
  37.3 9.6 %collective-permute-start.7 = (bf16[32,2048]{1,0:T(8,128)(2,1)S(1)}, bf16[32,2048]{1,0:T(8,128)(2,1)S(1)}, u32[]{:S(2)}, u32[]{:S(2)}) collective-permute-start(bf16[32,2048]{1,0:T(8,128)(2,1)S(1)} %get-tuple-element.107), channel_id=1, source_target_pairs={{0,1},{1,0},{2,3},{3,2},{4,5},{5,4},{6,7},{7,6},{8,9},{9,8},{10,11... | collective-permute-start | bytes 393224 | tf_op jit(solution)/shard_map/ppermute | solution.py:56
  37.4 9.9 %collective-permute-start.8 = (bf16[32,2048]{1,0:T(8,128)(2,1)S(1)}, bf16[32,2048]{1,0:T(8,128)(2,1)S(1)}, u32[]{:S(2)}, u32[]{:S(2)}) collective-permute-start(bf16[32,2048]{1,0:T(8,128)(2,1)S(1)} %get-tuple-element.108), channel_id=1, source_target_pairs={{0,2},{1,3},{2,0},{3,1},{4,6},{5,7},{6,4},{7,5},{8,10},{9,11},{10,... | collective-permute-start | bytes 393224 | tf_op jit(solution)/shard_map/ppermute | solution.py:56
  39.1 9.7 %collective-permute-start.9 = (bf16[32,2048]{1,0:T(8,128)(2,1)S(1)}, bf16[32,2048]{1,0:T(8,128)(2,1)S(1)}, u32[]{:S(2)}, u32[]{:S(2)}) collective-permute-start(bf16[32,2048]{1,0:T(8,128)(2,1)S(1)} %get-tuple-element.109), channel_id=1, source_target_pairs={{0,3},{1,2},{2,1},{3,0},{4,7},{5,6},{6,5},{7,4},{8,11},{9,10},{10,... | collective-permute-start | bytes 393224 | tf_op jit(solution)/shard_map/ppermute | solution.py:56
  45.4 7.3 %collective-permute-start.14 = (bf16[40,2048]{1,0:T(8,128)(2,1)}, bf16[40,2048]{1,0:T(8,128)(2,1)S(1)}, u32[]{:S(2)}, u32[]{:S(2)}) collective-permute-start(bf16[40,2048]{1,0:T(8,128)(2,1)} %get-tuple-element.115), channel_id=1, source_target_pairs={{0,2},{1,3},{2,0},{3,1},{4,6},{5,7},{6,4},{7,5},{8,10},{9,11},{10,... | collective-permute-start | bytes 491528 | tf_op jit(solution)/shard_map/ppermute | solution.py:56
  47.0 10.0 %collective-permute-start.15 = (bf16[40,2048]{1,0:T(8,128)(2,1)}, bf16[40,2048]{1,0:T(8,128)(2,1)S(1)}, u32[]{:S(2)}, u32[]{:S(2)}) collective-permute-start(bf16[40,2048]{1,0:T(8,128)(2,1)} %get-tuple-element.116), channel_id=1, source_target_pairs={{0,3},{1,2},{2,1},{3,0},{4,7},{5,6},{6,5},{7,4},{8,11},{9,10},{10,... | collective-permute-start | bytes 491528 | tf_op jit(solution)/shard_map/ppermute | solution.py:56
  47.3 11.8 %collective-permute-start.16 = (bf16[40,2048]{1,0:T(8,128)(2,1)}, bf16[40,2048]{1,0:T(8,128)(2,1)S(1)}, u32[]{:S(2)}, u32[]{:S(2)}) collective-permute-start(bf16[40,2048]{1,0:T(8,128)(2,1)} %get-tuple-element.117), channel_id=1, source_target_pairs={{0,4},{1,5},{2,6},{3,7},{4,0},{5,1},{6,2},{7,3},{8,12},{9,13},{10,... | collective-permute-start | bytes 491528 | tf_op jit(solution)/shard_map/ppermute | solution.py:56
  48.8 15.1 %collective-permute-start.17 = (bf16[40,2048]{1,0:T(8,128)(2,1)}, bf16[40,2048]{1,0:T(8,128)(2,1)S(1)}, u32[]{:S(2)}, u32[]{:S(2)}) collective-permute-start(bf16[40,2048]{1,0:T(8,128)(2,1)} %get-tuple-element.118), channel_id=1, source_target_pairs={{0,5},{1,4},{2,7},{3,6},{4,1},{5,0},{6,3},{7,2},{8,13},{9,12},{10,... | collective-permute-start | bytes 491528 | tf_op jit(solution)/shard_map/ppermute | solution.py:56
  49.0 17.3 %collective-permute-start.18 = (bf16[40,2048]{1,0:T(8,128)(2,1)}, bf16[40,2048]{1,0:T(8,128)(2,1)S(1)}, u32[]{:S(2)}, u32[]{:S(2)}) collective-permute-start(bf16[40,2048]{1,0:T(8,128)(2,1)} %get-tuple-element.119), channel_id=1, source_target_pairs={{0,6},{1,7},{2,4},{3,5},{4,2},{5,3},{6,0},{7,1},{8,14},{9,15},{10,... | collective-permute-start | bytes 491528 | tf_op jit(solution)/shard_map/ppermute | solution.py:56
  52.7 13.6 %collective-permute-start.19 = (bf16[40,2048]{1,0:T(8,128)(2,1)}, bf16[40,2048]{1,0:T(8,128)(2,1)S(1)}, u32[]{:S(2)}, u32[]{:S(2)}) collective-permute-start(bf16[40,2048]{1,0:T(8,128)(2,1)} %get-tuple-element.120), channel_id=1, source_target_pairs={{0,7},{1,6},{2,5},{3,4},{4,3},{5,2},{6,1},{7,0},{8,15},{9,14},{10,... | collective-permute-start | bytes 491528 | tf_op jit(solution)/shard_map/ppermute | solution.py:56
  57.0 9.4 %collective-permute-start.20 = (bf16[32,2176]{1,0:T(8,128)(2,1)S(1)}, bf16[32,2176]{1,0:T(8,128)(2,1)S(1)}, u32[]{:S(2)}, u32[]{:S(2)}) collective-permute-start(bf16[32,2176]{1,0:T(8,128)(2,1)S(1)} %get-tuple-element.123.refs_4_), channel_id=1, source_target_pairs={{0,8},{8,0},{16,24},{24,16},{1,9},{9,1},{17,25},{25,17},{2,10},{10... | collective-permute-start | bytes 417800 | tf_op jit(solution)/shard_map/ppermute | solution.py:56
  59.1 13.4 %collective-permute-start.21 = (bf16[32,2176]{1,0:T(8,128)(2,1)S(1)}, bf16[32,2176]{1,0:T(8,128)(2,1)S(1)}, u32[]{:S(2)}, u32[]{:S(2)}) collective-permute-start(bf16[32,2176]{1,0:T(8,128)(2,1)S(1)} %get-tuple-element.123.refs_4_), channel_id=1, source_target_pairs={{0,16},{8,24},{16,0},{24,8},{1,17},{9,25},{17,1},{25,9},{2,18},{10... | collective-permute-start | bytes 417800 | tf_op jit(solution)/shard_map/ppermute | solution.py:56
  63.9 8.6 %collective-permute-start.22 = (bf16[32,2176]{1,0:T(8,128)(2,1)S(1)}, bf16[32,2176]{1,0:T(8,128)(2,1)S(1)}, u32[]{:S(2)}, u32[]{:S(2)}) collective-permute-start(bf16[32,2176]{1,0:T(8,128)(2,1)S(1)} %get-tuple-element.123.refs_4_), channel_id=1, source_target_pairs={{0,24},{8,16},{16,8},{24,0},{1,25},{9,17},{17,9},{25,1},{2,26},{10... | collective-permute-start | bytes 417800 | tf_op jit(solution)/shard_map/ppermute | solution.py:56
  75.8 22.6 %all-to-all-start = ((bf16[8,40,2176]{2,1,0:T(8,128)(2,1)}), bf16[8,40,2176]{2,1,0:T(8,128)(2,1)S(1)}, u32[]{:S(2)}, u32[]{:S(2)}) async-start(bf16[8,40,2176]{2,1,0:T(8,128)(2,1)} %bitcast.41), calls=%async_computation | async-start | bytes 2785280 | tf_op jit(solution)/shard_map/all_to_all | solution.py:83
  79.4 43.3 %all-gather.3.cloned.1.call-start = ((), (), s32[]{:S(2)}) async-start(), calls=%async_computation.5 | async-start | bytes 1966080 | tf_op jit(solution)/shard_map/all_gather | solution.py:79
  108.8 22.6 %all-to-all-start.1 = ((bf16[8,40,2176]{2,1,0:T(8,128)(2,1)}), bf16[8,40,2176]{2,1,0:T(8,128)(2,1)S(1)}, u32[]{:S(2)}, u32[]{:S(2)}) async-start(bf16[8,40,2176]{2,1,0:T(8,128)(2,1)} %bitcast.42), calls=%async_computation.1 | async-start | bytes 2785280 | tf_op jit(solution)/shard_map/all_to_all | solution.py:83
  133.4 8.3 %collective-permute-start.23 = (bf16[32,2176]{1,0:T(8,128)(2,1)S(1)}, bf16[32,2176]{1,0:T(8,128)(2,1)S(1)}, u32[]{:S(2)}, u32[]{:S(2)}) collective-permute-start(bf16[32,2176]{1,0:T(8,128)(2,1)S(1)} %get-tuple-element.134), channel_id=1, source_target_pairs={{0,8},{8,0},{16,24},{24,16},{1,9},{9,1},{17,25},{25,17},{2,10},{10... | collective-permute-start | bytes 417800 | tf_op jit(solution)/shard_map/ppermute | solution.py:56
  137.0 10.5 %collective-permute-start.24 = (bf16[32,2176]{1,0:T(8,128)(2,1)S(1)}, bf16[32,2176]{1,0:T(8,128)(2,1)S(1)}, u32[]{:S(2)}, u32[]{:S(2)}) collective-permute-start(bf16[32,2176]{1,0:T(8,128)(2,1)S(1)} %get-tuple-element.135), channel_id=1, source_target_pairs={{0,16},{8,24},{16,0},{24,8},{1,17},{9,25},{17,1},{25,9},{2,18},{10... | collective-permute-start | bytes 417800 | tf_op jit(solution)/shard_map/ppermute | solution.py:56
  138.0 9.5 %collective-permute-start.25 = (bf16[32,2176]{1,0:T(8,128)(2,1)S(1)}, bf16[32,2176]{1,0:T(8,128)(2,1)S(1)}, u32[]{:S(2)}, u32[]{:S(2)}) collective-permute-start(bf16[32,2176]{1,0:T(8,128)(2,1)S(1)} %get-tuple-element.136), channel_id=1, source_target_pairs={{0,24},{8,16},{16,8},{24,0},{1,25},{9,17},{17,9},{25,1},{2,26},{10... | collective-permute-start | bytes 417800 | tf_op jit(solution)/shard_map/ppermute | solution.py:56
  149.7 7.0 %collective-permute-start.29 = (bf16[80,512]{1,0:T(8,128)(2,1)S(1)}, bf16[80,512]{1,0:T(8,128)(2,1)S(1)}, u32[]{:S(2)}, u32[]{:S(2)}) collective-permute-start(bf16[80,512]{1,0:T(8,128)(2,1)S(1)} %get-tuple-element.138), channel_id=1, source_target_pairs={{0,8},{8,0},{16,24},{24,16},{1,9},{9,1},{17,25},{25,17},{2,10},{10... | collective-permute-start | bytes 245768 | tf_op jit(solution)/shard_map/ppermute | solution.py:56
  151.8 12.6 %collective-permute-start.26 = (bf16[32,2048]{1,0:T(8,128)(2,1)S(1)}, bf16[32,2048]{1,0:T(8,128)(2,1)S(1)}, u32[]{:S(2)}, u32[]{:S(2)}) collective-permute-start(bf16[32,2048]{1,0:T(8,128)(2,1)S(1)} %get-tuple-element.137.refs_10_), channel_id=1, source_target_pairs={{0,1},{1,0},{2,3},{3,2},{4,5},{5,4},{6,7},{7,6},{8,9},{9,8},{10,11... | collective-permute-start | bytes 393224 | tf_op jit(solution)/shard_map/ppermute | solution.py:56
  151.8 12.6 %collective-permute-start.27 = (bf16[32,2048]{1,0:T(8,128)(2,1)S(1)}, bf16[32,2048]{1,0:T(8,128)(2,1)S(1)}, u32[]{:S(2)}, u32[]{:S(2)}) collective-permute-start(bf16[32,2048]{1,0:T(8,128)(2,1)S(1)} %get-tuple-element.137.refs_10_), channel_id=1, source_target_pairs={{0,2},{1,3},{2,0},{3,1},{4,6},{5,7},{6,4},{7,5},{8,10},{9,11},{10,... | collective-permute-start | bytes 393224 | tf_op jit(solution)/shard_map/ppermute | solution.py:56
  155.5 8.8 %collective-permute-start.28 = (bf16[32,2048]{1,0:T(8,128)(2,1)S(1)}, bf16[32,2048]{1,0:T(8,128)(2,1)S(1)}, u32[]{:S(2)}, u32[]{:S(2)}) collective-permute-start(bf16[32,2048]{1,0:T(8,128)(2,1)S(1)} %get-tuple-element.137.refs_10_), channel_id=1, source_target_pairs={{0,3},{1,2},{2,1},{3,0},{4,7},{5,6},{6,5},{7,4},{8,11},{9,10},{10,... | collective-permute-start | bytes 393224 | tf_op jit(solution)/shard_map/ppermute | solution.py:56
  155.7 8.7 %collective-permute-start.30 = (bf16[80,512]{1,0:T(8,128)(2,1)S(1)}, bf16[80,512]{1,0:T(8,128)(2,1)S(1)}, u32[]{:S(2)}, u32[]{:S(2)}) collective-permute-start(bf16[80,512]{1,0:T(8,128)(2,1)S(1)} %get-tuple-element.139), channel_id=1, source_target_pairs={{0,16},{8,24},{16,0},{24,8},{1,17},{9,25},{17,1},{25,9},{2,18},{10... | collective-permute-start | bytes 245768 | tf_op jit(solution)/shard_map/ppermute | solution.py:56
  156.7 7.7 %collective-permute-start.31 = (bf16[80,512]{1,0:T(8,128)(2,1)S(1)}, bf16[80,512]{1,0:T(8,128)(2,1)S(1)}, u32[]{:S(2)}, u32[]{:S(2)}) collective-permute-start(bf16[80,512]{1,0:T(8,128)(2,1)S(1)} %get-tuple-element.140), channel_id=1, source_target_pairs={{0,24},{8,16},{16,8},{24,0},{1,25},{9,17},{17,9},{25,1},{2,26},{10... | collective-permute-start | bytes 245768 | tf_op jit(solution)/shard_map/ppermute | solution.py:56
  173.3 19.0 %all-to-all-start.2 = ((bf16[8,128,256]{2,1,0:T(8,128)(2,1)}), bf16[8,128,256]{2,1,0:T(8,128)(2,1)S(1)}, u32[]{:S(2)}, u32[]{:S(2)}) async-start(bf16[8,128,256]{2,1,0:T(8,128)(2,1)} %get-tuple-element.144), calls=%async_computation.2 | async-start | bytes 1048576 | tf_op jit(solution)/shard_map/all_to_all | solution.py:83
  177.6 38.6 %all-gather.5.cloned.1.call-start = ((), (), s32[]{:S(2)}) async-start(), calls=%async_computation.6 | async-start | bytes 1310720 | tf_op jit(solution)/shard_map/all_gather | solution.py:79
  185.9 11.1 %collective-permute-start.34 = (bf16[160,1024]{1,0:T(8,128)(2,1)}, bf16[160,1024]{1,0:T(8,128)(2,1)S(1)}, u32[]{:S(2)}, u32[]{:S(2)}) collective-permute-start(bf16[160,1024]{1,0:T(8,128)(2,1)} %shard_map.297.refs_2_.refs_5_), channel_id=1, source_target_pairs={{0,2},{1,3},{2,0},{3,1},{4,6},{5,7},{6,4},{7,5},{8,10},{9,11},{10,... | collective-permute-start | bytes 983048 | tf_op jit(solution)/shard_map/ppermute | solution.py:56
  192.3 33.3 %all-to-all-start.3 = ((bf16[8,40,2048]{2,1,0:T(8,128)(2,1)}), bf16[8,40,2048]{2,1,0:T(8,128)(2,1)S(1)}, u32[]{:S(2)}, u32[]{:S(2)}) async-start(bf16[8,40,2048]{2,1,0:T(8,128)(2,1)} %bitcast.21), calls=%async_computation.3 | async-start | bytes 2621440 | tf_op jit(solution)/shard_map/all_to_all | solution.py:83
  204.0 16.7 %collective-permute-start.36 = (bf16[64,2048]{1,0:T(8,128)(2,1)S(1)}, bf16[64,2048]{1,0:T(8,128)(2,1)S(1)}, u32[]{:S(2)}, u32[]{:S(2)}) collective-permute-start(bf16[64,2048]{1,0:T(8,128)(2,1)S(1)} %get-tuple-element.148.refs_6_.refs_4_.refs_3_), channel_id=1, source_target_pairs={{0,2},{1,3},{2,0},{3,1},{4,6},{5,7},{6,4},{7,5},{8,10},{9,11},{10,... | collective-permute-start | bytes 786440 | tf_op jit(solution)/shard_map/ppermute | solution.py:56
  210.3 18.0 %collective-permute-start.42 = (bf16[1024,256]{1,0:T(8,128)(2,1)}, bf16[1024,256]{1,0:T(8,128)(2,1)S(1)}, u32[]{:S(2)}, u32[]{:S(2)}) collective-permute-start(bf16[1024,256]{1,0:T(8,128)(2,1)} %get-tuple-element.159), channel_id=1, source_target_pairs={{0,4},{4,0},{1,5},{5,1},{2,6},{6,2},{3,7},{7,3},{8,12},{12,8},{9,1... | collective-permute-start | bytes 1572872 | tf_op jit(solution)/shard_map/ppermute | solution.py:56
  211.8 8.5 %collective-permute-start.37 = (bf16[128,256]{1,0:T(8,128)(2,1)S(1)}, bf16[128,256]{1,0:T(8,128)(2,1)S(1)}, u32[]{:S(2)}, u32[]{:S(2)}) collective-permute-start(bf16[128,256]{1,0:T(8,128)(2,1)S(1)} %get-tuple-element.151.refs_1_), channel_id=1, source_target_pairs={{0,8},{8,0},{16,24},{24,16},{1,9},{9,1},{17,25},{25,17},{2,10},{10... | collective-permute-start | bytes 196616 | tf_op jit(solution)/shard_map/ppermute | solution.py:56
  212.2 8.1 %collective-permute-start.38 = (bf16[128,256]{1,0:T(8,128)(2,1)S(1)}, bf16[128,256]{1,0:T(8,128)(2,1)S(1)}, u32[]{:S(2)}, u32[]{:S(2)}) collective-permute-start(bf16[128,256]{1,0:T(8,128)(2,1)S(1)} %get-tuple-element.151.refs_1_), channel_id=1, source_target_pairs={{0,16},{8,24},{16,0},{24,8},{1,17},{9,25},{17,1},{25,9},{2,18},{10... | collective-permute-start | bytes 196616 | tf_op jit(solution)/shard_map/ppermute | solution.py:56
  224.2 27.9 %collective-permute-start.46 = (bf16[256,1024]{1,0:T(8,128)(2,1)}, bf16[256,1024]{1,0:T(8,128)(2,1)S(1)}, u32[]{:S(2)}, u32[]{:S(2)}) collective-permute-start(bf16[256,1024]{1,0:T(8,128)(2,1)} %get-tuple-element.165), channel_id=1, source_target_pairs={{0,4},{4,0},{1,5},{5,1},{2,6},{6,2},{3,7},{7,3},{8,12},{12,8},{9,1... | collective-permute-start | bytes 1572872 | tf_op jit(solution)/shard_map/ppermute | solution.py:56
  231.2 20.9 %all-to-all-start.4 = ((bf16[32,32,128]{2,1,0:T(8,128)(2,1)}), bf16[32,32,128]{2,1,0:T(8,128)(2,1)S(1)}, u32[]{:S(2)}, u32[]{:S(2)}) async-start(bf16[32,32,128]{2,1,0:T(8,128)(2,1)} %get-tuple-element.160.refs_9_), calls=%async_computation.4 | async-start | bytes 524288 | tf_op jit(solution)/shard_map/all_to_all | solution.py:83
  233.8 12.2 %collective-permute-start.43 = (bf16[32,2048]{1,0:T(8,128)(2,1)}, bf16[32,2048]{1,0:T(8,128)(2,1)S(1)}, u32[]{:S(2)}, u32[]{:S(2)}) collective-permute-start(bf16[32,2048]{1,0:T(8,128)(2,1)} %copy-done.12), channel_id=1, source_target_pairs={{0,8},{8,0},{16,24},{24,16},{1,9},{9,1},{17,25},{25,17},{2,10},{10... | collective-permute-start | bytes 393224 | tf_op jit(solution)/shard_map/ppermute | solution.py:56
  235.6 16.5 %collective-permute-start.44 = (bf16[32,2048]{1,0:T(8,128)(2,1)}, bf16[32,2048]{1,0:T(8,128)(2,1)S(1)}, u32[]{:S(2)}, u32[]{:S(2)}) collective-permute-start(bf16[32,2048]{1,0:T(8,128)(2,1)} %copy-done.11), channel_id=1, source_target_pairs={{0,16},{8,24},{16,0},{24,8},{1,17},{9,25},{17,1},{25,9},{2,18},{10... | collective-permute-start | bytes 393224 | tf_op jit(solution)/shard_map/ppermute | solution.py:56
  238.0 14.0 %collective-permute-start.45 = (bf16[32,2048]{1,0:T(8,128)(2,1)S(1)}, bf16[32,2048]{1,0:T(8,128)(2,1)S(1)}, u32[]{:S(2)}, u32[]{:S(2)}) collective-permute-start(bf16[32,2048]{1,0:T(8,128)(2,1)S(1)} %get-tuple-element.164), channel_id=1, source_target_pairs={{0,24},{8,16},{16,8},{24,0},{1,25},{9,17},{17,9},{25,1},{2,26},{10... | collective-permute-start | bytes 393224 | tf_op jit(solution)/shard_map/ppermute | solution.py:56
  241.2 10.8 %collective-permute-start.47 = (bf16[256,256]{1,0:T(8,128)(2,1)}, bf16[256,256]{1,0:T(8,128)(2,1)S(1)}, u32[]{:S(2)}, u32[]{:S(2)}) collective-permute-start(bf16[256,256]{1,0:T(8,128)(2,1)} %get-tuple-element.166), channel_id=1, source_target_pairs={{0,4},{4,0},{1,5},{5,1},{2,6},{6,2},{3,7},{7,3},{8,12},{12,8},{9,1... | collective-permute-start | bytes 393224 | tf_op jit(solution)/shard_map/ppermute | solution.py:56
  (23 other events, 227.8 us)
Sparse Core Ops, SparseCore 0:
  81.8 39.6 all-gather.2
  180.0 29.7 all-gather.4
